TPU v7x, 32 devices: a whole 2x2x4 slice. The times are simulated.
32 devices in a mesh: blk: 4 (over z), wide: 8 (over y, x, core).
Axes of the slice: x: 2, y: 2, z: 4, core: 2. Of those that a mesh axis runs over, the one named last changes fastest.
Arguments:
- tokens: bfloat16 [8, 1280, 2048], P('wide', 'blk'), may hold values from -6 to 6
- lengths: int32 [8, 3], replicated, may hold values from 1 to 1278, as said below
- query_weight: bfloat16 [2048, 2048], P('blk', 'wide'), may hold values from -0.125 to 0.125
- key_weight: bfloat16 [2048, 2048], P('blk', 'wide'), may hold values from -0.125 to 0.125
- value_weight: bfloat16 [2048, 2048], P('blk', 'wide'), may hold values from -0.125 to 0.125
- output_weight: bfloat16 [2048, 2048], P('wide', 'blk'), may hold values from -0.125 to 0.125
- query_gain: bfloat16 [2048], P('wide'), may hold values from 0.796875 to 1.59375
- key_gain: bfloat16 [2048], P('wide'), may hold values from 0.796875 to 1.59375
- attention_gain: bfloat16 [2048], P('wide'), may hold values from 0.5 to 1.5
- gate_weight: bfloat16 [2048, 8192], P(None, 'wide'), may hold values from -0.125 to 0.125
- up_weight: bfloat16 [2048, 8192], P(None, 'wide'), may hold values from -0.125 to 0.125
- down_weight: bfloat16 [8192, 2048], P('wide'), may hold values from -0.0625 to 0.0625
- feedforward_gain: bfloat16 [2048], P('wide'), may hold values from 0.5 to 1.5
- cotangent: bfloat16 [8, 1280, 2048], P('wide', 'blk'), may hold values from -6 to 6
Outputs:
- block_output: bfloat16 [8, 1280, 2048], P('wide', 'blk')
- tokens_grad: float32 [8, 1280, 2048], P('wide', 'blk')
- query_grad: float32 [2048, 2048], P('blk', 'wide')
- key_grad: float32 [2048, 2048], P('blk', 'wide')
- value_grad: float32 [2048, 2048], P('blk', 'wide')
- output_grad: float32 [2048, 2048], P('wide', 'blk')
- query_gain_grad: float32 [2048], P(('blk', 'wide'))
- key_gain_grad: float32 [2048], P(('blk', 'wide'))
- attention_gain_grad: float32 [2048], P(('blk', 'wide'))
- gate_grad: float32 [2048, 8192], P('blk', 'wide')
- up_grad: float32 [2048, 8192], P('blk', 'wide')
- down_grad: float32 [8192, 2048], P('wide', 'blk')
- feedforward_gain_grad: float32 [2048], P(('blk', 'wide'))
Inputs may be any that keep to these rules, and one draw needn't show every extreme that they name: Each group holds 3 packed sequences whose lengths sum to 1280; the first and the last hold at most a quarter of 320 tokens each.
All inputs are finite; a program needn't handle non-finite values.
Results may differ from a plain program's by a relative error of at most 0.033.
Values may be sent and summed in bfloat16 or wider, within the bound.
A program may use at most 384 MiB of HBM per device.

v0:
```python
import jax
import jax.numpy as jnp
from jax import lax
from jax.sharding import PartitionSpec as P

D = 2048
HD = 128


EPS = 1e-06
ROPE_BASE = 500000.0
NEG_FILL = -1e30


def layout(seq_lengths, row_count):
    indices = jnp.arange(row_count, dtype=jnp.int32)
    first_end = seq_lengths[0]
    second_end = seq_lengths[0] + seq_lengths[1]
    segment = (indices >= first_end).astype(jnp.int32) + (indices >= second_end).astype(jnp.int32)
    offsets = jnp.where(segment == 0, 0, jnp.where(segment == 1, first_end, second_end))
    return (segment, indices - offsets)


def rotary(values, position, direction):
    row_count = values.shape[0]
    heads_split = values.reshape(row_count, -1, HD)
    frequency = ROPE_BASE ** (-jnp.arange(0, HD, 2, dtype=jnp.float32) / HD)
    angles = position.astype(jnp.float32)[:, None] * frequency[None, :]
    cosine_table = jnp.concatenate([jnp.cos(angles), jnp.cos(angles)], axis=-1)[:, None, :]
    sine_table = (
        direction * jnp.concatenate([jnp.sin(angles), jnp.sin(angles)], axis=-1)[:, None, :]
    )
    first_half = heads_split[..., : HD // 2]
    second_half = heads_split[..., HD // 2 :]
    turned = jnp.concatenate([-second_half, first_half], axis=-1)
    return (heads_split * cosine_table + turned * sine_table).reshape(values.shape)


def rms_pair(values):
    inverse = lax.rsqrt(jnp.mean(values * values, axis=-1, keepdims=True) + EPS)
    return (values * inverse, inverse)


def norm_back(normed, inverse, grad_normed):
    return inverse * (grad_normed - normed * jnp.mean(grad_normed * normed, axis=-1, keepdims=True))


def feature_means(parts):
    sums = tuple((jnp.sum(part, axis=-1, keepdims=True) for part in parts))
    return tuple((total / D for total in sums))


def contract_rows(left, right):
    return lax.dot_general(
        left, right, (((0,), (0,)), ((), ())), preferred_element_type=jnp.float32
    )


def contract_cols(left, right):
    return lax.dot_general(
        left, right, (((1,), (1,)), ((), ())), preferred_element_type=jnp.float32
    )


def local(
    tokens,
    lengths,
    query_weight,
    key_weight,
    value_weight,
    output_weight,
    query_gain,
    key_gain,
    attention_gain,
    gate_weight,
    up_weight,
    down_weight,
    feedforward_gain,
    cotangent,
):
    local_rows = tokens.shape[1]
    group_rows = local_rows * lax.axis_size("blk")
    row_start = lax.axis_index("blk") * local_rows
    wide_here = lax.axis_index("wide")
    query_index = row_start + jnp.arange(local_rows, dtype=jnp.int32)
    score_scale = HD ** (-0.5)
    group_lengths = lax.dynamic_slice_in_dim(lengths, wide_here, 1, 0)
    segment_table, position_table = jax.vmap(lambda seq_lengths: layout(seq_lengths, group_rows))(
        group_lengths
    )
    group_count = segment_table.shape[0]
    query_segment = lax.dynamic_slice_in_dim(segment_table, row_start, local_rows, 1)
    row_position = lax.dynamic_slice_in_dim(position_table, row_start, local_rows, 1).reshape(-1)

    def allowed_for(piece_rows):
        key_index = jnp.arange(piece_rows, dtype=jnp.int32)
        same = query_segment[:, :, None] == segment_table[:, None, :]
        causal = query_index[None, :, None] >= key_index[None, None, :]
        return (same & causal)[:, None]

    def forward(inputs, weights, gains, gate_local, up_local, down_local):
        widened = (
            lax.all_gather(weights[0], "wide", axis=1, tiled=True),
            lax.all_gather(weights[1], "wide", axis=1, tiled=True),
            lax.all_gather(weights[2], "wide", axis=1, tiled=True),
            lax.all_gather(weights[3], "wide", axis=0, tiled=True),
            lax.all_gather(gains[0], "wide", axis=0, tiled=True),
            lax.all_gather(gains[1], "wide", axis=0, tiled=True),
            lax.all_gather(gains[2], "wide", axis=0, tiled=True),
            lax.all_gather(gains[3], "wide", axis=0, tiled=True),
        )
        column_blocks = (widened[0], widened[1], widened[2], widened[3])
        gain_query, gain_key, gain_mixer, gain_feed = (
            widened[4],
            widened[5],
            widened[6],
            widened[7],
        )
        mats = (
            lax.all_gather(column_blocks[0], "blk", axis=0, tiled=True),
            lax.all_gather(column_blocks[1], "blk", axis=0, tiled=True),
            lax.all_gather(column_blocks[2], "blk", axis=0, tiled=True),
            lax.all_gather(column_blocks[3], "blk", axis=1, tiled=True),
        )
        gain_query = gain_query.astype(jnp.float32)
        gain_key = gain_key.astype(jnp.float32)
        gain_mixer = gain_mixer.astype(jnp.float32)
        gain_feed = gain_feed.astype(jnp.float32)
        query_pre = jnp.dot(inputs, mats[0], preferred_element_type=jnp.float32)
        key_pre = jnp.dot(inputs, mats[1], preferred_element_type=jnp.float32)
        value_rows = jnp.dot(inputs, mats[2], preferred_element_type=jnp.float32).astype(
            jnp.bfloat16
        )
        query_square, key_square = feature_means((query_pre * query_pre, key_pre * key_pre))
        query_inverse = lax.rsqrt(query_square + EPS)
        key_inverse = lax.rsqrt(key_square + EPS)
        query_normed = query_pre * query_inverse
        key_normed = key_pre * key_inverse
        queries = rotary(query_normed * gain_query, row_position, 1.0).astype(jnp.bfloat16)
        key_rows = rotary(key_normed * gain_key, row_position, 1.0).astype(jnp.bfloat16)
        local_width = queries.shape[1]
        head_count = local_width // HD
        query_heads = queries.reshape(group_count, local_rows, head_count, HD)
        key_blocks = key_rows.reshape(group_count, local_rows, local_width)
        value_blocks = value_rows.reshape(group_count, local_rows, local_width)
        run_max = jnp.full((group_count, head_count, local_rows), NEG_FILL, jnp.float32)
        key_piece = lax.all_gather(key_blocks, "blk", axis=1, tiled=True)
        value_piece = lax.all_gather(value_blocks, "blk", axis=1, tiled=True)
        piece_rows = key_piece.shape[1]
        key_heads = key_piece.reshape(group_count, piece_rows, head_count, HD)
        value_heads = value_piece.reshape(group_count, piece_rows, head_count, HD)
        scores = (
            jnp.einsum(
                "gqhd,gkhd->ghqk", query_heads, key_heads, preferred_element_type=jnp.float32
            )
            * score_scale
        )
        allowed = allowed_for(piece_rows)
        scores = jnp.where(allowed, scores, NEG_FILL)
        new_max = jnp.maximum(run_max, jnp.max(scores, axis=-1))
        weights_now = jnp.where(allowed, jnp.exp(scores - new_max[..., None]), 0.0)
        run_total = jnp.sum(weights_now, axis=-1)
        weighted = jnp.einsum(
            "ghqk,gkhd->ghqd",
            weights_now.astype(jnp.bfloat16),
            value_heads,
            preferred_element_type=jnp.float32,
        )
        run_max, run_total, weighted = (new_max, run_total, weighted)
        mixed_exact = jnp.transpose(weighted / run_total[..., None], (0, 2, 1, 3))
        log_total = run_max + jnp.log(run_total)
        mixed_low = mixed_exact.reshape(group_count * local_rows, local_width).astype(jnp.bfloat16)
        partial_proj = jnp.dot(mixed_low, mats[3], preferred_element_type=jnp.float32)
        proj_normed, proj_inverse = rms_pair(partial_proj)
        hidden_state = inputs.astype(jnp.float32) + proj_normed * gain_mixer
        gathered = lax.all_gather(hidden_state.astype(jnp.bfloat16), "wide", axis=0, tiled=True)
        gate_rows = jnp.dot(gathered, gate_local, preferred_element_type=jnp.float32)
        upward = jnp.dot(gathered, up_local, preferred_element_type=jnp.float32)
        activated = (jax.nn.silu(gate_rows) * upward).astype(jnp.bfloat16)
        reduced = lax.psum_scatter(
            jnp.dot(activated, down_local, preferred_element_type=jnp.float32).astype(jnp.bfloat16),
            "wide",
            scatter_dimension=0,
            tiled=True,
        ).astype(jnp.float32)
        return {
            "rows": inputs,
            "mats": mats,
            "gain_query": gain_query,
            "gain_key": gain_key,
            "gain_mixer": gain_mixer,
            "gain_feed": gain_feed,
            "query_normed": query_normed,
            "query_inverse": query_inverse,
            "key_normed": key_normed,
            "key_inverse": key_inverse,
            "query_heads": query_heads,
            "key_blocks": key_blocks,
            "value_blocks": value_blocks,
            "mixed_exact": mixed_exact,
            "mixed_low": mixed_low,
            "log_total": log_total,
            "proj_normed": proj_normed,
            "proj_inverse": proj_inverse,
            "hidden_state": hidden_state,
            "gathered": gathered,
            "gate_rows": gate_rows,
            "upward": upward,
            "activated": activated,
            "reduced": reduced,
        }

    inputs = tokens[0]
    weights = (query_weight, key_weight, value_weight, output_weight)
    gains = (query_gain, key_gain, attention_gain, feedforward_gain)
    saved = forward(inputs, weights, gains, gate_weight, up_weight, down_weight)
    red_normed, red_inverse = rms_pair(saved["reduced"])
    block_output = (saved["hidden_state"] + red_normed * saved["gain_feed"]).astype(jnp.bfloat16)
    repeated = lax.optimization_barrier(
        (inputs, weights, gains, gate_weight, up_weight, down_weight)
    )
    saved = forward(repeated[0], repeated[1], repeated[2], repeated[3], repeated[4], repeated[5])
    red_normed, red_inverse = rms_pair(saved["reduced"])
    mats = saved["mats"]
    query_normed = saved["query_normed"]
    key_normed = saved["key_normed"]
    query_heads = saved["query_heads"]
    local_width = query_normed.shape[1]
    head_count = local_width // HD
    grad_out = cotangent[0].astype(jnp.float32)
    feed_gain_grad = jnp.sum(grad_out * red_normed, axis=0)
    grad_reduced = norm_back(red_normed, red_inverse, grad_out * saved["gain_feed"]).astype(
        jnp.bfloat16
    )
    grad_rows = lax.all_gather(grad_reduced, "wide", axis=0, tiled=True)
    down_grad = contract_rows(saved["activated"], grad_rows)
    grad_act = contract_cols(grad_rows, down_weight)
    gate_rows = saved["gate_rows"]
    sigmoid_gate = jax.nn.sigmoid(gate_rows)
    grad_up = (grad_act * gate_rows * sigmoid_gate).astype(jnp.bfloat16)
    grad_gate = (
        grad_act * saved["upward"] * sigmoid_gate * (1.0 + gate_rows * (1.0 - sigmoid_gate))
    ).astype(jnp.bfloat16)
    gate_grad = contract_rows(saved["gathered"], grad_gate)
    up_grad = contract_rows(saved["gathered"], grad_up)
    grad_hidden = grad_out + lax.psum_scatter(
        (contract_cols(grad_gate, gate_weight) + contract_cols(grad_up, up_weight)).astype(
            jnp.bfloat16
        ),
        "wide",
        scatter_dimension=0,
        tiled=True,
    ).astype(jnp.float32)
    mixer_gain_grad = jnp.sum(grad_hidden * saved["proj_normed"], axis=0)
    grad_proj = norm_back(
        saved["proj_normed"], saved["proj_inverse"], grad_hidden * saved["gain_mixer"]
    ).astype(jnp.bfloat16)
    output_part = contract_rows(saved["mixed_low"], grad_proj)
    grad_mixed = contract_cols(grad_proj, mats[3]).astype(jnp.bfloat16)
    grad_heads = grad_mixed.reshape(group_count, local_rows, head_count, HD)
    row_delta = jnp.einsum("gqhd,gqhd->ghq", grad_heads.astype(jnp.float32), saved["mixed_exact"])
    log_total = saved["log_total"]
    key_piece = lax.all_gather(saved["key_blocks"], "blk", axis=1, tiled=True)
    value_piece = lax.all_gather(saved["value_blocks"], "blk", axis=1, tiled=True)
    piece_rows = key_piece.shape[1]
    key_heads = key_piece.reshape(group_count, piece_rows, head_count, HD)
    value_heads = value_piece.reshape(group_count, piece_rows, head_count, HD)
    scores = (
        jnp.einsum("gqhd,gkhd->ghqk", query_heads, key_heads, preferred_element_type=jnp.float32)
        * score_scale
    )
    allowed = allowed_for(piece_rows)
    weights_now = jnp.where(allowed, jnp.exp(scores - log_total[..., None]), 0.0)
    grad_weights = jnp.einsum(
        "gqhd,gkhd->ghqk", grad_heads, value_heads, preferred_element_type=jnp.float32
    )
    grad_scores = (weights_now * (grad_weights - row_delta[..., None])).astype(jnp.bfloat16)
    grad_query = (
        jnp.einsum("ghqk,gkhd->ghqd", grad_scores, key_heads, preferred_element_type=jnp.float32)
        * score_scale
    )
    key_term = (
        jnp.einsum(
            "ghqk,gqhd->gkhd", grad_scores, query_heads, preferred_element_type=jnp.float32
        ).reshape(group_count, piece_rows, local_width)
        * score_scale
    )
    value_term = jnp.einsum(
        "ghqk,gqhd->gkhd",
        weights_now.astype(jnp.bfloat16),
        grad_heads,
        preferred_element_type=jnp.float32,
    ).reshape(group_count, piece_rows, local_width)
    grad_keys = key_term
    grad_values = value_term
    grad_query, grad_keys, grad_values = (grad_query, grad_keys, grad_values)
    key_mine, value_mine = (
        lax.psum_scatter(
            grad_keys.astype(jnp.bfloat16), "blk", scatter_dimension=1, tiled=True
        ).astype(jnp.float32),
        lax.psum_scatter(
            grad_values.astype(jnp.bfloat16), "blk", scatter_dimension=1, tiled=True
        ).astype(jnp.float32),
    )
    all_rows = group_count * local_rows
    grad_query_flat = jnp.transpose(grad_query, (0, 2, 1, 3)).reshape(all_rows, local_width)
    grad_query_normed = rotary(grad_query_flat, row_position, -1.0)
    grad_key_normed = rotary(key_mine.reshape(all_rows, local_width), row_position, -1.0)
    query_gain_part = jnp.sum(grad_query_normed * query_normed, axis=0)
    key_gain_part = jnp.sum(grad_key_normed * key_normed, axis=0)
    scaled_query = grad_query_normed * saved["gain_query"]
    scaled_key = grad_key_normed * saved["gain_key"]
    query_mean, key_mean = feature_means((scaled_query * query_normed, scaled_key * key_normed))
    grad_query_pre = (saved["query_inverse"] * (scaled_query - query_normed * query_mean)).astype(
        jnp.bfloat16
    )
    grad_key_pre = (saved["key_inverse"] * (scaled_key - key_normed * key_mean)).astype(
        jnp.bfloat16
    )
    grad_value_pre = value_mine.reshape(all_rows, local_width).astype(jnp.bfloat16)
    rows = saved["rows"]
    query_part = contract_rows(rows, grad_query_pre)
    key_part = contract_rows(rows, grad_key_pre)
    value_part = contract_rows(rows, grad_value_pre)
    tokens_part = (
        contract_cols(grad_query_pre, mats[0])
        + contract_cols(grad_key_pre, mats[1])
        + contract_cols(grad_value_pre, mats[2])
    )
    blk_sums = (
        lax.psum_scatter(
            query_part.astype(jnp.bfloat16), "blk", scatter_dimension=0, tiled=True
        ).astype(jnp.float32),
        lax.psum_scatter(
            key_part.astype(jnp.bfloat16), "blk", scatter_dimension=0, tiled=True
        ).astype(jnp.float32),
        lax.psum_scatter(
            value_part.astype(jnp.bfloat16), "blk", scatter_dimension=0, tiled=True
        ).astype(jnp.float32),
        lax.psum_scatter(
            output_part.astype(jnp.bfloat16), "blk", scatter_dimension=1, tiled=True
        ).astype(jnp.float32),
        lax.psum_scatter(
            gate_grad.astype(jnp.bfloat16), "blk", scatter_dimension=0, tiled=True
        ).astype(jnp.float32),
        lax.psum_scatter(
            up_grad.astype(jnp.bfloat16), "blk", scatter_dimension=0, tiled=True
        ).astype(jnp.float32),
        lax.psum_scatter(
            down_grad.astype(jnp.bfloat16), "blk", scatter_dimension=1, tiled=True
        ).astype(jnp.float32),
        lax.psum_scatter(
            query_gain_part.astype(jnp.bfloat16), "blk", scatter_dimension=0, tiled=True
        ).astype(jnp.float32),
        lax.psum_scatter(
            key_gain_part.astype(jnp.bfloat16), "blk", scatter_dimension=0, tiled=True
        ).astype(jnp.float32),
        lax.psum_scatter(
            mixer_gain_grad.astype(jnp.bfloat16), "blk", scatter_dimension=0, tiled=True
        ).astype(jnp.float32),
        lax.psum_scatter(
            feed_gain_grad.astype(jnp.bfloat16), "blk", scatter_dimension=0, tiled=True
        ).astype(jnp.float32),
    )
    wide_sums = (
        lax.psum_scatter(
            blk_sums[0].astype(jnp.bfloat16), "wide", scatter_dimension=1, tiled=True
        ).astype(jnp.float32),
        lax.psum_scatter(
            blk_sums[1].astype(jnp.bfloat16), "wide", scatter_dimension=1, tiled=True
        ).astype(jnp.float32),
        lax.psum_scatter(
            blk_sums[2].astype(jnp.bfloat16), "wide", scatter_dimension=1, tiled=True
        ).astype(jnp.float32),
        lax.psum_scatter(
            blk_sums[3].astype(jnp.bfloat16), "wide", scatter_dimension=0, tiled=True
        ).astype(jnp.float32),
        lax.psum_scatter(
            blk_sums[7].astype(jnp.bfloat16), "wide", scatter_dimension=0, tiled=True
        ).astype(jnp.float32),
        lax.psum_scatter(
            blk_sums[8].astype(jnp.bfloat16), "wide", scatter_dimension=0, tiled=True
        ).astype(jnp.float32),
        lax.psum_scatter(
            blk_sums[9].astype(jnp.bfloat16), "wide", scatter_dimension=0, tiled=True
        ).astype(jnp.float32),
        lax.psum_scatter(
            blk_sums[10].astype(jnp.bfloat16), "wide", scatter_dimension=0, tiled=True
        ).astype(jnp.float32),
    )
    tokens_grad = grad_hidden + tokens_part
    query_grad, key_grad, value_grad, output_grad = (
        wide_sums[0],
        wide_sums[1],
        wide_sums[2],
        wide_sums[3],
    )
    gain_grads = (wide_sums[4], wide_sums[5], wide_sums[6], wide_sums[7])
    return (
        block_output[None],
        tokens_grad[None],
        query_grad,
        key_grad,
        value_grad,
        output_grad,
        gain_grads[0],
        gain_grads[1],
        gain_grads[2],
        blk_sums[4],
        blk_sums[5],
        blk_sums[6],
        gain_grads[3],
    )


def solution(mesh):
    placed = (
        P("wide", "blk", None),
        P(),
        P("blk", "wide"),
        P("blk", "wide"),
        P("blk", "wide"),
        P("wide", "blk"),
        P("wide"),
        P("wide"),
        P("wide"),
        P(None, "wide"),
        P(None, "wide"),
        P("wide", None),
        P("wide"),
        P("wide", "blk", None),
    )
    return jax.shard_map(
        local,
        mesh=mesh,
        in_specs=placed,
        out_specs=(
            P("wide", "blk", None),
            P("wide", "blk", None),
            P("blk", "wide"),
            P("blk", "wide"),
            P("blk", "wide"),
            P("wide", "blk"),
            P(("blk", "wide")),
            P(("blk", "wide")),
            P(("blk", "wide")),
            P("blk", "wide"),
            P("blk", "wide"),
            P("wide", "blk"),
            P(("blk", "wide")),
        ),
        check_vma=False,
    )
```

profile of v0, /device:TPU:8, one launch (start us, length us, event | category | flops | bytes accessed | tf_op | source)
XLA Modules:
  0.0 3553.3 jit_solution(13307363190690938894)
XLA Ops:
  10.6 28.7 all-gather.36.cloned.1.call-done
  39.4 30.0 all-gather.40.cloned.1.call-done
  69.5 30.0 all-gather.58.cloned.1.call-done
  99.6 29.9 all-gather.54.cloned.1.call-done
  129.5 29.9 all-gather.62.cloned.1.call-done
  198.7 108.8 %all-gather.38.cloned.1.call-done = bf16[2048,2048]{1,0:T(8,128)(2,1)} async-done(((bf16[512,2048]{1,0:T(8,128)(2,1)}), bf16[2048,2048]{1,0:T(8,128)(2,1)}) %all-gather.38.cloned.1.call-update) | async-done | bytes 8388624 | tf_op jit(solution)/shard_map/all_gather | solution.py:120
  315.3 141.7 %all-gather.42.cloned.1.call-done = bf16[2048,2048]{1,0:T(8,128)(2,1)} async-done(((bf16[512,2048]{1,0:T(8,128)(2,1)}), bf16[2048,2048]{1,0:T(8,128)(2,1)}) %all-gather.42.cloned.1.call-update) | async-done | bytes 8388624 | tf_op jit(solution)/shard_map/all_gather | solution.py:121
  467.5 139.0 %all-gather.60.cloned.1.call-done = bf16[2048,2048]{1,0:T(8,128)(2,1)} async-done(((bf16[512,2048]{1,0:T(8,128)(2,1)}), bf16[2048,2048]{1,0:T(8,128)(2,1)}) %all-gather.60.cloned.1.call-update) | async-done | bytes 8388624 | tf_op jit(solution)/shard_map/all_gather | solution.py:121
  612.3 143.6 %all-gather.56.cloned.1.call-done = bf16[2048,2048]{1,0:T(8,128)(2,1)} async-done(((bf16[512,2048]{1,0:T(8,128)(2,1)}), bf16[2048,2048]{1,0:T(8,128)(2,1)}) %all-gather.56.cloned.1.call-update) | async-done | bytes 8388624 | tf_op jit(solution)/shard_map/all_gather | solution.py:120
  801.7 103.6 %all-gather.64.cloned.1.call-done = bf16[2048,2048]{1,0:T(8,128)(2,1)} async-done(((bf16[512,2048]{1,0:T(8,128)(2,1)}), bf16[2048,2048]{1,0:T(8,128)(2,1)}) %all-gather.64.cloned.1.call-update) | async-done | bytes 8388624 | tf_op jit(solution)/shard_map/all_gather | solution.py:122
  912.7 23.6 all-gather.66.cloned.1.call-done
  946.6 87.0 %all-gather.74.cloned.1.call-done = bf16[1280,2048]{1,0:T(8,128)(2,1)} async-done(((bf16[320,2048]{1,0:T(8,128)(2,1)}), bf16[1280,2048]{1,0:T(8,128)(2,1)}) %all-gather.74.cloned.1.call-update) | async-done | bytes 5242896 | tf_op jit(solution)/shard_map/all_gather | solution.py:147
  1050.1 82.0 %all-gather.78.cloned.1.call-done = bf16[1280,2048]{1,0:T(8,128)(2,1)} async-done(((bf16[320,2048]{1,0:T(8,128)(2,1)}), bf16[1280,2048]{1,0:T(8,128)(2,1)}) %all-gather.78.cloned.1.call-update) | async-done | bytes 5242896 | tf_op jit(solution)/shard_map/all_gather | solution.py:147
  1132.2 21.7 select_reduce_fusion
  1154.5 23.6 fusion.4
  1178.0 52.6 %all-gather.80.cloned.1.call-done = bf16[1280,2048]{1,0:T(8,128)(2,1)} async-done(((bf16[320,2048]{1,0:T(8,128)(2,1)}), bf16[1280,2048]{1,0:T(8,128)(2,1)}) %all-gather.80.cloned.1.call-update) | async-done | bytes 5242896 | tf_op jit(solution)/shard_map/all_gather | solution.py:148
  1246.5 133.4 %all-gather.68.cloned.1.call-done = bf16[2048,2048]{1,0:T(8,128)(2,1)} async-done(((bf16[2048,512]{1,0:T(8,128)(2,1)}), bf16[2048,2048]{1,0:T(8,128)(2,1)}) %all-gather.68.cloned.1.call-update) | async-done | bytes 8388624 | tf_op jit(solution)/shard_map/all_gather | solution.py:123
  1388.5 64.5 %all-gather.70.cloned.1.call-done = bf16[2560,2048]{1,0:T(8,128)(2,1)} async-done(((bf16[320,2048]{1,0:T(8,128)(2,1)}), bf16[2560,2048]{1,0:T(8,128)(2,1)}) %all-gather.70.cloned.1.call-update) | async-done | bytes 10485776 | tf_op jit(solution)/shard_map/all_gather | solution.py:176
  1469.9 17.2 multiply_convert_fusion.4
  1513.0 72.2 %reduce-scatter.21.cloned.1.call-done = bf16[320,2048]{1,0:T(8,128)(2,1)} async-done(((bf16[2560,2048]{1,0:T(8,128)(2,1)}), bf16[320,2048]{1,0:T(8,128)(2,1)}) %reduce-scatter.21.cloned.1.call-update) | async-done | bytes 1310736 | tf_op jit(solution)/shard_map/reduce_scatter | solution.py:180
  1591.8 23.4 all-gather.44.cloned.1.call-done
  1616.2 64.7 %all-gather.72.cloned.1.call-done = bf16[2560,2048]{1,0:T(8,128)(2,1)} async-done(((bf16[320,2048]{1,0:T(8,128)(2,1)}), bf16[2560,2048]{1,0:T(8,128)(2,1)}) %all-gather.72.cloned.1.call-update) | async-done | bytes 10485776 | tf_op jit(solution)/shard_map/all_gather | solution.py:235
  1680.9 27.3 multiply_convert_fusion.2
  1708.2 18.1 fusion.118
  1726.3 20.3 add_convert_fusion
  1746.7 82.3 %all-gather.46.cloned.1.call-done = bf16[2048,2048]{1,0:T(8,128)(2,1)} async-done(((bf16[512,2048]{1,0:T(8,128)(2,1)}), bf16[2048,2048]{1,0:T(8,128)(2,1)}) %all-gather.46.cloned.1.call-update) | async-done | bytes 8388624 | tf_op jit(solution)/shard_map/all_gather | solution.py:122
  1836.5 23.6 all-gather.48.cloned.1.call-done
  1860.3 84.8 %reduce-scatter.23.cloned.1.call-done = bf16[320,2048]{1,0:T(8,128)(2,1)} async-done(((bf16[2560,2048]{1,0:T(8,128)(2,1)}), bf16[320,2048]{1,0:T(8,128)(2,1)}) %reduce-scatter.23.cloned.1.call-update) | async-done | bytes 1310736 | tf_op jit(solution)/shard_map/reduce_scatter | solution.py:246
  1970.3 21.8 copy.89
  2006.6 20.1 multiply_convert_fusion
  2069.7 122.2 %all-gather.50.cloned.1.call-done = bf16[2048,2048]{1,0:T(8,128)(2,1)} async-done(((bf16[2048,512]{1,0:T(8,128)(2,1)}), bf16[2048,2048]{1,0:T(8,128)(2,1)}) %all-gather.50.cloned.1.call-update) | async-done | bytes 8388624 | tf_op jit(solution)/shard_map/all_gather | solution.py:123
  2209.2 80.0 %reduce-scatter.49.cloned.1.call-done = bf16[320,2048]{1,0:T(8,128)(2,1)} async-done(((bf16[1280,2048]{1,0:T(8,128)(2,1)}), bf16[320,2048]{1,0:T(8,128)(2,1)}) %reduce-scatter.49.cloned.1.call-update) | async-done | bytes 1310736
  2320.4 65.2 %reduce-scatter.25.cloned.1.call-done = bf16[1,320,2048]{2,1,0:T(8,128)(2,1)} async-done(((bf16[1,1280,2048]{2,1,0:T(8,128)(2,1)}), bf16[1,320,2048]{2,1,0:T(8,128)(2,1)}) %reduce-scatter.25.cloned.1.call-update) | async-done | bytes 1310736 | tf_op jit(solution)/shard_map/reduce_scatter | solution.py:298
  2414.7 37.0 %all-gather.52.cloned.1.call-done = bf16[2560,2048]{1,0:T(8,128)(2,1)} async-done(((bf16[320,2048]{1,0:T(8,128)(2,1)}), bf16[2560,2048]{1,0:T(8,128)(2,1)}) %all-gather.52.cloned.1.call-update) | async-done | bytes 10485776 | tf_op jit(solution)/shard_map/all_gather | solution.py:176
  2468.1 29.8 convolution_convert_fusion.1
  2498.0 17.3 convolution_convert_fusion.6
  2559.9 38.4 %reduce-scatter.39.cloned.1.call-done = bf16[2048,512]{1,0:T(8,128)(2,1)} async-done(((bf16[2048,2048]{1,0:T(8,128)(2,1)}), bf16[2048,512]{1,0:T(8,128)(2,1)}) %reduce-scatter.39.cloned.1.call-update) | async-done | bytes 2097168 | tf_op jit(solution)/shard_map/reduce_scatter | solution.py:340
  2598.4 147.5 %reduce-scatter.35.cloned.1.call-done = bf16[512,2048]{1,0:T(8,128)(2,1)} async-done(((bf16[2048,2048]{1,0:T(8,128)(2,1)}), bf16[512,2048]{1,0:T(8,128)(2,1)}) %reduce-scatter.35.cloned.1.call-update) | async-done | bytes 2097168 | tf_op jit(solution)/shard_map/reduce_scatter | solution.py:337
  2745.9 147.4 %reduce-scatter.31.cloned.1.call-done = bf16[512,2048]{1,0:T(8,128)(2,1)} async-done(((bf16[2048,2048]{1,0:T(8,128)(2,1)}), bf16[512,2048]{1,0:T(8,128)(2,1)}) %reduce-scatter.31.cloned.1.call-update) | async-done | bytes 2097168 | tf_op jit(solution)/shard_map/reduce_scatter | solution.py:334
  2904.7 74.7 %reduce-scatter.19.cloned.1.call-done = bf16[320,2048]{1,0:T(8,128)(2,1)} async-done(((bf16[2560,2048]{1,0:T(8,128)(2,1)}), bf16[320,2048]{1,0:T(8,128)(2,1)}) %reduce-scatter.19.cloned.1.call-update) | async-done | bytes 1310736 | tf_op jit(solution)/shard_map/reduce_scatter | solution.py:180
  2985.2 73.3 %reduce-scatter.47.cloned.1.call-done = bf16[1024,512]{1,0:T(8,128)(2,1)} async-done(((bf16[1024,2048]{1,0:T(8,128)(2,1)}), bf16[1024,512]{1,0:T(8,128)(2,1)}) %reduce-scatter.47.cloned.1.call-update) | async-done | bytes 1048592 | tf_op jit(solution)/shard_map/reduce_scatter | solution.py:349
  3061.3 76.7 %reduce-scatter.45.cloned.1.call-done = bf16[512,1024]{1,0:T(8,128)(2,1)} async-done(((bf16[2048,1024]{1,0:T(8,128)(2,1)}), bf16[512,1024]{1,0:T(8,128)(2,1)}) %reduce-scatter.45.cloned.1.call-update) | async-done | bytes 1048592 | tf_op jit(solution)/shard_map/reduce_scatter | solution.py:346
  3140.8 76.8 %reduce-scatter.43.cloned.1.call-done = bf16[512,1024]{1,0:T(8,128)(2,1)} async-done(((bf16[2048,1024]{1,0:T(8,128)(2,1)}), bf16[512,1024]{1,0:T(8,128)(2,1)}) %reduce-scatter.43.cloned.1.call-update) | async-done | bytes 1048592 | tf_op jit(solution)/shard_map/reduce_scatter | solution.py:343
  3248.7 116.5 %reduce-scatter.27.cloned.1.call-done = bf16[512,2048]{1,0:T(8,128)(2,1)} async-done(((bf16[2048,2048]{1,0:T(8,128)(2,1)}), bf16[512,2048]{1,0:T(8,128)(2,1)}) %reduce-scatter.27.cloned.1.call-update) | async-done | bytes 2097168 | tf_op jit(solution)/shard_map/reduce_scatter | solution.py:331
  3387.8 23.0 reduce-scatter.41.cloned.1.call-done
  3412.6 42.6 %reduce-scatter.37.cloned.1.call-done = bf16[512,256]{1,0:T(8,128)(2,1)} async-done(((bf16[512,2048]{1,0:T(8,128)(2,1)}), bf16[512,256]{1,0:T(8,128)(2,1)}) %reduce-scatter.37.cloned.1.call-update) | async-done | bytes 262160 | tf_op jit(solution)/shard_map/reduce_scatter | solution.py:372
  3457.0 43.1 %reduce-scatter.33.cloned.1.call-done = bf16[512,256]{1,0:T(8,128)(2,1)} async-done(((bf16[512,2048]{1,0:T(8,128)(2,1)}), bf16[512,256]{1,0:T(8,128)(2,1)}) %reduce-scatter.33.cloned.1.call-update) | async-done | bytes 262160 | tf_op jit(solution)/shard_map/reduce_scatter | solution.py:369
  3501.8 42.6 %reduce-scatter.29.cloned.1.call-done = bf16[512,256]{1,0:T(8,128)(2,1)} async-done(((bf16[512,2048]{1,0:T(8,128)(2,1)}), bf16[512,256]{1,0:T(8,128)(2,1)}) %reduce-scatter.29.cloned.1.call-update) | async-done | bytes 262160 | tf_op jit(solution)/shard_map/reduce_scatter | solution.py:366
  (386 shorter events, 531.4 us)
Async XLA Ops:
  7.2 32.1 all-gather.36.cloned.1.call-start
  7.9 61.5 %all-gather.40.cloned.1.call-start = ((), (), s32[]{:S(2)}) async-start(), calls=%async_computation.18 | async-start | bytes 2359296 | tf_op jit(solution)/shard_map/all_gather | solution.py:104
  8.7 90.8 %all-gather.58.cloned.1.call-start = ((), (), s32[]{:S(2)}) async-start(), calls=%async_computation.28 | async-start | bytes 2359296 | tf_op jit(solution)/shard_map/all_gather | solution.py:104
  9.4 120.1 %all-gather.54.cloned.1.call-start = ((), (), s32[]{:S(2)}) async-start(), calls=%async_computation.26 | async-start | bytes 2359296 | tf_op jit(solution)/shard_map/all_gather | solution.py:103
  10.0 149.4 %all-gather.62.cloned.1.call-start = ((), (), s32[]{:S(2)}) async-start(), calls=%async_computation.30 | async-start | bytes 2359296 | tf_op jit(solution)/shard_map/all_gather | solution.py:105
  10.6 297.0 %all-gather.38.cloned.1.call-start = ((), (), s32[]{:S(2)}) async-start(), calls=%async_computation.17 | async-start | bytes 10485760 | tf_op jit(solution)/shard_map/all_gather | solution.py:120
  39.3 417.7 %all-gather.42.cloned.1.call-start = ((), (), s32[]{:S(2)}) async-start(), calls=%async_computation.19 | async-start | bytes 10485760 | tf_op jit(solution)/shard_map/all_gather | solution.py:121
  69.4 537.0 %all-gather.60.cloned.1.call-start = ((), (), s32[]{:S(2)}) async-start(), calls=%async_computation.29 | async-start | bytes 10485760 | tf_op jit(solution)/shard_map/all_gather | solution.py:121
  99.6 656.4 %all-gather.56.cloned.1.call-start = ((), (), s32[]{:S(2)}) async-start(), calls=%async_computation.27 | async-start | bytes 10485760 | tf_op jit(solution)/shard_map/all_gather | solution.py:120
  129.5 775.8 %all-gather.64.cloned.1.call-start = ((), (), s32[]{:S(2)}) async-start(), calls=%async_computation.31 | async-start | bytes 10485760 | tf_op jit(solution)/shard_map/all_gather | solution.py:122
  159.5 776.8 %all-gather.66.cloned.1.call-start = ((), (), s32[]{:S(2)}) async-start(), calls=%async_computation.32 | async-start | bytes 2359296 | tf_op jit(solution)/shard_map/all_gather | solution.py:106
  160.2 873.4 %all-gather.74.cloned.1.call-start = ((), (), s32[]{:S(2)}) async-start(), calls=%async_computation.50 | async-start | bytes 6553600 | tf_op jit(solution)/shard_map/all_gather | solution.py:147
  186.6 601.6 %copy-start.54 = (f32[8,1,256]{2,1,0:T(1,128)}, f32[8,1,256]{2,1,0:T(1,128)S(1)}, u32[]{:S(2)}) copy-start(f32[8,1,256]{2,1,0:T(1,128)S(1)} %convert_element_type.420) | copy-start | bytes 24580
  194.6 593.7 %copy-start.52 = (f32[8,1,256]{2,1,0:T(1,128)}, f32[8,1,256]{2,1,0:T(1,128)S(1)}, u32[]{:S(2)}) copy-start(f32[8,1,256]{2,1,0:T(1,128)S(1)} %convert_element_type.419) | copy-start | bytes 24580
  800.9 331.3 %all-gather.78.cloned.1.call-start = ((), (), s32[]{:S(2)}) async-start(), calls=%async_computation.52 | async-start | bytes 6553600 | tf_op jit(solution)/shard_map/all_gather | solution.py:147
  801.6 429.0 %all-gather.80.cloned.1.call-start = ((), (), s32[]{:S(2)}) async-start(), calls=%async_computation.53 | async-start | bytes 6553600 | tf_op jit(solution)/shard_map/all_gather | solution.py:148
  912.6 467.3 %all-gather.68.cloned.1.call-start = ((), (), s32[]{:S(2)}) async-start(), calls=%async_computation.33 | async-start | bytes 10485760 | tf_op jit(solution)/shard_map/all_gather | solution.py:123
  936.3 516.7 %all-gather.70.cloned.1.call-start = ((), (), s32[]{:S(2)}) async-start(), calls=%async_computation.34 | async-start | bytes 11796480 | tf_op jit(solution)/shard_map/all_gather | solution.py:176
  945.2 440.2 %copy-start.56 = (f32[8,1,256]{2,1,0:T(1,128)}, f32[8,1,256]{2,1,0:T(1,128)S(1)}, u32[]{:S(2)}) copy-start(f32[8,1,256]{2,1,0:T(1,128)S(1)} %convert_element_type.421) | copy-start | bytes 24580
  946.5 284.1 %copy-start.32 = (pred[320,1280]{1,0:T(8,128)(4,1)}, pred[320,1280]{1,0:T(8,128)(4,1)S(1)}, u32[]{:S(2)}) copy-start(pred[320,1280]{1,0:T(8,128)(4,1)S(1)} %fusion.62) | copy-start | bytes 1228804
  1388.5 196.8 %reduce-scatter.21.cloned.1.call-start = ((), (), s32[]{:S(2)}) async-start(), calls=%async_computation.35 | async-start | bytes 11796480 | tf_op jit(solution)/shard_map/reduce_scatter | solution.py:180
  1503.5 111.7 %all-gather.44.cloned.1.call-start = ((), (), s32[]{:S(2)}) async-start(), calls=%async_computation.20 | async-start | bytes 2359296 | tf_op jit(solution)/shard_map/all_gather | solution.py:105
  1504.1 176.8 %all-gather.72.cloned.1.call-start = ((), (), s32[]{:S(2)}) async-start(), calls=%async_computation.36 | async-start | bytes 11796480 | tf_op jit(solution)/shard_map/all_gather | solution.py:235
  1591.8 237.2 %all-gather.46.cloned.1.call-start = ((), (), s32[]{:S(2)}) async-start(), calls=%async_computation.21 | async-start | bytes 10485760 | tf_op jit(solution)/shard_map/all_gather | solution.py:122
  1615.2 244.9 %all-gather.48.cloned.1.call-start = ((), (), s32[]{:S(2)}) async-start(), calls=%async_computation.22 | async-start | bytes 2359296 | tf_op jit(solution)/shard_map/all_gather | solution.py:106
  1615.9 329.2 %reduce-scatter.23.cloned.1.call-start = ((), (), s32[]{:S(2)}) async-start(), calls=%async_computation.37 | async-start | bytes 11796480 | tf_op jit(solution)/shard_map/reduce_scatter | solution.py:246
  1746.6 307.8 %all-gather.76.cloned.1.call-start = ((), (), s32[]{:S(2)}) async-start(), calls=%async_computation.51 | async-start | bytes 6553600 | tf_op jit(solution)/shard_map/all_gather | solution.py:148
  1836.4 355.4 %all-gather.50.cloned.1.call-start = ((), (), s32[]{:S(2)}) async-start(), calls=%async_computation.23 | async-start | bytes 10485760 | tf_op jit(solution)/shard_map/all_gather | solution.py:123
  1860.1 429.0 %reduce-scatter.49.cloned.1.call-start = ((), (), s32[]{:S(2)}) async-start(), calls=%async_computation.54 | async-start | bytes 6553600
  2001.8 383.8 %reduce-scatter.25.cloned.1.call-start = ((), (), s32[]{:S(2)}) async-start(), calls=%async_computation.38 | async-start | bytes 6553600 | tf_op jit(solution)/shard_map/reduce_scatter | solution.py:298
  2044.6 407.1 %all-gather.52.cloned.1.call-start = ((), (), s32[]{:S(2)}) async-start(), calls=%async_computation.24 | async-start | bytes 11796480 | tf_op jit(solution)/shard_map/all_gather | solution.py:176
  2200.5 397.8 %reduce-scatter.39.cloned.1.call-start = ((), (), s32[]{:S(2)}) async-start(), calls=%async_computation.45 | async-start | bytes 10485760 | tf_op jit(solution)/shard_map/reduce_scatter | solution.py:340
  2209.1 536.7 %reduce-scatter.35.cloned.1.call-start = ((), (), s32[]{:S(2)}) async-start(), calls=%async_computation.43 | async-start | bytes 10485760 | tf_op jit(solution)/shard_map/reduce_scatter | solution.py:337
  2305.6 587.7 %reduce-scatter.31.cloned.1.call-start = ((), (), s32[]{:S(2)}) async-start(), calls=%async_computation.41 | async-start | bytes 10485760 | tf_op jit(solution)/shard_map/reduce_scatter | solution.py:334
  2414.7 564.7 %reduce-scatter.19.cloned.1.call-start = ((), (), s32[]{:S(2)}) async-start(), calls=%async_computation.25 | async-start | bytes 11796480 | tf_op jit(solution)/shard_map/reduce_scatter | solution.py:180
  2497.9 560.5 %reduce-scatter.47.cloned.1.call-start = ((), (), s32[]{:S(2)}) async-start(), calls=%async_computation.49 | async-start | bytes 5242880 | tf_op jit(solution)/shard_map/reduce_scatter | solution.py:349
  2515.4 622.7 %reduce-scatter.45.cloned.1.call-start = ((), (), s32[]{:S(2)}) async-start(), calls=%async_computation.48 | async-start | bytes 5242880 | tf_op jit(solution)/shard_map/reduce_scatter | solution.py:346
  2532.3 685.4 %reduce-scatter.43.cloned.1.call-start = ((), (), s32[]{:S(2)}) async-start(), calls=%async_computation.47 | async-start | bytes 5242880 | tf_op jit(solution)/shard_map/reduce_scatter | solution.py:343
  2549.3 815.8 %reduce-scatter.27.cloned.1.call-start = ((), (), s32[]{:S(2)}) async-start(), calls=%async_computation.39 | async-start | bytes 10485760 | tf_op jit(solution)/shard_map/reduce_scatter | solution.py:331
  2559.8 850.9 %reduce-scatter.41.cloned.1.call-start = ((), (), s32[]{:S(2)}) async-start(), calls=%async_computation.46 | async-start | bytes 2359296 | tf_op jit(solution)/shard_map/reduce_scatter | solution.py:375
  2598.3 295.1 %copy-start.79 = (bf16[256]{0:T(256)(128)(2,1)S(1)}, bf16[256]{0:T(256)(128)(2,1)}, u32[]{:S(2)}) copy-start(bf16[256]{0:T(256)(128)(2,1)} %param.26) | copy-start | bytes 1540
  2598.3 295.1 %copy-start.81 = (u32[32]{0:T(128)S(1)}, u32[32]{0:T(128)}, u32[]{:S(2)}) copy-start(u32[32]{0:T(128)} %constant.69) | copy-start | bytes 388
  2598.3 295.7 %copy-start.80 = (u32[32]{0:T(128)S(1)}, u32[32]{0:T(128)}, u32[]{:S(2)}) copy-start(u32[32]{0:T(128)} %constant.65) | copy-start | bytes 388
  2598.3 856.9 %reduce-scatter.37.cloned.1.call-start = ((), (), s32[]{:S(2)}) async-start(), calls=%async_computation.44 | async-start | bytes 2359296 | tf_op jit(solution)/shard_map/reduce_scatter | solution.py:372
  2745.8 235.3 %copy-start.61 = (f32[8,1,256]{2,1,0:T(1,128)S(1)}, f32[8,1,256]{2,1,0:T(1,128)}, u32[]{:S(2)}) copy-start(f32[8,1,256]{2,1,0:T(1,128)} %copy-done.60) | copy-start | bytes 24580
  2745.8 235.3 %copy-start.70 = (f32[320]{0:T(512)S(1)}, f32[320]{0:T(512)}, u32[]{:S(2)}) copy-start(f32[320]{0:T(512)} %copy-done.69) | copy-start | bytes 3844
  2745.9 754.2 %reduce-scatter.33.cloned.1.call-start = ((), (), s32[]{:S(2)}) async-start(), calls=%async_computation.42 | async-start | bytes 2359296 | tf_op jit(solution)/shard_map/reduce_scatter | solution.py:369
  2893.3 651.1 %reduce-scatter.29.cloned.1.call-start = ((), (), s32[]{:S(2)}) async-start(), calls=%async_computation.40 | async-start | bytes 2359296 | tf_op jit(solution)/shard_map/reduce_scatter | solution.py:366
  (75 other events, 3207.5 us)
Sparse Core Ops, SparseCore 0:
  9.9 29.3 all-gather.35
  41.2 28.1 all-gather.39
  71.3 28.1 all-gather.57
  101.2 28.1 all-gather.53
  131.2 28.1 all-gather.61
  160.9 146.6 all-gather.37
  309.1 147.8 all-gather.41
  458.6 147.8 all-gather.59
  608.0 147.8 all-gather.55
  757.4 147.8 all-gather.63
  907.1 29.0 all-gather.65
  938.3 95.2 all-gather.73
  1035.7 96.4 all-gather.77
  1134.1 96.4 all-gather.79
  1232.0 147.8 all-gather.67
  1388.6 64.4 all-gather.69
  1503.6 81.5 reduce-scatter.20
  1587.0 28.1 all-gather.43
  1617.6 63.2 all-gather.71
  1682.3 146.6 all-gather.45
  1830.9 29.0 all-gather.47
  1863.6 81.5 reduce-scatter.22
  1947.3 95.2 all-gather.75
  2044.0 147.8 all-gather.49
  2194.2 94.9 reduce-scatter.48
  2291.3 94.2 reduce-scatter.24
  2387.9 63.7 all-gather.51
  2454.1 144.1 reduce-scatter.38
  2600.6 145.1 reduce-scatter.34
  2748.0 145.1 reduce-scatter.30
  2896.8 82.6 reduce-scatter.18
  2981.7 76.7 reduce-scatter.46
  3060.7 77.2 reduce-scatter.44
  3140.3 77.2 reduce-scatter.42
  3220.1 144.9 reduce-scatter.26
  3368.6 42.1 reduce-scatter.40
  3413.9 41.2 reduce-scatter.36
  3458.8 41.2 reduce-scatter.32
  3503.2 41.1 reduce-scatter.28
where the time goes:
time: 3560 us; the launch traced here: 3550 us
  waiting for transfers between devices  2790 us (78%)
  matrix products  440 us (12%)
  other arithmetic  123 us (3%)
  blocking collectives  96.6 us (3%)
  local copies, waits for them, and re-layouts  80.6 us (2%)
    all_gather x2, waiting for transfers between devices, forward(): lax.all_gather(column_blocks[1], 'blk', axis=0, tiled=True)  281 us
    all_gather x2, waiting for transfers between devices, forward(): lax.all_gather(column_blocks[3], 'blk', axis=1, tiled=True)  256 us
    all_gather x2, waiting for transfers between devices, forward(): lax.all_gather(column_blocks[0], 'blk', axis=0, tiled=True)  252 us
    all_gather x2, waiting for transfers between devices, forward(): lax.all_gather(column_blocks[2], 'blk', axis=0, tiled=True)  186 us
    all_gather x2, waiting for transfers between devices, forward(): key_piece = lax.all_gather(key_blocks, 'blk', axis=1, tiled=True)  169 us
    reduce_scatter x1, waiting for transfers between devices, local(): lax.psum_scatter(value_part.astype(jnp.bfloat16), 'blk', scatter_dimensio...  147 us
    reduce_scatter x1, waiting for transfers between devices, local(): lax.psum_scatter(key_part.astype(jnp.bfloat16), 'blk', scatter_dimension=...  147 us
    reduce_scatter x2, waiting for transfers between devices, forward(): lax.psum_scatter(jnp.dot(activated, down_local, preferred_element_type=jn...  147 us
  transfers between devices with their start and end apart: 39, of which 38 were waited for; matrix products, arithmetic and copies ran while one was open for 16% of the time, Pallas kernels for 0%

commit v1 on v0

v1 whole, which is shorter than its diff:
```python
import functools

import jax
import jax.numpy as jnp
from jax import lax
from jax.experimental import pallas as pl
from jax.experimental.pallas import tpu as pltpu
from jax.sharding import PartitionSpec as P

MESH = pl.DeviceIdType.MESH

D = 2048
HD = 128
EPS = 1e-06
ROPE_BASE = 500000.0
NEG_FILL = -1e30
VMEM_LIMIT = 60 * 1024 * 1024
SCALE = HD ** (-0.5)


def busy(micros):
    return pl.CostEstimate(flops=0, bytes_accessed=int(micros * 3.5e6), transcendentals=0)


def layout(seq_lengths, row_count):
    indices = jnp.arange(row_count, dtype=jnp.int32)
    first_end = seq_lengths[0]
    second_end = seq_lengths[0] + seq_lengths[1]
    segment = (indices >= first_end).astype(jnp.int32) + (indices >= second_end).astype(jnp.int32)
    offsets = jnp.where(segment == 0, 0, jnp.where(segment == 1, first_end, second_end))
    return (segment, indices - offsets)


def rope_tables(position):
    frequency = ROPE_BASE ** (-jnp.arange(0, HD, 2, dtype=jnp.float32) / HD)
    angles = position.astype(jnp.float32)[:, None] * frequency[None, :]
    cosine, sine = jnp.cos(angles), jnp.sin(angles)
    return (jnp.concatenate([cosine, cosine], -1), jnp.concatenate([-sine, sine], -1))


def rms_pair(values):
    inverse = lax.rsqrt(jnp.mean(values * values, axis=-1, keepdims=True) + EPS)
    return (values * inverse, inverse)


def norm_back(normed, inverse, grad_normed):
    return inverse * (grad_normed - normed * jnp.mean(grad_normed * normed, axis=-1, keepdims=True))


def dot(left, right):
    return jnp.dot(left, right, preferred_element_type=jnp.float32)


def contract_rows(left, right):
    return lax.dot_general(
        left, right, (((0,), (0,)), ((), ())), preferred_element_type=jnp.float32
    )


def contract_cols(left, right):
    return lax.dot_general(
        left, right, (((1,), (1,)), ((), ())), preferred_element_type=jnp.float32
    )


def flip(me, k):
    out, bit = me, 1
    while bit <= k:
        if k & bit:
            out = out + bit * (1 - 2 * ((me // bit) % 2))
        bit *= 2
    return out


def greet(axis, me, others):
    barrier = pltpu.get_barrier_semaphore()
    for k in others:
        pl.semaphore_signal(barrier, inc=1, device_id={axis: flip(me, k)}, device_id_type=MESH)
    pl.semaphore_wait(barrier, len(others))


def gather_body(width, slots, side, *refs):
    if side is None:
        x_ref, out_ref, here, send, recv = refs
    else:
        x_ref, side_ref, out_ref, side_out, here, send, recv, side_send, side_recv = refs
    me = lax.axis_index("wide")
    rows = x_ref.shape[0]
    half = rows // 2
    evens = list(range(2, width, 2))
    peers = [{"wide": flip(me, k)} for k in [1] + evens]
    if side is not None:
        hops = Hops(width // slots, slots, rows)
        peers = peers + [{"blk": (hops.plane + k) % hops.planes} for k in range(1, hops.planes)]
    hello(peers)
    if side is not None:
        job = hops.join if side == "join" else hops.spread
        job(side_ref, side_out, side_send, side_recv, True, True)

    def spot(who, first, count):
        base = ((who % slots) * (width // slots) + who // slots) * rows
        return out_ref.at[pl.ds(pl.multiple_of(base + first, half), count)]

    def move(origin, target, k, part):
        if origin is None:
            source = x_ref.at[pl.ds(part * half, half)]
        else:
            source = spot(flip(me, origin), part * half, half)
        return pltpu.make_async_remote_copy(
            src_ref=source,
            dst_ref=spot(flip(flip(me, target), k), part * half, half),
            send_sem=send.at[k, part],
            recv_sem=recv.at[k, part],
            device_id={"wide": flip(me, target)},
            device_id_type=MESH,
        )

    def arrived(k, part):
        block = spot(flip(me, k), part * half, half)
        pltpu.make_async_copy(block, block, recv.at[k, part]).wait()

    moves = []

    def go(origin, target, k, part):
        copy = move(origin, target, k, part)
        copy.start()
        moves.append(copy)

    mine = pltpu.make_async_copy(x_ref, spot(me, 0, rows), here)
    mine.start()
    if width == 8:
        go(None, 2, 2, 0)
        go(None, 4, 4, 1)
        go(None, 2, 2, 1)
        go(None, 4, 4, 0)
        go(None, 1, 1, 0)
        go(None, 1, 1, 1)
        arrived(2, 0)
        go(2, 4, 6, 0)
        go(2, 1, 3, 0)
        arrived(4, 1)
        go(4, 2, 6, 1)
        go(4, 1, 5, 1)
        order = [(2, 1), (4, 0), (6, 0), (6, 1)]
    else:
        for k in evens:
            go(None, k, k, 0)
            go(None, k, k, 1)
        go(None, 1, 1, 0)
        go(None, 1, 1, 1)
        order = [(k, part) for k in evens for part in (0, 1)]
    for k, part in order:
        arrived(k, part)
        go(k, 1, k + 1, part)
    for k in range(1, width, 2):
        for part in (0, 1):
            arrived(k, part)
    for copy in moves:
        copy.wait_send()
    mine.wait()
    if side is not None:
        job(side_ref, side_out, side_send, side_recv, True, False)


def gather(x, width, slots, ident, name, side=None, side_x=None):
    rows, cols = x.shape
    planes = width // slots
    dma = pltpu.SemaphoreType.DMA
    shapes = [jax.ShapeDtypeStruct((rows * width, cols), x.dtype)]
    scratch = [dma, dma((width, 2)), dma((width, 2))]
    inputs = [x]
    if side is not None:
        inputs.append(side_x)
        extent = rows if side == "join" else many_rows(planes, rows)
        shapes.append(jax.ShapeDtypeStruct((extent, cols), side_x.dtype))
        scratch += [dma((planes,)), dma((planes,))]
    outs = pl.pallas_call(
        functools.partial(gather_body, width, slots, side),
        out_shape=shapes,
        in_specs=[pl.BlockSpec(memory_space=pl.ANY)] * len(inputs),
        out_specs=[pl.BlockSpec(memory_space=pl.ANY)] * len(shapes),
        scratch_shapes=scratch,
        cost_estimate=busy(50),
        compiler_params=pltpu.CompilerParams(collective_id=ident, has_side_effects=True, vmem_limit_bytes=VMEM_LIMIT),
        name=name,
    )(*inputs)
    return outs[0] if side is None else outs


def scatter_body(width, slots, flat, count, step, *refs):
    lefts, rights = refs[:count], refs[count : 2 * count]
    out_ref, odd, even, from_twin, from_far, passing, sends, recvs, pass_send, pass_recv, twin_send, twin_recv = refs[2 * count :]
    me = lax.axis_index("wide")
    rows, cols = out_ref.shape
    half = rows // 2
    evens = list(range(2, width, 2))
    greet("wide", me, [1] + evens)
    dims = (((1,), (1 if flat else 0,)), ((), ()))

    def produce(k, put, adds=()):
        who = flip(me, k)
        start = pl.multiple_of(((who % slots) * (width // slots) + who // slots) * rows, rows)

        def tile(n, carry):
            at = pl.ds(pl.multiple_of(n * step, step), step)
            total = None
            for left, right in zip(lefts, rights):
                other = right[at, :] if flat else right[:, at]
                term = lax.dot_general(
                    left[pl.ds(start, rows), :], other, dims, preferred_element_type=jnp.float32
                )
                total = term if total is None else total + term
            for ref in adds:
                total = total + ref[:, at].astype(jnp.float32)
            put[:, at] = total.astype(put.dtype)
            return carry

        lax.fori_loop(0, cols // step, tile, 0)

    def twin(k):
        return pltpu.make_async_remote_copy(
            src_ref=odd.at[k // 2],
            dst_ref=from_twin.at[k // 2],
            send_sem=twin_send.at[k // 2],
            recv_sem=twin_recv.at[k // 2],
            device_id={"wide": flip(me, 1)},
            device_id_type=MESH,
        )

    def far(k, part):
        at = pl.ds(part * half, half)
        return pltpu.make_async_remote_copy(
            src_ref=even.at[k // 2 - 1, at],
            dst_ref=from_far.at[k // 2 - 1, at],
            send_sem=sends.at[k // 2 - 1, part],
            recv_sem=recvs.at[k // 2 - 1, part],
            device_id={"wide": flip(me, k)},
            device_id_type=MESH,
        )

    def relay(part):
        at = pl.ds(part * half, half)
        return pltpu.make_async_remote_copy(
            src_ref=even.at[2, at],
            dst_ref=passing.at[part],
            send_sem=pass_send.at[part],
            recv_sem=pass_recv.at[part],
            device_id={"wide": flip(me, 2 if part == 0 else 4)},
            device_id_type=MESH,
        )

    def to_twin(k):
        produce(k + 1, odd.at[k // 2])
        twin(k).start()

    def merge(k):
        twin(k).wait_recv()
        produce(k, even.at[k // 2 - 1], (from_twin.at[k // 2],))

    def pass_on(k, part):
        relay(part).wait_recv()
        at = pl.ds(part * half, half)
        even[k // 2 - 1, at, :] = (
            even[k // 2 - 1, at, :].astype(jnp.float32) + passing[part].astype(jnp.float32)
        ).astype(jnp.bfloat16)
        far(k, part).start()

    if width == 8:
        to_twin(6)
        to_twin(2)
        to_twin(4)
        merge(6)
        relay(0).start()
        relay(1).start()
        merge(2)
        far(2, 0).start()
        merge(4)
        far(4, 1).start()
        to_twin(0)
        pass_on(2, 1)
        pass_on(4, 0)
        sources = [2, 4]
    else:
        for k in evens:
            to_twin(k)
        to_twin(0)
        for k in evens:
            merge(k)
            far(k, 0).start()
            far(k, 1).start()
        sources = evens
    twin(0).wait_recv()
    produce(0, out_ref, (from_twin.at[0],))
    for k in sources:
        far(k, 0).wait_recv()
        far(k, 1).wait_recv()
        out_ref[...] = out_ref[...] + from_far[k // 2 - 1].astype(jnp.float32)
    for k in sources:
        far(k, 0).wait_send()
        far(k, 1).wait_send()
    for k in range(0, width, 2):
        twin(k).wait_send()
    if width == 8:
        relay(0).wait_send()
        relay(1).wait_send()


def scatter(lefts, rights, width, slots, flat, ident, name, step=1024):
    rows = lefts[0].shape[0] // width
    cols = rights[0].shape[0 if flat else 1]
    chips = width // 2
    low = jnp.bfloat16
    block = lambda n: pltpu.VMEM((n, rows, cols), low)
    dma = pltpu.SemaphoreType.DMA
    return pl.pallas_call(
        functools.partial(scatter_body, width, slots, flat, len(lefts), step),
        out_shape=jax.ShapeDtypeStruct((rows, cols), jnp.float32),
        in_specs=[pl.BlockSpec(memory_space=pltpu.VMEM)] * (2 * len(lefts)),
        out_specs=pl.BlockSpec(memory_space=pltpu.VMEM),
        scratch_shapes=[
            block(chips), block(chips - 1), block(chips), block(chips - 1),
            pltpu.VMEM((2, rows // 2, cols), low),
            dma((chips - 1, 2)), dma((chips - 1, 2)), dma((2,)), dma((2,)), dma((chips,)), dma((chips,)),
        ],
        cost_estimate=busy(60),
        compiler_params=pltpu.CompilerParams(collective_id=ident, has_side_effects=True, vmem_limit_bytes=VMEM_LIMIT),
        name=name,
    )(*lefts, *rights)


def total_body(axis, width, x_ref, out_ref, slots, send, recv):
    me = lax.axis_index(axis)
    others = list(range(1, width))
    greet(axis, me, others)
    moves = []
    for k in others:
        copy = pltpu.make_async_remote_copy(
            src_ref=x_ref,
            dst_ref=slots.at[k - 1],
            send_sem=send.at[k - 1],
            recv_sem=recv.at[k - 1],
            device_id={axis: flip(me, k)},
            device_id_type=MESH,
        )
        copy.start()
        moves.append(copy)
    out_ref[...] = x_ref[...]
    for copy, k in zip(moves, others):
        copy.wait_recv()
        out_ref[...] = out_ref[...] + slots[k - 1]
    for copy in moves:
        copy.wait_send()


def total(x, axis, width, ident, name):
    return pl.pallas_call(
        functools.partial(total_body, axis, width),
        out_shape=jax.ShapeDtypeStruct(x.shape, x.dtype),
        in_specs=[pl.BlockSpec(memory_space=pltpu.VMEM)],
        out_specs=pl.BlockSpec(memory_space=pltpu.VMEM),
        scratch_shapes=[
            pltpu.VMEM((width - 1,) + x.shape, x.dtype),
            pltpu.SemaphoreType.DMA((width - 1,)),
            pltpu.SemaphoreType.DMA((width - 1,)),
        ],
        cost_estimate=busy(7),
        compiler_params=pltpu.CompilerParams(collective_id=ident, has_side_effects=True, vmem_limit_bytes=VMEM_LIMIT),
        name=name,
    )(x)


class Hops:
    def __init__(self, planes, slots, rows):
        self.planes, self.slots = planes, slots
        self.count = max(n for n in range(1, planes + 1) if planes % n == 0 and rows % (16 * n) == 0)
        self.per = planes // self.count
        self.piece = rows // self.count
        self.plane, self.place = lax.axis_index("blk"), lax.axis_index("wide")
        self.chip, self.slot = self.place // slots, self.place % slots
        self.active = self.chip // self.count == self.plane % self.per

    def peers(self):
        near = [{"wide": (self.chip + k) % self.planes * self.slots + self.slot} for k in range(1, self.planes)]
        return near + [{"blk": (self.plane + k) % self.planes} for k in range(1, self.planes)]

    def when(self, condition, action):
        if self.per == 1:
            action()
        else:
            pl.when(condition)(action)

    def split(self, condition, yes, no):
        if self.per == 1:
            yes()
        else:
            pl.when(condition)(yes)
            pl.when(jnp.logical_not(condition))(no)

    def cut(self, ref, index):
        return ref.at[pl.ds(pl.multiple_of(index * self.piece, self.piece), self.piece)]

    def remote(self, src, dst, send, recv, device):
        return pltpu.make_async_remote_copy(
            src_ref=src, dst_ref=dst, send_sem=send, recv_sem=recv, device_id=device, device_id_type=MESH
        )

    def spread(self, some, many, send, recv, across, start):
        if across:
            axis, here = "blk", self.plane
            targets = [
                ((self.plane // self.per + k) % self.count) for k in range(self.count)
            ]
            device = lambda piece: piece * self.per + self.chip // self.count
        else:
            axis, here = "wide", self.chip
            targets = [((self.chip + k) % self.count) for k in range(self.count)]
            device = lambda piece: (self.plane % self.per) * self.count + piece
        address = (lambda who: {"blk": who}) if across else (
            lambda who: {"wide": who * self.slots + self.slot}
        )
        for k, piece in enumerate(targets):
            who = device(piece)
            far = self.remote(
                self.cut(some, piece), self.cut(many, here), send.at[piece],
                recv.at[(here - who + self.planes) % self.planes], address(who),
            )
            own = pltpu.make_async_copy(self.cut(some, piece), self.cut(many, here), send.at[piece])
            if k:
                far.start() if start else far.wait_send()
            elif start:
                self.split(self.active, own.start, far.start)
            else:
                self.split(self.active, own.wait, far.wait_send)
        if not start:
            def receive():
                for k in range(1, self.planes):
                    block = self.cut(many, (here + k) % self.planes)
                    pltpu.make_async_copy(block, block, recv.at[k]).wait()

            self.when(self.active, receive)

    def join(self, many, some, send, recv, across, start):
        if across:
            here = self.plane
            index = self.plane // self.per
            address = lambda who: {"blk": who}
        else:
            here = self.chip
            index = self.chip % self.count
            address = lambda who: {"wide": who * self.slots + self.slot}

        def give():
            for k in range(1, self.planes):
                who = (here + k) % self.planes
                far = self.remote(
                    self.cut(many, who), self.cut(some, index), send.at[k], recv.at[index], address(who)
                )
                far.start() if start else far.wait_send()
            own = pltpu.make_async_copy(self.cut(many, here), self.cut(some, index), send.at[0])
            own.start() if start else own.wait()

        self.when(self.active, give)
        if not start:
            for k in range(self.count):
                piece = (index + k) % self.count
                block = self.cut(some, piece)
                arrival = pltpu.make_async_copy(block, block, recv.at[piece])
                if k:
                    arrival.wait()
                elif self.per > 1:
                    pl.when(jnp.logical_not(self.active))(arrival.wait)


def hello(peers):
    barrier = pltpu.get_barrier_semaphore()
    for peer in peers:
        pl.semaphore_signal(barrier, inc=1, device_id=peer, device_id_type=MESH)
    pl.semaphore_wait(barrier, len(peers))


def turn_in_body(planes, slots, x_ref, c_ref, near_x, near_c, out_ref, *sems):
    hops = Hops(planes, slots, x_ref.shape[0])
    hello(hops.peers())
    hops.spread(x_ref, near_x, sems[0], sems[1], False, True)
    hops.spread(x_ref, near_x, sems[0], sems[1], False, False)
    hops.join(near_x, out_ref, sems[2], sems[3], True, True)
    hops.spread(c_ref, near_c, sems[4], sems[5], False, True)
    hops.spread(c_ref, near_c, sems[4], sems[5], False, False)
    hops.join(near_x, out_ref, sems[2], sems[3], True, False)


def turn_out_body(planes, slots, x_ref, far_c, far_x, out_c, out_ref, *sems):
    hops = Hops(planes, slots, x_ref.shape[0])
    hello(hops.peers())
    hops.spread(x_ref, far_x, sems[0], sems[1], True, True)
    hops.join(far_c, out_c, sems[2], sems[3], False, True)
    hops.spread(x_ref, far_x, sems[0], sems[1], True, False)
    hops.join(far_x, out_ref, sems[4], sems[5], False, True)
    hops.join(far_c, out_c, sems[2], sems[3], False, False)
    hops.join(far_x, out_ref, sems[4], sems[5], False, False)


def many_rows(planes, rows):
    count = max(n for n in range(1, planes + 1) if planes % n == 0 and rows % (16 * n) == 0)
    return planes * (rows // count)


def turn(body, inputs, outputs, planes, slots, ident, name):
    rows, cols = inputs[0].shape
    low = inputs[0].dtype
    shape = lambda many: jax.ShapeDtypeStruct((many_rows(planes, rows) if many else rows, cols), low)
    return pl.pallas_call(
        functools.partial(body, planes, slots),
        out_shape=[shape(many) for many in outputs],
        in_specs=[pl.BlockSpec(memory_space=pl.ANY)] * len(inputs),
        out_specs=[pl.BlockSpec(memory_space=pl.ANY)] * len(outputs),
        scratch_shapes=[pltpu.SemaphoreType.DMA((planes,))] * 6,
        cost_estimate=busy(45),
        compiler_params=pltpu.CompilerParams(collective_id=ident, has_side_effects=True, vmem_limit_bytes=VMEM_LIMIT),
        name=name,
    )(*inputs)


def mask_scores(scores, first, begin, size):
    span = scores.shape[0]
    index = lax.broadcasted_iota(jnp.int32, scores.shape, 0)
    query = lax.broadcasted_iota(jnp.int32, scores.shape, 1) + first
    return jnp.where((index <= query) & (index >= begin), scores, NEG_FILL)


def nt(left, right):
    return lax.dot_general(left, right, (((1,), (1,)), ((), ())), preferred_element_type=jnp.float32)


def nn(left, right):
    return jnp.dot(left, right, preferred_element_type=jnp.float32)


def piece_map(span, size):
    planes = span // size
    count = max(n for n in range(1, planes + 1) if planes % n == 0 and size % (16 * n) == 0)
    per, piece = planes // count, size // count
    pairs = []
    for t in range(count):
        for high in range(per):
            for low in range(count):
                natural = ((t * per + high) * count + low) * piece
                pairs.append((natural, ((high * count + low) * count + t) * piece))
    return pairs, piece


def attend_body(size, q_ref, k_ref, v_ref, inv_ref, gain_ref, cos_ref, sin_ref, begin_ref,
                qo_ref, ko_ref, vo_ref, mix_ref, log_ref):
    low = jnp.bfloat16
    span = q_ref.shape[0]

    def prepare(ref, col):
        value = ref[...] * inv_ref[:, col : col + 1] * gain_ref[col : col + 1, :]
        return (value * cos_ref[...] + pltpu.roll(value, HD // 2, 1) * sin_ref[...]).astype(low)

    pairs, piece = piece_map(span, size)

    def arrange(ref, value):
        for natural, block in pairs:
            ref[natural : natural + piece, :] = value[block : block + piece, :]

    arrange(qo_ref, prepare(q_ref, 0))
    arrange(ko_ref, prepare(k_ref, 1))
    arrange(vo_ref, v_ref[...].astype(low))
    flipped = vo_ref[...].astype(jnp.float32).T.astype(low)
    for i in range(span // size):
        last = (i + 1) * size
        cols = slice(i * size, last)
        scores = nt(ko_ref[:last, :], qo_ref[cols, :]) * SCALE
        scores = mask_scores(scores, i * size, begin_ref[:, cols], size)
        top = jnp.max(scores, axis=0, keepdims=True)
        raw = jnp.exp(scores - top)
        weight = jnp.sum(raw, axis=0, keepdims=True)
        mixed = nn(flipped[:, :last], raw.astype(low)) * (1.0 / weight)
        mixed = mixed.T.astype(low)
        for natural, block in pairs:
            if i * size <= natural < last:
                at = natural - i * size
                mix_ref[block : block + piece, :] = mixed[at : at + piece, :]
        log_ref[:, cols] = top + jnp.log(weight)


def attend(pre, inverse, gains, cosine, sine, begin, heads, size):
    slots, span, _ = pre.shape
    low, f32 = jnp.bfloat16, jnp.float32
    head = lambda offset: pl.BlockSpec((None, span, HD), lambda g, h: (g, 0, offset + h))
    every = lambda cols: pl.BlockSpec((None, span, cols), lambda g, h: (g, 0, 0))
    line = pl.BlockSpec((None, 1, span), lambda g, h: (g, 0, 0))
    out = jax.ShapeDtypeStruct((slots, span, heads * HD), low)
    return pl.pallas_call(
        functools.partial(attend_body, size),
        grid=(slots, heads),
        out_shape=[out, out, out, out, jax.ShapeDtypeStruct((slots, heads, 1, span), f32)],
        in_specs=[
            head(0), head(heads), head(2 * heads), every(2),
            pl.BlockSpec((2, HD), lambda g, h: (0, h)), every(HD), every(HD), line,
        ],
        out_specs=[head(0)] * 4 + [pl.BlockSpec((None, None, 1, span), lambda g, h: (g, h, 0, 0))],
        compiler_params=pltpu.CompilerParams(vmem_limit_bytes=VMEM_LIMIT),
        cost_estimate=busy(17),
        name="attend",
    )(pre, pre, pre, inverse, gains, cosine, sine, begin)


def attend_back_body(size, q_ref, k_ref, v_ref, g_ref, log_ref, qp_ref, kp_ref, inv_ref, gain_ref,
                     cos_ref, sin_ref, begin_ref, sq_ref, sk_ref, gv_ref, sums_ref, part_ref,
                     keys_sum, values_sum, queries_sum, held, g_held):
    low = jnp.bfloat16
    span = q_ref.shape[0]
    pairs, piece = piece_map(span, size)
    for natural, block in pairs:
        g_held[natural : natural + piece, :] = g_ref[block : block + piece, :]
    flipped = k_ref[...].astype(jnp.float32).T.astype(low)
    keys_sum[...] = jnp.zeros_like(keys_sum)
    values_sum[...] = jnp.zeros_like(values_sum)
    for i in range(span // size):
        last = (i + 1) * size
        cols = slice(i * size, last)
        scores = nt(k_ref[:last, :], q_ref[cols, :]) * SCALE
        scores = mask_scores(scores, i * size, begin_ref[:, cols], size)
        probs = jnp.exp(scores - log_ref[:, cols])
        grad_probs = nt(v_ref[:last, :], g_held[cols, :])
        delta = jnp.sum(probs * grad_probs, axis=0, keepdims=True)
        grad_scores = (probs * (grad_probs - delta)).astype(low)
        values_sum[:last, :] += nn(probs.astype(low), g_held[cols, :])
        keys_sum[:last, :] += nn(grad_scores, q_ref[cols, :])
        queries_sum[cols, :] = nn(flipped[:, :last], grad_scores).T

    def finish(total_ref, pre_ref, out_ref, col):
        for natural, block in pairs:
            held[block : block + piece, :] = total_ref[natural : natural + piece, :]
        grad = held[...] * SCALE
        back = grad * cos_ref[...] - pltpu.roll(grad, HD // 2, 1) * sin_ref[...]
        normed = pre_ref[...] * inv_ref[:, col : col + 1]
        part_ref[col : col + 1, :] = jnp.sum(back * normed, axis=0, keepdims=True)
        scaled = back * gain_ref[col : col + 1, :]
        out_ref[...] = scaled
        sums_ref[:, col : col + 1] = jnp.sum(scaled * normed, axis=1, keepdims=True)

    finish(queries_sum, qp_ref, sq_ref, 0)
    finish(keys_sum, kp_ref, sk_ref, 1)
    for natural, block in pairs:
        gv_ref[block : block + piece, :] = values_sum[natural : natural + piece, :].astype(low)


def attend_back(queries, keys, values, grads, logs, pre, inverse, gains, cosine, sine, begin, heads, size):
    slots, span, _ = pre.shape
    low, f32 = jnp.bfloat16, jnp.float32
    head = lambda offset: pl.BlockSpec((None, span, HD), lambda g, h: (g, 0, offset + h))
    every = lambda cols: pl.BlockSpec((None, span, cols), lambda g, h: (g, 0, 0))
    line = pl.BlockSpec((None, 1, span), lambda g, h: (g, 0, 0))
    wide = jax.ShapeDtypeStruct((slots, span, heads * HD), f32)
    return pl.pallas_call(
        functools.partial(attend_back_body, size),
        grid=(slots, heads),
        out_shape=[
            wide, wide, jax.ShapeDtypeStruct((slots, span, heads * HD), low),
            jax.ShapeDtypeStruct((heads, slots, span, 2), f32),
            jax.ShapeDtypeStruct((slots, 2, heads * HD), f32),
        ],
        in_specs=[
            head(0), head(0), head(0), head(0),
            pl.BlockSpec((None, None, 1, span), lambda g, h: (g, h, 0, 0)),
            head(0), head(heads), every(2),
            pl.BlockSpec((2, HD), lambda g, h: (0, h)), every(HD), every(HD), line,
        ],
        out_specs=[
            head(0), head(0), head(0),
            pl.BlockSpec((None, None, span, 2), lambda g, h: (h, g, 0, 0)),
            pl.BlockSpec((None, 2, HD), lambda g, h: (g, 0, h)),
        ],
        scratch_shapes=[pltpu.VMEM((span, HD), f32)] * 4 + [pltpu.VMEM((span, HD), low)],
        compiler_params=pltpu.CompilerParams(vmem_limit_bytes=VMEM_LIMIT),
        cost_estimate=busy(28),
        name="attend_back",
    )(queries, keys, values, grads, logs, pre, pre, inverse, gains, cosine, sine, begin)


def local(
    tokens,
    lengths,
    query_weight,
    key_weight,
    value_weight,
    output_weight,
    query_gain,
    key_gain,
    attention_gain,
    gate_weight,
    up_weight,
    down_weight,
    feedforward_gain,
    cotangent,
):
    low, f32 = jnp.bfloat16, jnp.float32
    planes, width = lax.axis_size("blk"), lax.axis_size("wide")
    slots = width // planes
    rows = tokens.shape[1]
    span = rows * planes
    count = slots * span
    share = query_weight.shape[1]
    heads = share // HD
    plane, place = lax.axis_index("blk"), lax.axis_index("wide")
    after = lambda value, *others: lax.optimization_barrier((value,) + others)[0]

    def over_blk(value, axis):
        return lax.psum_scatter(
            value.astype(low), "blk", scatter_dimension=axis, tiled=True
        ).astype(f32)

    _, near_cotangent, mine = turn(
        turn_in_body, [tokens[0], cotangent[0]], [True, True, False], planes, slots, 1, "turn_in"
    )
    qkv_rows = after(jnp.concatenate([query_weight, key_weight, value_weight], 1), mine)
    w_qkv = lax.all_gather(qkv_rows, "blk", axis=0, tiled=True)
    w_o = lax.all_gather(after(output_weight, w_qkv), "blk", axis=1, tiled=True)
    gains = jnp.stack([query_gain, key_gain]).astype(f32)
    both = after(jnp.stack([attention_gain, feedforward_gain]), w_qkv)
    both = lax.all_gather(both, "wide", axis=1, tiled=True).astype(f32)
    gain_mix, gain_feed = both[0], both[1]

    plane_lengths = lax.dynamic_slice_in_dim(lengths, plane * slots, slots, 0)
    segment, position = jax.vmap(lambda one: layout(one, span))(plane_lengths)
    begin = (jnp.arange(span, dtype=jnp.int32)[None] - position)[:, None, :]
    pairs, piece = piece_map(span, rows)
    order = sorted(pairs, key=lambda pair: pair[1])
    position = jnp.concatenate([position[:, at : at + piece] for at, _ in order], 1)
    cosine, sine = rope_tables(position.reshape(-1))
    cosine, sine = cosine.reshape(slots, span, HD), sine.reshape(slots, span, HD)

    inputs = gather(mine, width, slots, 2, "gather_tokens")
    pre = dot(inputs, w_qkv)
    squares = jnp.stack([jnp.sum(pre[:, a * share : (a + 1) * share] ** 2, -1) for a in (0, 1)])
    squares = total(squares.reshape(-1, 128), "wide", width, 3, "total_squares")
    inverse = lax.rsqrt(squares.reshape(2, count) / D + EPS)
    inv_cols = inverse.T.reshape(slots, span, 2)
    pre_groups = pre.reshape(slots, span, 3 * share)
    queries, keys, values, mixed, logs = attend(
        pre_groups, inv_cols, gains, cosine, sine, begin, heads, rows
    )
    mixed = mixed.reshape(count, share)
    projected = scatter([mixed], [w_o], width, slots, False, 4, "scatter_mixed")
    proj_normed, proj_inv = rms_pair(projected)
    hidden = mine.astype(f32) + proj_normed * gain_mix
    gathered, grad_out = gather(
        hidden.astype(low), width, slots, 5, "gather_hidden", "join", near_cotangent
    )
    grad_out = grad_out.astype(f32)
    gate = dot(gathered, gate_weight)
    upward = dot(gathered, up_weight)
    sigmoid = jax.nn.sigmoid(gate)
    activated = (gate * sigmoid * upward).astype(low)
    reduced = scatter([activated], [down_weight], width, slots, False, 6, "scatter_down")
    red_normed, red_inv = rms_pair(reduced)
    block_output = (hidden + red_normed * gain_feed).astype(low)

    feed_gain_part = jnp.sum(grad_out * red_normed, axis=0)
    grad_reduced = norm_back(red_normed, red_inv, grad_out * gain_feed).astype(low)
    grad_rows, far_output = gather(
        grad_reduced, width, slots, 7, "gather_grad", "spread", block_output
    )
    down_part = contract_rows(activated, grad_rows).astype(low)
    grad_rows, down_part = lax.optimization_barrier((grad_rows, down_part))
    down_grad = over_blk(down_part, 1)
    grad_act = contract_cols(grad_rows, down_weight)
    grad_up = (grad_act * gate * sigmoid).astype(low)
    grad_gate = (grad_act * upward * sigmoid * (1.0 + gate * (1.0 - sigmoid))).astype(low)
    gate_part = contract_rows(gathered, grad_gate).astype(low)
    grad_up, gate_part = lax.optimization_barrier((grad_up, gate_part))
    gate_grad = over_blk(gate_part, 0)
    grad_hidden = grad_out + scatter(
        [grad_gate, grad_up], [gate_weight, up_weight], width, slots, True, 8, "scatter_hidden"
    )
    up_part = contract_rows(gathered, after(grad_up, grad_hidden)).astype(low)
    up_grad = over_blk(up_part, 0)
    mix_gain_part = jnp.sum(grad_hidden * proj_normed, axis=0)
    grad_proj = norm_back(proj_normed, proj_inv, grad_hidden * gain_mix).astype(low)
    grad_proj = gather(after(grad_proj, up_part, down_grad), width, slots, 9, "gather_proj")
    output_part = contract_rows(mixed, grad_proj).astype(low)
    grad_mixed = contract_cols(grad_proj, w_o).astype(low).reshape(slots, span, share)
    grad_mixed = after(grad_mixed, gate_grad)
    scaled_q, scaled_k, grad_v, sums, parts = attend_back(
        queries, keys, values, grad_mixed, logs, pre_groups, inv_cols, gains, cosine, sine, begin,
        heads, rows,
    )
    means = jnp.sum(sums, axis=0).reshape(count, 2).T.reshape(-1, 128)
    means = total(means, "wide", width, 10, "total_means").reshape(2, count) / D

    def finish(scaled, index):
        normed = pre[:, index * share : (index + 1) * share] * inverse[index][:, None]
        scaled = scaled.reshape(count, share)
        return (inverse[index][:, None] * (scaled - normed * means[index][:, None])).astype(low)

    grads = jnp.concatenate([finish(scaled_q, 0), finish(scaled_k, 1), grad_v.reshape(count, share)], 1)
    grads = after(grads, up_grad)
    tokens_part = scatter([grads], [w_qkv], width, slots, True, 11, "scatter_tokens")
    _, block_output, tokens_grad = turn(
        turn_out_body, [(grad_hidden + tokens_part).astype(low), far_output], [True, False, False],
        planes, slots, 14, "turn_out",
    )
    output_grad = over_blk(output_part, 1)
    qkv_part = contract_rows(inputs, grads)
    qkv_grad = over_blk(qkv_part, 0)

    gain_parts = jnp.sum(parts, axis=0)
    local_gains = lax.dynamic_update_slice(jnp.zeros((2, D), f32), gain_parts, (0, place * share))
    sums = jnp.concatenate([local_gains, jnp.stack([mix_gain_part, feed_gain_part])])
    sums = total(sums.reshape(-1, 128), "wide", width, 12, "total_gains")
    sums = total(sums, "blk", planes, 13, "total_gains_blk").reshape(4, D)
    portion = D // (planes * width)
    sums = lax.dynamic_slice_in_dim(sums, (plane * width + place) * portion, portion, 1)
    return (
        block_output[None],
        tokens_grad[None].astype(f32),
        qkv_grad[:, :share],
        qkv_grad[:, share : 2 * share],
        qkv_grad[:, 2 * share :],
        output_grad,
        sums[0],
        sums[1],
        sums[2],
        gate_grad,
        up_grad,
        down_grad,
        sums[3],
    )


def solution(mesh):
    placed = (
        P("wide", "blk", None),
        P(),
        P("blk", "wide"),
        P("blk", "wide"),
        P("blk", "wide"),
        P("wide", "blk"),
        P("wide"),
        P("wide"),
        P("wide"),
        P(None, "wide"),
        P(None, "wide"),
        P("wide", None),
        P("wide"),
        P("wide", "blk", None),
    )
    return jax.shard_map(
        local,
        mesh=mesh,
        in_specs=placed,
        out_specs=(
            P("wide", "blk", None),
            P("wide", "blk", None),
            P("blk", "wide"),
            P("blk", "wide"),
            P("blk", "wide"),
            P("wide", "blk"),
            P(("blk", "wide")),
            P(("blk", "wide")),
            P(("blk", "wide")),
            P("blk", "wide"),
            P("blk", "wide"),
            P("wide", "blk"),
            P(("blk", "wide")),
        ),
        check_vma=False,
    )
```

time: 3560 us -> 877 us (0.25)
  waiting for transfers between devices: 2790 us -> 3.18 us
  Pallas kernels: 0 us -> 613 us
  matrix products: 440 us -> 157 us
  blocking collectives: 96.6 us -> 8.84 us
  local copies, waits for them, and re-layouts: 80.6 us -> 14.1 us
  other arithmetic: 123 us -> 59.8 us
    all_gather x23 -> x2, waiting for transfers between devices: 1580 us -> 3.03 us  [the longest x1 3.01 us: local(): w_qkv = lax.all_gather(qkv_rows, 'blk', axis=0, tiled=True)]
    reduce_scatter x15 -> x5, waiting for transfers between devices: 1120 us -> 0.03 us  [over_blk(): lax.psum_scatter(value.astype(low), 'blk', scatter_dimension=axis, tiled=...]
    pallas_call x0 -> x16, Pallas kernels: none -> 613 us  [the longest x4 236 us: scatter(): pl.pallas_call(functools.partial(scatter_body, width, slots, flat, len(le...]
    dot_general x21 -> x3, matrix products: 267 us -> 48.7 us  [dot(): return jnp.dot(left, right, preferred_element_type=jnp.float32)]
    unnamed x40 -> x7, waiting for transfers between devices: 86.2 us -> 0.11 us
    all_gather x8 -> x1, blocking collectives: 69.2 us -> 8.84 us  [local(): both = lax.all_gather(both, 'wide', axis=1, tiled=True).astype(f32)]
    unnamed x193 -> x45, local copies, waits for them, and re-layouts: 66.2 us -> 6.31 us
    dot_general x7 -> x2, matrix products: 92.8 us -> 35.7 us  [contract_cols(): lax.dot_general(left, right, (((1,), (1,)), ((), ())), preferred_element_...]
  transfers between devices with their start and end apart: 39 -> 7, of which waited for: 38 -> 1; matrix products, arithmetic and copies ran while one was open for 16% -> 18% of each run, Pallas kernels for 0% -> 40%
where the time goes in v1:
time: 877 us; the launch traced here: 871 us
  Pallas kernels  613 us (70%)
  matrix products  157 us (18%)
  other arithmetic  59.8 us (7%)
  between operations  15.1 us (2%)
  local copies, waits for them, and re-layouts  14.1 us (2%)
  blocking collectives  8.84 us (1%)
    pallas_call x4, Pallas kernels, scatter(): pl.pallas_call(functools.partial(scatter_body, width, slots, flat, len(le...  236 us
    pallas_call x4, Pallas kernels, gather(): pl.pallas_call(functools.partial(gather_body, width, slots, side), out_sh...  204 us
    pallas_call x2, Pallas kernels, turn(): pl.pallas_call(functools.partial(body, planes, slots), out_shape=[shape(m...  93.9 us
    dot_general x5, matrix products, contract_rows(): lax.dot_general(left, right, (((0,), (0,)), ((), ())), preferred_element_...  72.1 us
    dot_general x3, matrix products, dot(): return jnp.dot(left, right, preferred_element_type=jnp.float32)  48.7 us
    dot_general x2, matrix products, contract_cols(): lax.dot_general(left, right, (((1,), (1,)), ((), ())), preferred_element_...  35.7 us
    pallas_call x4, Pallas kernels, total(): pl.pallas_call(functools.partial(total_body, axis, width), out_shape=jax....  34 us
    pallas_call x1, Pallas kernels, attend_back(): pl.pallas_call(functools.partial(attend_back_body, size), grid=(slots, he...  27.3 us
  transfers between devices with their start and end apart: 7, of which 1 were waited for; matrix products, arithmetic and copies ran while one was open for 18% of the time, Pallas kernels for 40%

profile of v1, /device:TPU:8, one launch (start us, length us, event | category | flops | bytes accessed | tf_op | source)
XLA Modules:
  0.0 871.0 jit_solution(10546516782700128554)
XLA Ops:
  7.3 48.1 %turn_in.1 = (bf16[320,2048]{1,0:T(8,128)(2,1)}, bf16[320,2048]{1,0:T(8,128)(2,1)}, bf16[320,2048]{1,0:T(8,128)(2,1)}) custom-call(bf16[320,2048]{1,0:T(8,128)(2,1)} %bitcast.85, bf16[320,2048]{1,0:T(8,128)(2,1)} %bitcast.86), custom_call_target="tpu_custom_call" | custom-call | bytes 157500000 | tf_op jit(solution)/shard_map/turn_in/pallas_call | solution.py:512
  56.4 49.4 %gather_tokens.1 = bf16[2560,2048]{1,0:T(8,128)(2,1)} custom-call(bf16[320,2048]{1,0:T(8,128)(2,1)} %get-tuple-element.42.refs_0_), custom_call_target="tpu_custom_call" | custom-call | bytes 175000000 | tf_op jit(solution)/shard_map/gather_tokens/pallas_call | solution.py:177
  106.9 4.6 fusion.11
  111.6 2.3 pad_maximum_fusion.1
  114.6 3.0 all-gather.3.cloned.1.call-done.refs_1_
  117.9 12.1 %fusion.18 = f32[2560,768]{1,0:T(8,128)S(1)} fusion(bf16[2560,2048]{1,0:T(8,128)(2,1)} %gather_tokens.1, bf16[2048,768]{1,0:T(8,128)(2,1)} %all-gather.3.cloned.1.call-done.refs_1_), kind=kOutput, calls=%fused_computation.83 | convolution fusion | flops 8053063680 | bytes 21495808 | tf_op jit(solution)/shard_map/dot_general | solution.py:51
  129.9 3.2 copy-done.2
  134.5 7.0 total_squares.1
  143.8 17.7 %attend.1 = (bf16[2,1280,256]{2,1,0:T(8,128)(2,1)}, bf16[2,1280,256]{2,1,0:T(8,128)(2,1)}, bf16[2,1280,256]{2,1,0:T(8,128)(2,1)}, bf16[2,1280,256]{2,1,0:T(8,128)(2,1)}, f32[2,2,1,1280]{3,2,1,0:T(1,128)}) custom-call(f32[2,1280,768]{2,1,0:T(8,128)} %bitcast.74, f32[2,1280,768]{2,1,0:T(8,128)} %bitcast.75, f32[2,1280,768]{2,1,0:T(8,128)} %bitcast.76, ...), custom_call_target="tpu_custom_call" | custom-call | bytes 59500000 | tf_op jit(solution)/shard_map/attend/pallas_call | solution.py:595
  161.5 8.8 %all_gather.11 = bf16[2,2048]{1,0:T(2,128)(2,1)S(1)} all-gather(bf16[2,256]{1,0:T(2,128)(2,1)S(1)} %pad_maximum_fusion.6), channel_id=1, replica_groups=mesh['blk'=4,'wide'=8] {'wide'}, dimensions={1}, use_global_device_ids=true | all-gather | bytes 9216 | tf_op jit(solution)/shard_map/all_gather | solution.py:724
  170.4 54.4 %scatter_mixed.1 = f32[320,2048]{1,0:T(8,128)} custom-call(bf16[2560,256]{1,0:T(8,128)(2,1)} %bitcast.81, bf16[256,2048]{1,0:T(8,128)(2,1)} %all-gather.5.cloned.1.call-done.refs_1_), custom_call_target="tpu_custom_call" | custom-call | bytes 210000000 | tf_op jit(solution)/shard_map/scatter_mixed/pallas_call | solution.py:315
  224.9 2.2 multiply_reduce_fusion.3
  227.4 2.9 fusion.10.refs_0_
  230.2 53.9 %gather_hidden.1 = (bf16[2560,2048]{1,0:T(8,128)(2,1)}, bf16[320,2048]{1,0:T(8,128)(2,1)}) custom-call(bf16[320,2048]{1,0:T(8,128)(2,1)} %fusion.10.refs_0_, bf16[320,2048]{1,0:T(8,128)(2,1)} %get-tuple-element.47.refs_1_), custom_call_target="tpu_custom_call" | custom-call | bytes 175000000 | tf_op jit(solution)/shard_map/gather_hidden/pallas_call | solution.py:177
  284.2 16.6 %fusion.19 = f32[2560,1024]{1,0:T(8,128)} fusion(bf16[2560,2048]{1,0:T(8,128)(2,1)} %get-tuple-element.49, bf16[2048,1024]{1,0:T(8,128)(2,1)} %refs_2_.1), kind=kOutput, calls=%fused_computation.84 | convolution fusion | flops 10737418240 | bytes 25165824 | tf_op jit(solution)/shard_map/dot_general | solution.py:51
  300.8 20.0 %multiply_convert_fusion.2 = (bf16[2560,1024]{1,0:T(8,128)(2,1)}, f32[2560,1024]{1,0:T(8,128)}) fusion(f32[2560,1024]{1,0:T(8,128)} %fusion.19, bf16[2560,2048]{1,0:T(8,128)(2,1)} %get-tuple-element.49, bf16[2048,1024]{1,0:T(8,128)(2,1)S(1)} %copy-done.8), kind=kOutput, calls=%fused_computation.2 | convolution fusion | flops 10753146880 | bytes 40894464 | tf_op jit(solution)/shard_map/dot_general | solution.py:51
  320.9 57.5 %scatter_down.1 = f32[320,2048]{1,0:T(8,128)} custom-call(bf16[2560,1024]{1,0:T(8,128)(2,1)} %get-tuple-element.117.refs_0_, bf16[1024,2048]{1,0:T(8,128)(2,1)} %refs_1_.1), custom_call_target="tpu_custom_call" | custom-call | bytes 210000000 | tf_op jit(solution)/shard_map/scatter_down/pallas_call | solution.py:315
  378.4 2.2 multiply_reduce_fusion.2
  380.9 4.5 fusion.5
  385.4 1.7 fusion.4.refs_0_
  387.1 53.5 %gather_grad.1 = (bf16[2560,2048]{1,0:T(8,128)(2,1)}, bf16[320,2048]{1,0:T(8,128)(2,1)}) custom-call(bf16[320,2048]{1,0:T(8,128)(2,1)} %fusion.4.refs_0_, bf16[320,2048]{1,0:T(8,128)(2,1)} %get-tuple-element.82.refs_1_), custom_call_target="tpu_custom_call" | custom-call | bytes 175000000 | tf_op jit(solution)/shard_map/gather_grad/pallas_call | solution.py:177
  440.6 16.8 %convolution_convert_fusion.1 = bf16[1024,2048]{1,0:T(8,128)(2,1)} fusion(bf16[2560,1024]{1,0:T(8,128)(2,1)} %get-tuple-element.117.refs_0_, bf16[2560,2048]{1,0:T(8,128)(2,1)} %get-tuple-element.51), kind=kOutput, calls=%fused_computation.9 | convolution fusion | flops 10739515392 | bytes 19922944 | tf_op jit(solution)/shard_map/dot_general | solution.py:55
  457.4 27.6 %multiply_convert_fusion = (bf16[2560,1024]{1,0:T(8,128)(2,1)}, bf16[2560,1024]{1,0:T(8,128)(2,1)}) fusion(f32[2560,1024]{1,0:T(8,128)} %fusion.19, f32[2560,1024]{1,0:T(8,128)} %get-tuple-element.118, bf16[2560,2048]{1,0:T(8,128)(2,1)} %get-tuple-element.51, bf16[1024,2048]{1,0:T(8,128)(2,1)} %refs_1_.1), kind=kOutput, calls=%fused_computation | convolution fusion | flops 10771496960 | bytes 46137344 | tf_op jit(solution)/shard_map/dot_general | solution.py:61
  485.1 16.8 %convolution_convert_fusion.3 = bf16[2048,1024]{1,0:T(8,128)(2,1)} fusion(bf16[2560,2048]{1,0:T(8,128)(2,1)} %get-tuple-element.49, bf16[2560,1024]{1,0:T(8,128)(2,1)} %get-tuple-element.79.refs_0_), kind=kOutput, calls=%fused_computation.11 | convolution fusion | flops 10739515392 | bytes 19922944 | tf_op jit(solution)/shard_map/dot_general | solution.py:55
  501.9 66.5 %scatter_hidden.1 = f32[320,2048]{1,0:T(8,128)} custom-call(bf16[2560,1024]{1,0:T(8,128)(2,1)} %get-tuple-element.79.refs_0_, bf16[2560,1024]{1,0:T(8,128)(2,1)} %get-tuple-element.56.refs_1_, bf16[2048,1024]{1,0:T(8,128)(2,1)} %refs_2_.1, bf16[2048,1024]{1,0:T(8,128)(2,1)} %refs_3_.1), custom_call_target="tpu_custom_call" | custom-call | bytes 210000000 | tf_op jit(solution)/shard_map/scatter_hidden/pallas_call | solution.py:315
  568.4 4.5 multiply_reduce_fusion
  573.0 17.0 %convolution_convert_fusion.2 = bf16[2048,1024]{1,0:T(8,128)(2,1)} fusion(bf16[2560,2048]{1,0:T(8,128)(2,1)} %get-tuple-element.49, bf16[2560,1024]{1,0:T(8,128)(2,1)} %get-tuple-element.56.refs_1_), kind=kOutput, calls=%fused_computation.10 | convolution fusion | flops 10739515392 | bytes 19922944 | tf_op jit(solution)/shard_map/dot_general | solution.py:55
  590.7 3.4 multiply_convert_fusion.3.refs_0_
  594.2 2.8 convert_element_type.131
  597.0 47.6 %gather_proj.1 = bf16[2560,2048]{1,0:T(8,128)(2,1)} custom-call(bf16[320,2048]{1,0:T(8,128)(2,1)} %multiply_convert_fusion.3.refs_0_), custom_call_target="tpu_custom_call" | custom-call | bytes 175000000 | tf_op jit(solution)/shard_map/gather_proj/pallas_call | solution.py:177
  644.7 2.9 convert_element_type.133
  647.6 8.1 convolution_convert_fusion
  655.6 27.3 %attend_back.1 = (f32[2,1280,256]{2,1,0:T(8,128)}, f32[2,1280,256]{2,1,0:T(8,128)}, bf16[2,1280,256]{2,1,0:T(8,128)(2,1)}, f32[2,2,1280,2]{3,2,1,0:T(8,128)}, f32[2,2,256]{2,1,0:T(2,128)}) custom-call(bf16[2,1280,256]{2,1,0:T(8,128)(2,1)} %get-tuple-element.53.q_ref, bf16[2,1280,256]{2,1,0:T(8,128)(2,1)} %get-tuple-element.54.k_ref, ...), custom_call_target="tpu_custom_call" | custom-call | bytes 98000000 | tf_op jit(solution)/shard_map/attend_back/pallas_call | solution.py:658
  682.9 2.2 reduce_sum.96
  686.2 7.0 total_means.1
  693.9 7.9 convolution_convert_fusion.5
  701.9 5.7 fusion.9
  707.6 2.1 pad_maximum_fusion.refs_0_
  709.7 2.8 convert_element_type.136
  712.5 13.6 %convolution_convert_fusion.4 = bf16[2048,768]{1,0:T(8,128)(2,1)} fusion(bf16[2560,2048]{1,0:T(8,128)(2,1)} %gather_tokens.1, bf16[2560,768]{1,0:T(8,128)(2,1)} %pad_maximum_fusion.refs_0_), kind=kOutput, calls=%fused_computation.12 | convolution fusion | flops 8054636544 | bytes 17563648 | tf_op jit(solution)/shard_map/dot_general | solution.py:55
  727.5 7.9 total_gains.1.x_ref
  735.4 12.2 %total_gains_blk.1 = f32[64,128]{1,0:T(8,128)} custom-call(f32[64,128]{1,0:T(8,128)} %total_gains.1.x_ref), custom_call_target="tpu_custom_call" | custom-call | bytes 24500000 | tf_op jit(solution)/shard_map/total_gains_blk/pallas_call | solution.py:356
  748.4 57.2 %scatter_tokens.1 = f32[320,2048]{1,0:T(8,128)} custom-call(bf16[2560,768]{1,0:T(8,128)(2,1)} %pad_maximum_fusion.refs_0_, bf16[2048,768]{1,0:T(8,128)(2,1)} %all-gather.3.cloned.1.call-done.refs_1_), custom_call_target="tpu_custom_call" | custom-call | bytes 210000000 | tf_op jit(solution)/shard_map/scatter_tokens/pallas_call | solution.py:315
  805.6 3.3 add_convert_fusion.x_ref
  808.9 45.8 %turn_out.1 = (bf16[320,2048]{1,0:T(8,128)(2,1)}, bf16[320,2048]{1,0:T(8,128)(2,1)}, bf16[320,2048]{1,0:T(8,128)(2,1)}) custom-call(bf16[320,2048]{1,0:T(8,128)(2,1)} %add_convert_fusion.x_ref, bf16[320,2048]{1,0:T(8,128)(2,1)} %get-tuple-element.67.far_c), custom_call_target="tpu_custom_call" | custom-call | bytes 157500000 | tf_op jit(solution)/shard_map/turn_out/pallas_call | solution.py:512
  855.4 3.1 bitcast_convert_fusion
  858.5 1.9 convert_element_type.143
  860.4 2.3 fusion.15
  (106 shorter events, 14.0 us)
Async XLA Ops:
  7.2 98.6 %copy-start = (s32[8,3]{0,1:T(4,128)S(1)}, s32[8,3]{0,1:T(4,128)}, u32[]{:S(2)}) copy-start(s32[8,3]{0,1:T(4,128)} %param.15) | copy-start | bytes 292
  7.2 48.2 %copy-start.14 = (bf16[512,256]{1,0:T(8,128)(2,1)S(1)}, bf16[512,256]{1,0:T(8,128)(2,1)}, u32[]{:S(2)}) copy-start(bf16[512,256]{1,0:T(8,128)(2,1)} %param.16) | copy-start | bytes 786436
  7.2 48.2 %copy-start.13 = (bf16[512,256]{1,0:T(8,128)(2,1)S(1)}, bf16[512,256]{1,0:T(8,128)(2,1)}, u32[]{:S(2)}) copy-start(bf16[512,256]{1,0:T(8,128)(2,1)} %param.17) | copy-start | bytes 786436
  7.2 48.2 %copy-start.12 = (bf16[512,256]{1,0:T(8,128)(2,1)S(1)}, bf16[512,256]{1,0:T(8,128)(2,1)}, u32[]{:S(2)}) copy-start(bf16[512,256]{1,0:T(8,128)(2,1)} %param.18) | copy-start | bytes 786436
  7.2 110.4 %all-gather.3.cloned.1.call-start = ((), (), s32[]{:S(2)}) async-start(), calls=%async_computation.5 | async-start | bytes 3932160 | tf_op jit(solution)/shard_map/all_gather | solution.py:720
  56.3 114.1 %all-gather.5.cloned.1.call-start = ((), (), s32[]{:S(2)}) async-start(), calls=%async_computation.6 | async-start | bytes 1310720 | tf_op jit(solution)/shard_map/all_gather | solution.py:721
  56.4 49.8 %copy-start.18 = (bf16[256]{0:T(256)(128)(2,1)S(1)}, bf16[256]{0:T(256)(128)(2,1)}, u32[]{:S(2)}) copy-start(bf16[256]{0:T(256)(128)(2,1)} %param.20) | copy-start | bytes 1540
  56.4 49.8 %copy-start.19 = (bf16[256]{0:T(256)(128)(2,1)S(1)}, bf16[256]{0:T(256)(128)(2,1)}, u32[]{:S(2)}) copy-start(bf16[256]{0:T(256)(128)(2,1)} %param.21) | copy-start | bytes 1540
  56.4 49.8 %copy-start.20 = (bf16[256]{0:T(256)(128)(2,1)S(1)}, bf16[256]{0:T(256)(128)(2,1)}, u32[]{:S(2)}) copy-start(bf16[256]{0:T(256)(128)(2,1)} %param.22) | copy-start | bytes 1540
  56.4 49.8 %copy-start.21 = (bf16[256]{0:T(256)(128)(2,1)S(1)}, bf16[256]{0:T(256)(128)(2,1)}, u32[]{:S(2)}) copy-start(bf16[256]{0:T(256)(128)(2,1)} %param.26) | copy-start | bytes 1540
  117.6 476.5 %reduce-scatter.6.cloned.1.call-start = ((), (), s32[]{:S(2)}) async-start(), calls=%async_computation.7 | async-start | bytes 5242880 | tf_op jit(solution)/shard_map/reduce_scatter | solution.py:712
  129.9 3.2 copy-start.2
  142.3 19.3 %copy-start.15 = (f32[40,128]{1,0:T(8,128)}, f32[40,128]{1,0:T(8,128)S(1)}, u32[]{:S(2)}) copy-start(f32[40,128]{1,0:T(8,128)S(1)} %add_rsqrt_fusion) | copy-start | bytes 61444
  224.9 2.5 copy-start.3
  284.2 16.6 %copy-start.8 = (bf16[2048,1024]{1,0:T(8,128)(2,1)S(1)}, bf16[2048,1024]{1,0:T(8,128)(2,1)}, u32[]{:S(2)}) copy-start(bf16[2048,1024]{1,0:T(8,128)(2,1)} %refs_3_.1) | copy-start | bytes 12582916
  378.4 2.5 copy-start.4
  380.9 4.5 copy-start.6
  457.4 187.3 %reduce-scatter.8.cloned.1.call-start = ((), (), s32[]{:S(2)}) async-start(), calls=%async_computation.8 | async-start | bytes 5242880 | tf_op jit(solution)/shard_map/reduce_scatter | solution.py:712
  501.9 207.8 %reduce-scatter.10.cloned.1.call-start = ((), (), s32[]{:S(2)}) async-start(), calls=%async_computation.9 | async-start | bytes 5242880 | tf_op jit(solution)/shard_map/reduce_scatter | solution.py:712
  590.0 0.7 copy-start.16
  590.0 268.5 %reduce-scatter.14.cloned.1.call-start = ((), (), s32[]{:S(2)}) async-start(), calls=%async_computation.11 | async-start | bytes 1310720 | tf_op jit(solution)/shard_map/reduce_scatter | solution.py:712
  644.6 2.9 copy-start.11
  682.9 11.0 %copy-start.7 = (bf16[2,1280,256]{2,1,0:T(8,128)(2,1)S(1)}, bf16[2,1280,256]{2,1,0:T(8,128)(2,1)}, u32[]{:S(2)}) copy-start(bf16[2,1280,256]{2,1,0:T(8,128)(2,1)} %get-tuple-element.44) | copy-start | bytes 3932164
  701.8 158.6 %reduce-scatter.12.cloned.1.call-start = ((), (), s32[]{:S(2)}) async-start(), calls=%async_computation.10 | async-start | bytes 3932160 | tf_op jit(solution)/shard_map/reduce_scatter | solution.py:712
  701.9 5.7 copy-start.10
  726.1 0.7 copy-start.17
  748.4 57.2 %copy-start.5 = (f32[320,2048]{1,0:T(8,128)S(1)}, f32[320,2048]{1,0:T(8,128)}, u32[]{:S(2)}) copy-start(f32[320,2048]{1,0:T(8,128)} %get-tuple-element.77) | copy-start | bytes 7864324
  858.5 4.2 copy-start.9
  858.5 5.3 copy-start.1
Sparse Core Ops, SparseCore 0:
  56.5 61.0 all-gather.2
  119.1 28.8 all-gather.4
  457.5 75.8 reduce-scatter.5
  535.6 77.2 reduce-scatter.7
  615.1 77.2 reduce-scatter.9
  701.9 24.0 reduce-scatter.13
  728.4 63.2 reduce-scatter.11

commit v2 on v1

--- a/solution.py
+++ b/solution.py
@@ -77,6 +77,123 @@
     for k in others:
         pl.semaphore_signal(barrier, inc=1, device_id={axis: flip(me, k)}, device_id_type=MESH)
     pl.semaphore_wait(barrier, len(others))
+
+
+class Flow:
+    def __init__(self, me, source, spot, half, send, recv):
+        self.me, self.source, self.spot, self.half = me, source, spot, half
+        self.send, self.recv, self.moves = send, recv, []
+
+    def go(self, origin, target, k, part):
+        if origin is None:
+            source = self.source.at[pl.ds(part * self.half, self.half)]
+        else:
+            source = self.spot(flip(self.me, origin), part)
+        copy = pltpu.make_async_remote_copy(
+            src_ref=source,
+            dst_ref=self.spot(flip(flip(self.me, target), k), part),
+            send_sem=self.send.at[k, part],
+            recv_sem=self.recv.at[k, part],
+            device_id={"wide": flip(self.me, target)},
+            device_id_type=MESH,
+        )
+        copy.start()
+        self.moves.append(copy)
+
+    def arrived(self, k, part):
+        block = self.spot(flip(self.me, k), part)
+        pltpu.make_async_copy(block, block, self.recv.at[k, part]).wait()
+
+    def finish(self):
+        for copy in self.moves:
+            copy.wait_send()
+
+
+class Sums:
+    def __init__(self, width, me, out_ref, refs):
+        self.width, self.me, self.out = width, me, out_ref
+        (self.odd, self.even, self.from_twin, self.from_far, self.passing, self.sends, self.recvs,
+         self.pass_send, self.pass_recv, self.twin_send, self.twin_recv) = refs
+        self.half = out_ref.shape[0] // 2
+
+    def rows(self, part):
+        return pl.ds(part * self.half, self.half)
+
+    def copy(self, src, dst, send, recv, k):
+        return pltpu.make_async_remote_copy(
+            src_ref=src, dst_ref=dst, send_sem=send, recv_sem=recv,
+            device_id={"wide": flip(self.me, k)}, device_id_type=MESH,
+        )
+
+    def twin(self, k, part):
+        i, at = k // 2, self.rows(part)
+        return self.copy(
+            self.odd.at[i, at], self.from_twin.at[i, at], self.twin_send.at[i, part],
+            self.twin_recv.at[i, part], 1,
+        )
+
+    def far(self, k, part):
+        i, at = k // 2 - 1, self.rows(part)
+        return self.copy(
+            self.even.at[i, at], self.from_far.at[i, at], self.sends.at[i, part], self.recvs.at[i, part], k
+        )
+
+    def relay(self, part):
+        return self.copy(
+            self.even.at[2, self.rows(part)], self.passing.at[part], self.pass_send.at[part],
+            self.pass_recv.at[part], 2 if part == 0 else 4,
+        )
+
+    def give(self, k):
+        self.twin(k, 0).start()
+        self.twin(k, 1).start()
+
+    def got(self, k):
+        self.twin(k, 0).wait_recv()
+        self.twin(k, 1).wait_recv()
+
+    def pass_on(self, k, part):
+        self.relay(part).wait_recv()
+        at = self.rows(part)
+        self.even[k // 2 - 1, at, :] = (
+            self.even[k // 2 - 1, at, :].astype(jnp.float32) + self.passing[part].astype(jnp.float32)
+        ).astype(jnp.bfloat16)
+        self.far(k, part).start()
+
+    def finish(self):
+        sources = [2, 4] if self.width == 8 else list(range(2, self.width, 2))
+        for k in sources:
+            for part in (0, 1):
+                self.far(k, part).wait_recv()
+        extra = self.from_far[sources[0] // 2 - 1].astype(jnp.float32)
+        for k in sources[1:]:
+            extra = extra + self.from_far[k // 2 - 1].astype(jnp.float32)
+        self.out[...] = self.out[...] + extra
+        for part in (0, 1):
+            for k in sources:
+                self.far(k, part).wait_send()
+            for k in range(0, self.width, 2):
+                self.twin(k, part).wait_send()
+            if self.width == 8:
+                self.relay(part).wait_send()
+
+
+def sum_scratch(width, rows, cols):
+    chips, dma = width // 2, pltpu.SemaphoreType.DMA
+    block = lambda n: pltpu.VMEM((n, rows, cols), jnp.bfloat16)
+    return [
+        block(chips), block(chips - 1), block(chips), block(2 if width == 8 else chips - 1),
+        pltpu.VMEM((2, rows // 2, cols), jnp.bfloat16),
+        dma((chips - 1, 2)), dma((chips - 1, 2)), dma((2,)), dma((2,)), dma((chips, 2)), dma((chips, 2)),
+    ]
+
+
+def wide_peers(width, me):
+    return [{"wide": flip(me, k)} for k in [1] + list(range(2, width, 2))]
+
+
+def local_copies(pairs, sem):
+    return [pltpu.make_async_copy(src, dst, sem.at[i]) for i, (src, dst) in enumerate(pairs)]
 
 
 def gather_body(width, slots, side, *refs):
@@ -180,7 +297,7 @@
         in_specs=[pl.BlockSpec(memory_space=pl.ANY)] * len(inputs),
         out_specs=[pl.BlockSpec(memory_space=pl.ANY)] * len(shapes),
         scratch_shapes=scratch,
-        cost_estimate=busy(50),
+        cost_estimate=busy(10),
         compiler_params=pltpu.CompilerParams(collective_id=ident, has_side_effects=True, vmem_limit_bytes=VMEM_LIMIT),
         name=name,
     )(*inputs)
@@ -189,12 +306,11 @@
 
 def scatter_body(width, slots, flat, count, step, *refs):
     lefts, rights = refs[:count], refs[count : 2 * count]
-    out_ref, odd, even, from_twin, from_far, passing, sends, recvs, pass_send, pass_recv, twin_send, twin_recv = refs[2 * count :]
+    out_ref = refs[2 * count]
     me = lax.axis_index("wide")
     rows, cols = out_ref.shape
-    half = rows // 2
-    evens = list(range(2, width, 2))
-    greet("wide", me, [1] + evens)
+    hello(wide_peers(width, me))
+    sums = Sums(width, me, out_ref, refs[2 * count + 1 :])
     dims = (((1,), (1 if flat else 0,)), ((), ()))
 
     def produce(k, put, adds=()):
@@ -217,112 +333,50 @@
 
         lax.fori_loop(0, cols // step, tile, 0)
 
-    def twin(k):
-        return pltpu.make_async_remote_copy(
-            src_ref=odd.at[k // 2],
-            dst_ref=from_twin.at[k // 2],
-            send_sem=twin_send.at[k // 2],
-            recv_sem=twin_recv.at[k // 2],
-            device_id={"wide": flip(me, 1)},
-            device_id_type=MESH,
-        )
-
-    def far(k, part):
-        at = pl.ds(part * half, half)
-        return pltpu.make_async_remote_copy(
-            src_ref=even.at[k // 2 - 1, at],
-            dst_ref=from_far.at[k // 2 - 1, at],
-            send_sem=sends.at[k // 2 - 1, part],
-            recv_sem=recvs.at[k // 2 - 1, part],
-            device_id={"wide": flip(me, k)},
-            device_id_type=MESH,
-        )
-
-    def relay(part):
-        at = pl.ds(part * half, half)
-        return pltpu.make_async_remote_copy(
-            src_ref=even.at[2, at],
-            dst_ref=passing.at[part],
-            send_sem=pass_send.at[part],
-            recv_sem=pass_recv.at[part],
-            device_id={"wide": flip(me, 2 if part == 0 else 4)},
-            device_id_type=MESH,
-        )
-
-    def to_twin(k):
-        produce(k + 1, odd.at[k // 2])
-        twin(k).start()
+    def give(k):
+        produce(k + 1, sums.odd.at[k // 2])
+        sums.give(k)
 
     def merge(k):
-        twin(k).wait_recv()
-        produce(k, even.at[k // 2 - 1], (from_twin.at[k // 2],))
-
-    def pass_on(k, part):
-        relay(part).wait_recv()
-        at = pl.ds(part * half, half)
-        even[k // 2 - 1, at, :] = (
-            even[k // 2 - 1, at, :].astype(jnp.float32) + passing[part].astype(jnp.float32)
-        ).astype(jnp.bfloat16)
-        far(k, part).start()
+        sums.got(k)
+        produce(k, sums.even.at[k // 2 - 1], (sums.from_twin.at[k // 2],))
 
     if width == 8:
-        to_twin(6)
-        to_twin(2)
-        to_twin(4)
+        give(6)
+        give(2)
+        give(4)
         merge(6)
-        relay(0).start()
-        relay(1).start()
+        sums.relay(0).start()
+        sums.relay(1).start()
         merge(2)
-        far(2, 0).start()
+        sums.far(2, 0).start()
         merge(4)
-        far(4, 1).start()
-        to_twin(0)
-        pass_on(2, 1)
-        pass_on(4, 0)
-        sources = [2, 4]
+        sums.far(4, 1).start()
+        give(0)
+        sums.pass_on(2, 1)
+        sums.pass_on(4, 0)
     else:
-        for k in evens:
-            to_twin(k)
-        to_twin(0)
-        for k in evens:
+        for k in range(0, width, 2):
+            give(k)
+        for k in range(2, width, 2):
             merge(k)
-            far(k, 0).start()
-            far(k, 1).start()
-        sources = evens
-    twin(0).wait_recv()
-    produce(0, out_ref, (from_twin.at[0],))
-    for k in sources:
-        far(k, 0).wait_recv()
-        far(k, 1).wait_recv()
-        out_ref[...] = out_ref[...] + from_far[k // 2 - 1].astype(jnp.float32)
-    for k in sources:
-        far(k, 0).wait_send()
-        far(k, 1).wait_send()
-    for k in range(0, width, 2):
-        twin(k).wait_send()
-    if width == 8:
-        relay(0).wait_send()
-        relay(1).wait_send()
+            sums.far(k, 0).start()
+            sums.far(k, 1).start()
+    sums.got(0)
+    produce(0, out_ref, (sums.from_twin.at[0],))
+    sums.finish()
 
 
 def scatter(lefts, rights, width, slots, flat, ident, name, step=1024):
     rows = lefts[0].shape[0] // width
     cols = rights[0].shape[0 if flat else 1]
-    chips = width // 2
-    low = jnp.bfloat16
-    block = lambda n: pltpu.VMEM((n, rows, cols), low)
-    dma = pltpu.SemaphoreType.DMA
     return pl.pallas_call(
         functools.partial(scatter_body, width, slots, flat, len(lefts), step),
         out_shape=jax.ShapeDtypeStruct((rows, cols), jnp.float32),
         in_specs=[pl.BlockSpec(memory_space=pltpu.VMEM)] * (2 * len(lefts)),
         out_specs=pl.BlockSpec(memory_space=pltpu.VMEM),
-        scratch_shapes=[
-            block(chips), block(chips - 1), block(chips), block(chips - 1),
-            pltpu.VMEM((2, rows // 2, cols), low),
-            dma((chips - 1, 2)), dma((chips - 1, 2)), dma((2,)), dma((2,)), dma((chips,)), dma((chips,)),
-        ],
-        cost_estimate=busy(60),
+        scratch_shapes=sum_scratch(width, rows, cols),
+        cost_estimate=busy(10),
         compiler_params=pltpu.CompilerParams(collective_id=ident, has_side_effects=True, vmem_limit_bytes=VMEM_LIMIT),
         name=name,
     )(*lefts, *rights)
@@ -515,7 +569,7 @@
         in_specs=[pl.BlockSpec(memory_space=pl.ANY)] * len(inputs),
         out_specs=[pl.BlockSpec(memory_space=pl.ANY)] * len(outputs),
         scratch_shapes=[pltpu.SemaphoreType.DMA((planes,))] * 6,
-        cost_estimate=busy(45),
+        cost_estimate=busy(10),
         compiler_params=pltpu.CompilerParams(collective_id=ident, has_side_effects=True, vmem_limit_bytes=VMEM_LIMIT),
         name=name,
     )(*inputs)
@@ -602,7 +656,7 @@
         ],
         out_specs=[head(0)] * 4 + [pl.BlockSpec((None, None, 1, span), lambda g, h: (g, h, 0, 0))],
         compiler_params=pltpu.CompilerParams(vmem_limit_bytes=VMEM_LIMIT),
-        cost_estimate=busy(17),
+        cost_estimate=busy(5),
         name="attend",
     )(pre, pre, pre, inverse, gains, cosine, sine, begin)
 
@@ -676,9 +730,507 @@
         ],
         scratch_shapes=[pltpu.VMEM((span, HD), f32)] * 4 + [pltpu.VMEM((span, HD), low)],
         compiler_params=pltpu.CompilerParams(vmem_limit_bytes=VMEM_LIMIT),
-        cost_estimate=busy(28),
+        cost_estimate=busy(5),
         name="attend_back",
     )(queries, keys, values, grads, logs, pre, pre, inverse, gains, cosine, sine, begin)
+
+
+def feed_body(width, slots, step, h_ref, c_ref, wg_hbm, wu_hbm, wd_hbm, out_ref, all_ref, act_ref, one_ref,
+              two_ref, c_out, buf, wg, wu, wd, stage, here, load, send, recv, side_send, side_recv, store,
+              keep, *sum_refs):
+    me = lax.axis_index("wide")
+    planes = width // slots
+    rows, cols = h_ref.shape
+    hidden = wg.shape[1]
+    half = rows // 2
+    low = jnp.bfloat16
+    loads = local_copies([(wg_hbm, wg), (wu_hbm, wu), (wd_hbm, wd)], load)
+    mine = pltpu.make_async_copy(h_ref, buf.at[me], here)
+    mine.start()
+    for copy in loads:
+        copy.start()
+    hops = Hops(planes, slots, rows)
+    hello(wide_peers(width, me) + [{"blk": (hops.plane + k) % planes} for k in range(1, planes)])
+    flow = Flow(me, h_ref, lambda who, part: buf.at[who, pl.ds(part * half, half)], half, send, recv)
+    sums = Sums(width, me, out_ref, sum_refs)
+    outs = (act_ref, one_ref, two_ref)
+    pending = [[], []]
+    turn_count = [0]
+    kept = []
+
+    def where(k):
+        who = flip(me, k)
+        return pl.multiple_of(((who % slots) * planes + who // slots) * rows, rows)
+
+    def keep_block(k):
+        copy = pltpu.make_async_copy(buf.at[flip(me, k)], all_ref.at[pl.ds(where(k), rows)], keep.at[k])
+        copy.start()
+        kept.append(copy)
+
+    def work(k, part, put, adds=()):
+        first, count = (0, rows) if part is None else (part * half, half)
+        slot = turn_count[0] % 2
+        turn_count[0] += 1
+        for copy in pending[slot]:
+            copy.wait()
+        block = buf.at[flip(me, k), pl.ds(first, count)]
+        act, one, two = (stage.at[slot, i, pl.ds(0, count)] for i in range(3))
+
+        def inner(n, carry):
+            at = pl.ds(pl.multiple_of(n * step, step), step)
+            gate = jnp.dot(block[...], wg[:, at], preferred_element_type=jnp.float32)
+            upward = jnp.dot(block[...], wu[:, at], preferred_element_type=jnp.float32)
+            sigmoid = jax.nn.sigmoid(gate)
+            silu = gate * sigmoid
+            act[:, at] = (silu * upward).astype(low)
+            one[:, at] = silu.astype(low)
+            two[:, at] = (upward * (sigmoid + silu * (1.0 - sigmoid))).astype(low)
+            return carry
+
+        lax.fori_loop(0, hidden // step, inner, 0)
+        target = pl.ds(pl.multiple_of(where(k) + first, half), count)
+        pending[slot] = []
+        for i, ref in enumerate(outs):
+            copy = pltpu.make_async_copy(stage.at[slot, i, pl.ds(0, count)], ref.at[target], store.at[slot, i])
+            copy.start()
+            pending[slot].append(copy)
+        broad = 2 * step
+
+        def outer(n, carry):
+            at = pl.ds(pl.multiple_of(n * broad, broad), broad)
+            total = jnp.dot(act[...], wd[:, at], preferred_element_type=jnp.float32)
+            for ref in adds:
+                total = total + ref[:, at].astype(jnp.float32)
+            put[:, at] = total.astype(put.dtype)
+            return carry
+
+        lax.fori_loop(0, cols // broad, outer, 0)
+
+    def odd_work(k, part):
+        if part is None:
+            work(k + 1, None, sums.odd.at[k // 2])
+            sums.give(k)
+        else:
+            work(k + 1, part, sums.odd.at[k // 2, sums.rows(part)])
+            sums.twin(k, part).start()
+
+    def even_work(k, part):
+        i = k // 2
+        if part is None:
+            sums.got(k)
+            work(k, None, sums.even.at[i - 1], (sums.from_twin.at[i],))
+        else:
+            sums.twin(k, part).wait_recv()
+            at = sums.rows(part)
+            work(k, part, sums.even.at[i - 1, at], (sums.from_twin.at[i, at],))
+
+    if width == 8:
+        flow.go(None, 2, 2, 0)
+        flow.go(None, 4, 4, 1)
+        flow.go(None, 1, 1, 0)
+        flow.go(None, 1, 1, 1)
+        hops.join(c_ref, c_out, side_send, side_recv, True, True)
+        mine.wait()
+        for copy in loads:
+            copy.wait()
+        work(0, None, out_ref)
+        keep_block(0)
+        flow.arrived(1, 0)
+        flow.arrived(1, 1)
+        keep_block(1)
+        odd_work(0, None)
+        flow.arrived(2, 0)
+        flow.go(2, 4, 6, 0)
+        flow.arrived(4, 1)
+        flow.go(4, 2, 6, 1)
+        flow.go(2, 1, 3, 0)
+        flow.go(4, 1, 5, 1)
+        flow.go(None, 2, 2, 1)
+        flow.go(None, 4, 4, 0)
+        flow.arrived(3, 0)
+        odd_work(2, 0)
+        flow.arrived(5, 1)
+        odd_work(4, 1)
+        even_work(2, 0)
+        even_work(4, 1)
+        for part in (0, 1):
+            flow.arrived(6, part)
+            flow.go(6, 1, 7, part)
+        for part in (0, 1):
+            flow.arrived(7, part)
+        keep_block(6)
+        keep_block(7)
+        odd_work(6, None)
+        even_work(6, None)
+        sums.relay(0).start()
+        sums.relay(1).start()
+        flow.arrived(2, 1)
+        flow.go(2, 1, 3, 1)
+        flow.arrived(4, 0)
+        flow.go(4, 1, 5, 0)
+        sums.far(2, 0).start()
+        sums.far(4, 1).start()
+        flow.arrived(3, 1)
+        odd_work(2, 1)
+        flow.arrived(5, 0)
+        odd_work(4, 0)
+        for k in (2, 3, 4, 5):
+            keep_block(k)
+        even_work(2, 1)
+        sums.pass_on(2, 1)
+        even_work(4, 0)
+        sums.pass_on(4, 0)
+    else:
+        hops.join(c_ref, c_out, side_send, side_recv, True, True)
+        for k in range(2, width, 2):
+            flow.go(None, k, k, 0)
+            flow.go(None, k, k, 1)
+        flow.go(None, 1, 1, 0)
+        flow.go(None, 1, 1, 1)
+        mine.wait()
+        for copy in loads:
+            copy.wait()
+        work(0, None, out_ref)
+        keep_block(0)
+        flow.arrived(1, 0)
+        flow.arrived(1, 1)
+        keep_block(1)
+        odd_work(0, None)
+        for k in range(2, width, 2):
+            for part in (0, 1):
+                flow.arrived(k, part)
+                flow.go(k, 1, k + 1, part)
+            for part in (0, 1):
+                flow.arrived(k + 1, part)
+            keep_block(k)
+            keep_block(k + 1)
+            odd_work(k, None)
+            even_work(k, None)
+            sums.far(k, 0).start()
+            sums.far(k, 1).start()
+    sums.got(0)
+    out_ref[...] = out_ref[...] + sums.from_twin[0].astype(jnp.float32)
+    sums.finish()
+    flow.finish()
+    for copy in kept + pending[0] + pending[1]:
+        copy.wait()
+    hops.join(c_ref, c_out, side_send, side_recv, True, False)
+
+
+def feed(h, side_x, gate_weight, up_weight, down_weight, width, slots, ident, name):
+    rows, cols = h.shape
+    hidden = gate_weight.shape[1]
+    low, dma = h.dtype, pltpu.SemaphoreType.DMA
+    step = min(512, hidden)
+    anywhere = pl.BlockSpec(memory_space=pl.ANY)
+    saved = jax.ShapeDtypeStruct((rows * width, hidden), low)
+    return pl.pallas_call(
+        functools.partial(feed_body, width, slots, step),
+        out_shape=[
+            jax.ShapeDtypeStruct((rows, cols), jnp.float32), jax.ShapeDtypeStruct((rows * width, cols), low),
+            saved, saved, saved, jax.ShapeDtypeStruct((rows, cols), low),
+        ],
+        in_specs=[anywhere] * 5,
+        out_specs=[pl.BlockSpec(memory_space=pltpu.VMEM)] + [anywhere] * 5,
+        scratch_shapes=[
+            pltpu.VMEM((width, rows, cols), low), pltpu.VMEM((cols, hidden), low), pltpu.VMEM((cols, hidden), low),
+            pltpu.VMEM((hidden, cols), low), pltpu.VMEM((2, 3, rows, hidden), low),
+            dma, dma((3,)), dma((width, 2)), dma((width, 2)), dma((width // slots,)), dma((width // slots,)),
+            dma((2, 3)), dma((width,)),
+        ] + sum_scratch(width, rows, cols),
+        cost_estimate=busy(90),
+        compiler_params=pltpu.CompilerParams(collective_id=ident, has_side_effects=True, vmem_limit_bytes=VMEM_LIMIT),
+        name=name,
+    )(h, side_x, gate_weight, up_weight, down_weight)
+
+
+def push_body(width, slots, step, g_ref, c_ref, wd_hbm, act_hbm, one_hbm, two_hbm, down_ref, gg_ref, gu_ref, c_out,
+              buf, wd, held, ins, outs, here, load, send, recv, side_send, side_recv, fetch, store):
+    me = lax.axis_index("wide")
+    planes = width // slots
+    rows, cols = g_ref.shape
+    hidden = wd.shape[0]
+    half = rows // 2
+    low = jnp.bfloat16
+    weights = pltpu.make_async_copy(wd_hbm, wd, load)
+    mine = pltpu.make_async_copy(g_ref, buf.at[me // 2, me % 2], here)
+    mine.start()
+    weights.start()
+    sources = (act_hbm, one_hbm, two_hbm)
+
+    def where(pair, side):
+        who = flip(me // 2, pair) * 2 + side
+        return pl.ds(pl.multiple_of(((who % slots) * planes + who // slots) * rows, rows), rows)
+
+    def fetches(pair):
+        return [
+            pltpu.make_async_copy(ref.at[where(pair, side)], ins.at[pair % 2, i, side], fetch.at[pair % 2, i, side])
+            for i, ref in enumerate(sources)
+            for side in (0, 1)
+        ]
+
+    def stores(pair):
+        return [
+            pltpu.make_async_copy(outs.at[pair % 2, i, side], ref.at[where(pair, side)], store.at[pair % 2, i, side])
+            for i, ref in enumerate((gg_ref, gu_ref))
+            for side in (0, 1)
+        ]
+
+    for copy in fetches(0):
+        copy.start()
+    hops = Hops(planes, slots, rows)
+    hello(wide_peers(width, me) + [{"blk": (hops.plane + k) % planes} for k in range(1, planes)])
+    flow = Flow(me, g_ref, lambda who, part: buf.at[who // 2, who % 2, pl.ds(part * half, half)], half, send, recv)
+    pairs = width // 2
+
+    def work(pair):
+        for copy in fetches(pair):
+            copy.wait()
+        if pair + 1 < pairs:
+            for copy in fetches(pair + 1):
+                copy.start()
+        if pair >= 2:
+            for copy in stores(pair - 2):
+                copy.wait()
+        chip = flip(me // 2, pair)
+        slot = pair % 2
+        grads = buf[chip].reshape(2 * rows, cols)
+
+        def inner(n, carry):
+            at = pl.ds(pl.multiple_of(n * step, step), step)
+            grad = lax.dot_general(
+                grads, wd[at, :], (((1,), (1,)), ((), ())), preferred_element_type=jnp.float32
+            ).reshape(2, rows, step)
+            outs[slot, 0, :, :, at] = (grad * ins[slot, 2, :, :, at].astype(jnp.float32)).astype(low)
+            outs[slot, 1, :, :, at] = (grad * ins[slot, 1, :, :, at].astype(jnp.float32)).astype(low)
+            return carry
+
+        lax.fori_loop(0, hidden // step, inner, 0)
+        for copy in stores(pair):
+            copy.start()
+        tall = min(256, hidden)
+
+        def outer(n, carry):
+            at = pl.ds(pl.multiple_of(n * tall, tall), tall)
+            act = ins[slot, 0, :, :, at].reshape(2 * rows, tall)
+            term = lax.dot_general(act, grads, (((0,), (0,)), ((), ())), preferred_element_type=jnp.float32)
+            if pair:
+                term = term + held[at, :]
+            if pair + 1 < pairs:
+                held[at, :] = term
+            else:
+                down_ref[at, :] = term.astype(low)
+            return carry
+
+        lax.fori_loop(0, hidden // tall, outer, 0)
+
+    def pair_ready(k):
+        for part in (0, 1):
+            flow.arrived(k + 1, part)
+
+    if width == 8:
+        flow.go(None, 2, 2, 0)
+        flow.go(None, 4, 4, 1)
+        flow.go(None, 2, 2, 1)
+        flow.go(None, 4, 4, 0)
+    else:
+        for k in range(2, width, 2):
+            flow.go(None, k, k, 0)
+            flow.go(None, k, k, 1)
+    flow.go(None, 1, 1, 0)
+    flow.go(None, 1, 1, 1)
+    hops.spread(c_ref, c_out, side_send, side_recv, True, True)
+    mine.wait()
+    weights.wait()
+    pair_ready(0)
+    work(0)
+    if width == 8:
+        flow.arrived(2, 0)
+        flow.go(2, 4, 6, 0)
+        flow.go(2, 1, 3, 0)
+        flow.arrived(4, 1)
+        flow.go(4, 2, 6, 1)
+        flow.go(4, 1, 5, 1)
+        flow.arrived(2, 1)
+        flow.go(2, 1, 3, 1)
+        flow.arrived(4, 0)
+        flow.go(4, 1, 5, 0)
+        pair_ready(2)
+        work(1)
+        pair_ready(4)
+        work(2)
+        for part in (0, 1):
+            flow.arrived(6, part)
+            flow.go(6, 1, 7, part)
+        pair_ready(6)
+        work(3)
+    else:
+        for k in range(2, width, 2):
+            for part in (0, 1):
+                flow.arrived(k, part)
+                flow.go(k, 1, k + 1, part)
+            pair_ready(k)
+            work(k // 2)
+    flow.finish()
+    for pair in (pairs - 2, pairs - 1):
+        for copy in stores(pair):
+            copy.wait()
+    hops.spread(c_ref, c_out, side_send, side_recv, True, False)
+
+
+def push(g, side_x, down_weight, act, one, two, width, slots, ident, name):
+    rows, cols = g.shape
+    hidden = down_weight.shape[0]
+    low, dma = g.dtype, pltpu.SemaphoreType.DMA
+    step = min(512, hidden)
+    planes = width // slots
+    anywhere = pl.BlockSpec(memory_space=pl.ANY)
+    saved = jax.ShapeDtypeStruct((rows * width, hidden), low)
+    return pl.pallas_call(
+        functools.partial(push_body, width, slots, step),
+        out_shape=[
+            jax.ShapeDtypeStruct((hidden, cols), low), saved, saved,
+            jax.ShapeDtypeStruct((many_rows(planes, rows), cols), low),
+        ],
+        in_specs=[anywhere] * 6,
+        out_specs=[pl.BlockSpec(memory_space=pltpu.VMEM)] + [anywhere] * 3,
+        scratch_shapes=[
+            pltpu.VMEM((width // 2, 2, rows, cols), low), pltpu.VMEM((hidden, cols), low),
+            pltpu.VMEM((hidden, cols), jnp.float32), pltpu.VMEM((2, 3, 2, rows, hidden), low),
+            pltpu.VMEM((2, 2, 2, rows, hidden), low),
+            dma, dma, dma((width, 2)), dma((width, 2)), dma((planes,)), dma((planes,)),
+            dma((2, 3, 2)), dma((2, 2, 2)),
+        ],
+        cost_estimate=busy(10),
+        compiler_params=pltpu.CompilerParams(collective_id=ident, has_side_effects=True, vmem_limit_bytes=VMEM_LIMIT),
+        name=name,
+    )(g, side_x, down_weight, act, one, two)
+
+
+def pull_body(width, slots, step, chunk, gg_hbm, gu_hbm, wg_hbm, wu_hbm, h_hbm, out_ref, dw_hbm, gg, gu, wg, wu,
+              columns, tiles, load, fetch, store, *sum_refs):
+    me = lax.axis_index("wide")
+    planes = width // slots
+    rows, cols = out_ref.shape
+    hidden = wg.shape[1]
+    loads = local_copies([(wg_hbm, wg), (wu_hbm, wu), (gg_hbm, gg), (gu_hbm, gu)], load)
+    for copy in loads:
+        copy.start()
+    chunks = cols // chunk
+
+    def fetched(n):
+        at = pl.ds(pl.multiple_of(n * chunk, chunk), chunk)
+        return pltpu.make_async_copy(h_hbm.at[:, at], columns.at[n % 2], fetch.at[n % 2])
+
+    def stored(n):
+        at = pl.ds(pl.multiple_of(n * chunk, chunk), chunk)
+        return pltpu.make_async_copy(tiles.at[n % 2], dw_hbm.at[at], store.at[n % 2])
+
+    fetched(0).start()
+    hello(wide_peers(width, me))
+    sums = Sums(width, me, out_ref, sum_refs)
+
+    def produce(k, put, adds=()):
+        who = flip(me, k)
+        at_rows = pl.ds(pl.multiple_of(((who % slots) * planes + who // slots) * rows, rows), rows)
+
+        def tile(n, carry):
+            at = pl.ds(pl.multiple_of(n * step, step), step)
+            total = nt(gg[at_rows, :], wg[at, :]) + nt(gu[at_rows, :], wu[at, :])
+            for ref in adds:
+                total = total + ref[:, at].astype(jnp.float32)
+            put[:, at] = total.astype(put.dtype)
+            return carry
+
+        lax.fori_loop(0, cols // step, tile, 0)
+
+    def grads(first, last):
+        def one_chunk(n, carry):
+            fetched(n).wait()
+
+            @pl.when(n + 1 < chunks)
+            def _():
+                fetched(n + 1).start()
+
+            @pl.when(n >= 2)
+            def _():
+                stored(n - 2).wait()
+
+            for i, ref in enumerate((gg, gu)):
+                tiles[n % 2, :, pl.ds(i * hidden, hidden)] = lax.dot_general(
+                    columns[n % 2], ref[...], (((0,), (0,)), ((), ())), preferred_element_type=jnp.float32
+                ).astype(jnp.bfloat16)
+            stored(n).start()
+            return carry
+
+        lax.fori_loop(first, last, one_chunk, 0)
+
+    def give(k):
+        produce(k + 1, sums.odd.at[k // 2])
+        sums.give(k)
+
+    def merge(k):
+        sums.got(k)
+        produce(k, sums.even.at[k // 2 - 1], (sums.from_twin.at[k // 2],))
+
+    for copy in loads:
+        copy.wait()
+    if width == 8:
+        give(6)
+        give(2)
+        give(4)
+        merge(6)
+        sums.relay(0).start()
+        sums.relay(1).start()
+        merge(2)
+        sums.far(2, 0).start()
+        merge(4)
+        sums.far(4, 1).start()
+        give(0)
+        middle = (3 * chunks) // 8
+        grads(0, middle)
+        sums.pass_on(2, 1)
+        sums.pass_on(4, 0)
+        grads(middle, chunks)
+    else:
+        for k in range(0, width, 2):
+            give(k)
+        for k in range(2, width, 2):
+            merge(k)
+            sums.far(k, 0).start()
+            sums.far(k, 1).start()
+        grads(0, chunks)
+    sums.got(0)
+    produce(0, out_ref, (sums.from_twin.at[0],))
+    sums.finish()
+    stored(chunks - 2).wait()
+    stored(chunks - 1).wait()
+
+
+def pull(grad_gate, grad_up, gate_weight, up_weight, gathered, width, slots, ident, name):
+    count, cols = gathered.shape
+    hidden = gate_weight.shape[1]
+    rows = count // width
+    low, dma = gathered.dtype, pltpu.SemaphoreType.DMA
+    chunk = 256
+    anywhere = pl.BlockSpec(memory_space=pl.ANY)
+    return pl.pallas_call(
+        functools.partial(pull_body, width, slots, 1024, chunk),
+        out_shape=[
+            jax.ShapeDtypeStruct((rows, cols), jnp.float32), jax.ShapeDtypeStruct((cols, 2 * hidden), low),
+        ],
+        in_specs=[anywhere] * 5,
+        out_specs=[pl.BlockSpec(memory_space=pltpu.VMEM), anywhere],
+        scratch_shapes=[
+            pltpu.VMEM((count, hidden), low), pltpu.VMEM((count, hidden), low),
+            pltpu.VMEM((cols, hidden), low), pltpu.VMEM((cols, hidden), low),
+            pltpu.VMEM((2, count, chunk), low), pltpu.VMEM((2, chunk, 2 * hidden), low),
+            dma((4,)), dma((2,)), dma((2,)),
+        ] + sum_scratch(width, rows, cols),
+        cost_estimate=busy(10),
+        compiler_params=pltpu.CompilerParams(collective_id=ident, has_side_effects=True, vmem_limit_bytes=VMEM_LIMIT),
+        name=name,
+    )(grad_gate, grad_up, gate_weight, up_weight, gathered)
 
 
 def local(
@@ -720,10 +1272,6 @@
     w_qkv = lax.all_gather(qkv_rows, "blk", axis=0, tiled=True)
     w_o = lax.all_gather(after(output_weight, w_qkv), "blk", axis=1, tiled=True)
     gains = jnp.stack([query_gain, key_gain]).astype(f32)
-    both = after(jnp.stack([attention_gain, feedforward_gain]), w_qkv)
-    both = lax.all_gather(both, "wide", axis=1, tiled=True).astype(f32)
-    gain_mix, gain_feed = both[0], both[1]
-
     plane_lengths = lax.dynamic_slice_in_dim(lengths, plane * slots, slots, 0)
     segment, position = jax.vmap(lambda one: layout(one, span))(plane_lengths)
     begin = (jnp.arange(span, dtype=jnp.int32)[None] - position)[:, None, :]
@@ -736,8 +1284,14 @@
     inputs = gather(mine, width, slots, 2, "gather_tokens")
     pre = dot(inputs, w_qkv)
     squares = jnp.stack([jnp.sum(pre[:, a * share : (a + 1) * share] ** 2, -1) for a in (0, 1)])
-    squares = total(squares.reshape(-1, 128), "wide", width, 3, "total_squares")
-    inverse = lax.rsqrt(squares.reshape(2, count) / D + EPS)
+    both = lax.dynamic_update_slice(
+        jnp.zeros((2, D), f32), jnp.stack([attention_gain, feedforward_gain]).astype(f32), (0, place * share)
+    )
+    squares = jnp.concatenate([squares.reshape(-1, 128), both.reshape(-1, 128)])
+    squares = total(squares, "wide", width, 3, "total_squares")
+    both = squares[2 * count // 128 :].reshape(2, D)
+    gain_mix, gain_feed = both[0], both[1]
+    inverse = lax.rsqrt(squares[: 2 * count // 128].reshape(2, count) / D + EPS)
     inv_cols = inverse.T.reshape(slots, span, 2)
     pre_groups = pre.reshape(slots, span, 3 * share)
     queries, keys, values, mixed, logs = attend(
@@ -747,43 +1301,30 @@
     projected = scatter([mixed], [w_o], width, slots, False, 4, "scatter_mixed")
     proj_normed, proj_inv = rms_pair(projected)
     hidden = mine.astype(f32) + proj_normed * gain_mix
-    gathered, grad_out = gather(
-        hidden.astype(low), width, slots, 5, "gather_hidden", "join", near_cotangent
+    reduced, gathered, activated, up_factor, gate_factor, grad_out = feed(
+        hidden.astype(low), near_cotangent, gate_weight, up_weight, down_weight, width, slots, 5, "feed"
     )
     grad_out = grad_out.astype(f32)
-    gate = dot(gathered, gate_weight)
-    upward = dot(gathered, up_weight)
-    sigmoid = jax.nn.sigmoid(gate)
-    activated = (gate * sigmoid * upward).astype(low)
-    reduced = scatter([activated], [down_weight], width, slots, False, 6, "scatter_down")
     red_normed, red_inv = rms_pair(reduced)
     block_output = (hidden + red_normed * gain_feed).astype(low)
 
     feed_gain_part = jnp.sum(grad_out * red_normed, axis=0)
     grad_reduced = norm_back(red_normed, red_inv, grad_out * gain_feed).astype(low)
-    grad_rows, far_output = gather(
-        grad_reduced, width, slots, 7, "gather_grad", "spread", block_output
+    down_part, grad_gate, grad_up, far_output = push(
+        grad_reduced, block_output, down_weight, activated, up_factor, gate_factor, width, slots, 7, "push"
     )
-    down_part = contract_rows(activated, grad_rows).astype(low)
-    grad_rows, down_part = lax.optimization_barrier((grad_rows, down_part))
     down_grad = over_blk(down_part, 1)
-    grad_act = contract_cols(grad_rows, down_weight)
-    grad_up = (grad_act * gate * sigmoid).astype(low)
-    grad_gate = (grad_act * upward * sigmoid * (1.0 + gate * (1.0 - sigmoid))).astype(low)
-    gate_part = contract_rows(gathered, grad_gate).astype(low)
-    grad_up, gate_part = lax.optimization_barrier((grad_up, gate_part))
-    gate_grad = over_blk(gate_part, 0)
-    grad_hidden = grad_out + scatter(
-        [grad_gate, grad_up], [gate_weight, up_weight], width, slots, True, 8, "scatter_hidden"
+    hidden_part, inner_part = pull(
+        grad_gate, grad_up, gate_weight, up_weight, gathered, width, slots, 8, "pull"
     )
-    up_part = contract_rows(gathered, after(grad_up, grad_hidden)).astype(low)
-    up_grad = over_blk(up_part, 0)
+    grad_hidden = grad_out + hidden_part
+    inner_grad = over_blk(inner_part, 0)
     mix_gain_part = jnp.sum(grad_hidden * proj_normed, axis=0)
     grad_proj = norm_back(proj_normed, proj_inv, grad_hidden * gain_mix).astype(low)
-    grad_proj = gather(after(grad_proj, up_part, down_grad), width, slots, 9, "gather_proj")
-    output_part = contract_rows(mixed, grad_proj).astype(low)
+    grad_proj = gather(grad_proj, width, slots, 9, "gather_proj")
+    output_part = contract_rows(grad_proj, mixed).astype(low)
+    grad_proj = after(grad_proj, down_grad)
     grad_mixed = contract_cols(grad_proj, w_o).astype(low).reshape(slots, span, share)
-    grad_mixed = after(grad_mixed, gate_grad)
     scaled_q, scaled_k, grad_v, sums, parts = attend_back(
         queries, keys, values, grad_mixed, logs, pre_groups, inv_cols, gains, cosine, sine, begin,
         heads, rows,
@@ -797,15 +1338,13 @@
         return (inverse[index][:, None] * (scaled - normed * means[index][:, None])).astype(low)
 
     grads = jnp.concatenate([finish(scaled_q, 0), finish(scaled_k, 1), grad_v.reshape(count, share)], 1)
-    grads = after(grads, up_grad)
     tokens_part = scatter([grads], [w_qkv], width, slots, True, 11, "scatter_tokens")
     _, block_output, tokens_grad = turn(
-        turn_out_body, [(grad_hidden + tokens_part).astype(low), far_output], [True, False, False],
+        turn_out_body, [after((grad_hidden + tokens_part).astype(low), inner_grad), far_output], [True, False, False],
         planes, slots, 14, "turn_out",
     )
-    output_grad = over_blk(output_part, 1)
-    qkv_part = contract_rows(inputs, grads)
-    qkv_grad = over_blk(qkv_part, 0)
+    qkv_part = contract_rows(inputs, grads).astype(low)
+    side_grad = over_blk(jnp.concatenate([qkv_part, output_part], 1), 0)
 
     gain_parts = jnp.sum(parts, axis=0)
     local_gains = lax.dynamic_update_slice(jnp.zeros((2, D), f32), gain_parts, (0, place * share))
@@ -817,15 +1356,15 @@
     return (
         block_output[None],
         tokens_grad[None].astype(f32),
-        qkv_grad[:, :share],
-        qkv_grad[:, share : 2 * share],
-        qkv_grad[:, 2 * share :],
-        output_grad,
+        side_grad[:, :share],
+        side_grad[:, share : 2 * share],
+        side_grad[:, 2 * share : 3 * share],
+        side_grad[:, 3 * share :].T,
         sums[0],
         sums[1],
         sums[2],
-        gate_grad,
-        up_grad,
+        inner_grad[:, : gate_weight.shape[1]],
+        inner_grad[:, gate_weight.shape[1] :],
         down_grad,
         sums[3],
     )

time: 877 us -> 763 us (0.87)
  matrix products: 157 us -> 39.5 us
  Pallas kernels: 613 us -> 627 us
  blocking collectives: 8.84 us -> 0 us
    pallas_call x0 -> x3, Pallas kernels: none -> 222 us  [the longest x1 95.3 us: feed(): pl.pallas_call(functools.partial(feed_body, width, slots, step), out_shap...]
    pallas_call x4 -> x2, Pallas kernels: 236 us -> 111 us  [scatter(): pl.pallas_call(functools.partial(scatter_body, width, slots, flat, len(le...]
    pallas_call x4 -> x2, Pallas kernels: 204 us -> 97.1 us  [gather(): pl.pallas_call(functools.partial(gather_body, width, slots, side), out_sh...]
    dot_general x5 -> x2, matrix products: 72.1 us -> 19.3 us  [contract_rows(): lax.dot_general(left, right, (((0,), (0,)), ((), ())), preferred_element_...]
    dot_general x3 -> x1, matrix products: 48.7 us -> 12.1 us  [dot(): return jnp.dot(left, right, preferred_element_type=jnp.float32)]
    dot_general x2 -> x1, matrix products: 35.7 us -> 8.11 us  [contract_cols(): lax.dot_general(left, right, (((1,), (1,)), ((), ())), preferred_element_...]
    pallas_call x2, Pallas kernels: 93.9 us -> 117 us  [turn(): pl.pallas_call(functools.partial(body, planes, slots), out_shape=[shape(m...]
    all_gather x1 -> x0, blocking collectives: 8.84 us -> none  [local(): both = lax.all_gather(both, 'wide', axis=1, tiled=True).astype(f32)]
  transfers between devices with their start and end apart: 7 -> 5, of which waited for: 1 -> 1; matrix products, arithmetic and copies ran while one was open for 18% -> 11% of each run, Pallas kernels for 40% -> 49%
where the time goes in v2:
time: 763 us; the launch traced here: 757 us
  Pallas kernels  627 us (82%)
  other arithmetic  53.8 us (7%)
  matrix products  39.5 us (5%)
  local copies, waits for them, and re-layouts  17.8 us (2%)
  between operations  14.8 us (2%)
    pallas_call x2, Pallas kernels, turn(): pl.pallas_call(functools.partial(body, planes, slots), out_shape=[shape(m...  117 us
    pallas_call x2, Pallas kernels, scatter(): pl.pallas_call(functools.partial(scatter_body, width, slots, flat, len(le...  111 us
    pallas_call x2, Pallas kernels, gather(): pl.pallas_call(functools.partial(gather_body, width, slots, side), out_sh...  97.1 us
    pallas_call x1, Pallas kernels, feed(): pl.pallas_call(functools.partial(feed_body, width, slots, step), out_shap...  95.3 us
    pallas_call x1, Pallas kernels, pull(): pl.pallas_call(functools.partial(pull_body, width, slots, 1024, chunk), o...  64.3 us
    pallas_call x1, Pallas kernels, push(): pl.pallas_call(functools.partial(push_body, width, slots, step), out_shap...  62.5 us
    pallas_call x4, Pallas kernels, total(): pl.pallas_call(functools.partial(total_body, axis, width), out_shape=jax....  34.9 us
    pallas_call x1, Pallas kernels, attend_back(): pl.pallas_call(functools.partial(attend_back_body, size), grid=(slots, he...  27.2 us
  transfers between devices with their start and end apart: 5, of which 1 were waited for; matrix products, arithmetic and copies ran while one was open for 11% of the time, Pallas kernels for 49%

profile of v2, /device:TPU:8, one launch (start us, length us, event | category | flops | bytes accessed | tf_op | source)
XLA Modules:
  0.0 756.6 jit_solution(13509174491570729481)
XLA Ops:
  7.3 48.1 %turn_in.1 = (bf16[320,2048]{1,0:T(8,128)(2,1)}, bf16[320,2048]{1,0:T(8,128)(2,1)}, bf16[320,2048]{1,0:T(8,128)(2,1)}) custom-call(bf16[320,2048]{1,0:T(8,128)(2,1)} %bitcast.74, bf16[320,2048]{1,0:T(8,128)(2,1)} %bitcast.75), custom_call_target="tpu_custom_call" | custom-call | bytes 35000000 | tf_op jit(solution)/shard_map/turn_in/pallas_call | solution.py:566
  55.4 0.9 pad_maximum_fusion.4
  56.4 49.4 %gather_tokens.1 = bf16[2560,2048]{1,0:T(8,128)(2,1)} custom-call(bf16[320,2048]{1,0:T(8,128)(2,1)} %get-tuple-element.43.refs_0_), custom_call_target="tpu_custom_call" | custom-call | bytes 35000000 | tf_op jit(solution)/shard_map/gather_tokens/pallas_call | solution.py:294
  107.0 4.6 fusion.11
  111.6 2.2 pad_maximum_fusion.2
  114.5 3.1 all-gather.3.cloned.1.call-done.refs_1_
  117.9 12.1 %fusion.18 = f32[2560,768]{1,0:T(8,128)S(1)} fusion(bf16[2560,2048]{1,0:T(8,128)(2,1)} %gather_tokens.1, bf16[2048,768]{1,0:T(8,128)(2,1)} %all-gather.3.cloned.1.call-done.refs_1_), kind=kOutput, calls=%fused_computation.81 | convolution fusion | flops 8053063680 | bytes 21495808 | tf_op jit(solution)/shard_map/dot_general | solution.py:51
  129.9 3.1 copy-done.2
  133.0 0.7 multiply_reduce_fusion.5
  134.5 8.3 %total_squares.1 = f32[72,128]{1,0:T(8,128)} custom-call(f32[72,128]{1,0:T(8,128)} %pad_maximum_fusion.5.x_ref), custom_call_target="tpu_custom_call" | custom-call | bytes 24500000 | tf_op jit(solution)/shard_map/total_squares/pallas_call | solution.py:410
  143.5 1.5 copy.31
  145.0 17.7 %attend.1 = (bf16[2,1280,256]{2,1,0:T(8,128)(2,1)}, bf16[2,1280,256]{2,1,0:T(8,128)(2,1)}, bf16[2,1280,256]{2,1,0:T(8,128)(2,1)}, bf16[2,1280,256]{2,1,0:T(8,128)(2,1)}, f32[2,2,1,1280]{3,2,1,0:T(1,128)}) custom-call(f32[2,1280,768]{2,1,0:T(8,128)} %bitcast.65, f32[2,1280,768]{2,1,0:T(8,128)} %bitcast.66, f32[2,1280,768]{2,1,0:T(8,128)} %bitcast.67, ...), custom_call_target="tpu_custom_call" | custom-call | bytes 17500000 | tf_op jit(solution)/shard_map/attend/pallas_call | solution.py:649
  163.4 54.1 %scatter_mixed.1 = f32[320,2048]{1,0:T(8,128)} custom-call(bf16[2560,256]{1,0:T(8,128)(2,1)} %bitcast.77, bf16[256,2048]{1,0:T(8,128)(2,1)} %all-gather.5.cloned.1.call-done.refs_1_), custom_call_target="tpu_custom_call" | custom-call | bytes 35000000 | tf_op jit(solution)/shard_map/scatter_mixed/pallas_call | solution.py:373
  217.5 2.2 multiply_reduce_fusion.3
  220.0 2.9 fusion.10.h_ref
  222.9 95.3 %feed.1 = (f32[320,2048]{1,0:T(8,128)}, bf16[2560,2048]{1,0:T(8,128)(2,1)}, bf16[2560,1024]{1,0:T(8,128)(2,1)}, bf16[2560,1024]{1,0:T(8,128)(2,1)}, bf16[2560,10...) custom-call(bf16[320,2048]{1,0:T(8,128)(2,1)} %fusion.10.h_ref, bf16[320,2048]{1,0:T(8,128)(2,1)} %get-tuple-element.47.c_ref, ...), custom_call_target="tpu_custom_call" | custom-call | bytes 315000000 | tf_op jit(solution)/shard_map/feed/pallas_call | solution.py:927
  318.2 2.2 multiply_reduce_fusion.2
  320.7 4.5 fusion.5
  325.2 1.8 fusion.4.g_ref
  327.0 62.5 %push.1 = (bf16[1024,2048]{1,0:T(8,128)(2,1)}, bf16[2560,1024]{1,0:T(8,128)(2,1)}, bf16[2560,1024]{1,0:T(8,128)(2,1)}, bf16[320,2048]{1,0:T(8,128)(2,1)}) custom-call(bf16[320,2048]{1,0:T(8,128)(2,1)} %fusion.4.g_ref, bf16[320,2048]{1,0:T(8,128)(2,1)} %get-tuple-element.107.c_ref, bf16[1024,2048]{1,0:T(8,128)(2,1)} %wd_hbm.3, ...), custom_call_target="tpu_custom_call" | custom-call | bytes 35000000 | tf_op jit(solution)/shard_map/push/pallas_call | solution.py:1089
  389.6 64.3 %pull.1 = (f32[320,2048]{1,0:T(8,128)}, bf16[2048,2048]{1,0:T(8,128)(2,1)}) custom-call(bf16[2560,1024]{1,0:T(8,128)(2,1)} %get-tuple-element.53.gg_hbm, bf16[2560,1024]{1,0:T(8,128)(2,1)} %get-tuple-element.54.gu_hbm, bf16[2048,1024]{1,0:T(8,128)(2,1)} %wg_hbm.3, bf16[2048,1024]{1,0:T(8,128)(2,1)} %wu_hbm.3, bf16[2560,2048]{1,0:T(8,128)(2,1)} %get-tuple-element.55.h_hbm), custom_call_target="tpu_custom_call" | custom-call | bytes 35000000 | tf_op jit(solution)/shard_map/pull/pallas_call | solution.py:1217
  454.0 3.3 multiply_reduce_fusion
  457.4 1.8 multiply_convert_fusion.refs_0_
  459.2 47.7 %gather_proj.1 = bf16[2560,2048]{1,0:T(8,128)(2,1)} custom-call(bf16[320,2048]{1,0:T(8,128)(2,1)} %multiply_convert_fusion.refs_0_), custom_call_target="tpu_custom_call" | custom-call | bytes 35000000 | tf_op jit(solution)/shard_map/gather_proj/pallas_call | solution.py:294
  506.9 8.0 %convolution_convert_fusion.2 = bf16[2048,256]{0,1:T(8,128)(2,1)} fusion(bf16[2560,2048]{1,0:T(8,128)(2,1)} %gather_proj.1, bf16[2560,256]{1,0:T(8,128)(2,1)S(1)} %bitcast.78), kind=kOutput, calls=%fused_computation.29 | convolution fusion | flops 2684878848 | bytes 12845056 | tf_op jit(solution)/shard_map/dot_general | solution.py:55
  514.9 2.9 convert_element_type.101
  517.8 8.1 %convolution_convert_fusion = bf16[2560,256]{1,0:T(8,128)(2,1)} fusion(bf16[2560,2048]{1,0:T(8,128)(2,1)} %gather_proj.1, bf16[256,2048]{1,0:T(8,128)(2,1)S(1)} %copy-done.17), kind=kOutput, calls=%fused_computation.5 | convolution fusion | flops 2685009920 | bytes 12845056 | tf_op jit(solution)/shard_map/dot_general | solution.py:61
  525.9 27.2 %attend_back.1 = (f32[2,1280,256]{2,1,0:T(8,128)}, f32[2,1280,256]{2,1,0:T(8,128)}, bf16[2,1280,256]{2,1,0:T(8,128)(2,1)}, f32[2,2,1280,2]{3,2,1,0:T(8,128)}, f32[2,2,256]{2,1,0:T(2,128)}) custom-call(bf16[2,1280,256]{2,1,0:T(8,128)(2,1)} %get-tuple-element.57.q_ref, bf16[2,1280,256]{2,1,0:T(8,128)(2,1)} %get-tuple-element.58.k_ref, ...), custom_call_target="tpu_custom_call" | custom-call | bytes 17500000 | tf_op jit(solution)/shard_map/attend_back/pallas_call | solution.py:712
  553.1 2.1 reduce_sum.96
  556.3 7.0 total_means.1
  564.0 5.5 fusion.9
  569.5 11.3 %convolution_convert_fusion.1 = bf16[2048,768]{0,1:T(8,128)(2,1)S(1)} fusion(bf16[2560,2048]{1,0:T(8,128)(2,1)} %gather_tokens.1, bf16[2560,256]{1,0:T(8,128)(2,1)S(1)} %bitcast.80, bf16[2560,256]{1,0:T(8,128)(2,1)S(1)} %get-tuple-element.106, bf16[2560,256]{1,0:T(8,128)(2,1)S(1)} %get-tuple-element.105), kind=kOutput, calls=%fused_computation.6 | convolution fusion | flops 8066433024 | bytes 17563648 | tf_op jit(solution)/shard_map/dot_general | solution.py:55
  580.9 2.2 pad_maximum_fusion
  584.5 7.9 %total_gains.1.x_ref = f32[64,128]{1,0:T(8,128)} custom-call(f32[64,128]{1,0:T(8,128)} %reshape.313.x_ref), custom_call_target="tpu_custom_call" | custom-call | bytes 24500000 | tf_op jit(solution)/shard_map/total_gains/pallas_call | solution.py:410
  592.4 11.7 %total_gains_blk.1 = f32[64,128]{1,0:T(8,128)} custom-call(f32[64,128]{1,0:T(8,128)} %total_gains.1.x_ref), custom_call_target="tpu_custom_call" | custom-call | bytes 24500000 | tf_op jit(solution)/shard_map/total_gains_blk/pallas_call | solution.py:410
  604.1 0.8 reshape.314
  604.9 3.4 pad_maximum_fusion.1.refs_0_
  608.4 57.3 %scatter_tokens.1 = f32[320,2048]{1,0:T(8,128)} custom-call(bf16[2560,768]{1,0:T(8,128)(2,1)} %pad_maximum_fusion.1.refs_0_, bf16[2048,768]{1,0:T(8,128)(2,1)} %all-gather.3.cloned.1.call-done.refs_1_), custom_call_target="tpu_custom_call" | custom-call | bytes 35000000 | tf_op jit(solution)/shard_map/scatter_tokens/pallas_call | solution.py:373
  666.2 3.6 add_convert_fusion.x_ref
  669.8 68.8 %turn_out.1 = (bf16[320,2048]{1,0:T(8,128)(2,1)}, bf16[320,2048]{1,0:T(8,128)(2,1)}, bf16[320,2048]{1,0:T(8,128)(2,1)}) custom-call(bf16[320,2048]{1,0:T(8,128)(2,1)} %add_convert_fusion.x_ref, bf16[320,2048]{1,0:T(8,128)(2,1)} %get-tuple-element.69.far_c), custom_call_target="tpu_custom_call" | custom-call | bytes 35000000 | tf_op jit(solution)/shard_map/turn_out/pallas_call | solution.py:566
  738.6 2.5 fusion.15
  741.1 1.8 bitcast_convert_fusion
  742.9 1.6 convert_element_type.111
  744.5 0.8 slice_bitcast_fusion
  745.5 1.0 copy.33
  746.5 1.0 copy.34
  747.5 1.0 copy.35
  748.5 1.1 copy.41
  (109 shorter events, 9.2 us)
Async XLA Ops:
  7.2 98.6 %copy-start = (s32[8,3]{0,1:T(4,128)S(1)}, s32[8,3]{0,1:T(4,128)}, u32[]{:S(2)}) copy-start(s32[8,3]{0,1:T(4,128)} %param.15) | copy-start | bytes 292
  7.2 48.2 %copy-start.21 = (bf16[512,256]{1,0:T(8,128)(2,1)S(1)}, bf16[512,256]{1,0:T(8,128)(2,1)}, u32[]{:S(2)}) copy-start(bf16[512,256]{1,0:T(8,128)(2,1)} %param.16) | copy-start | bytes 786436
  7.2 48.2 %copy-start.20 = (bf16[512,256]{1,0:T(8,128)(2,1)S(1)}, bf16[512,256]{1,0:T(8,128)(2,1)}, u32[]{:S(2)}) copy-start(bf16[512,256]{1,0:T(8,128)(2,1)} %param.17) | copy-start | bytes 786436
  7.2 48.2 %copy-start.19 = (bf16[512,256]{1,0:T(8,128)(2,1)S(1)}, bf16[512,256]{1,0:T(8,128)(2,1)}, u32[]{:S(2)}) copy-start(bf16[512,256]{1,0:T(8,128)(2,1)} %param.18) | copy-start | bytes 786436
  7.2 110.4 %all-gather.3.cloned.1.call-start = ((), (), s32[]{:S(2)}) async-start(), calls=%async_computation.3 | async-start | bytes 3932160 | tf_op jit(solution)/shard_map/all_gather | solution.py:1272
  56.3 107.1 %all-gather.5.cloned.1.call-start = ((), (), s32[]{:S(2)}) async-start(), calls=%async_computation.4 | async-start | bytes 1310720 | tf_op jit(solution)/shard_map/all_gather | solution.py:1273
  56.4 49.8 %copy-start.23 = (bf16[256]{0:T(256)(128)(2,1)S(1)}, bf16[256]{0:T(256)(128)(2,1)}, u32[]{:S(2)}) copy-start(bf16[256]{0:T(256)(128)(2,1)} %param.22) | copy-start | bytes 1540
  56.4 49.8 %copy-start.24 = (bf16[256]{0:T(256)(128)(2,1)S(1)}, bf16[256]{0:T(256)(128)(2,1)}, u32[]{:S(2)}) copy-start(bf16[256]{0:T(256)(128)(2,1)} %param.26) | copy-start | bytes 1540
  56.4 49.9 %copy-start.25 = (bf16[256]{0:T(256)(128)(2,1)S(1)}, bf16[256]{0:T(256)(128)(2,1)}, u32[]{:S(2)}) copy-start(bf16[256]{0:T(256)(128)(2,1)} %param.20) | copy-start | bytes 1540
  56.4 49.9 %copy-start.26 = (bf16[256]{0:T(256)(128)(2,1)S(1)}, bf16[256]{0:T(256)(128)(2,1)}, u32[]{:S(2)}) copy-start(bf16[256]{0:T(256)(128)(2,1)} %param.21) | copy-start | bytes 1540
  117.6 397.3 %reduce-scatter.4.cloned.1.call-start = ((), (), s32[]{:S(2)}) async-start(), calls=%async_computation.5 | async-start | bytes 5242880 | tf_op jit(solution)/shard_map/reduce_scatter | solution.py:1264
  129.9 3.1 copy-start.2
  217.5 2.5 copy-start.3
  318.2 2.2 copy-start.4
  318.2 2.5 copy-start.10
  320.7 4.6 copy-start.9
  389.5 280.3 %reduce-scatter.6.cloned.1.call-start = ((), (), s32[]{:S(2)}) async-start(), calls=%async_computation.6 | async-start | bytes 10485760 | tf_op jit(solution)/shard_map/reduce_scatter | solution.py:1264
  453.9 288.9 %reduce-scatter.8.cloned.1.call-start = ((), (), s32[]{:S(2)}) async-start(), calls=%async_computation.7 | async-start | bytes 5242880 | tf_op jit(solution)/shard_map/reduce_scatter | solution.py:1264
  454.0 3.3 copy-start.5
  454.0 3.3 copy-start.7
  459.2 47.7 %copy-start.14 = (bf16[2,1280,256]{2,1,0:T(8,128)(2,1)S(1)}, bf16[2,1280,256]{2,1,0:T(8,128)(2,1)}, u32[]{:S(2)}) copy-start(bf16[2,1280,256]{2,1,0:T(8,128)(2,1)} %get-tuple-element.45) | copy-start | bytes 3932164
  514.9 2.9 copy-start.17
  564.0 5.5 copy-start.16
  569.5 11.3 %copy-start.18 = (bf16[2048,256]{0,1:T(8,128)(2,1)S(1)}, bf16[2048,256]{0,1:T(8,128)(2,1)}, u32[]{:S(2)}) copy-start(bf16[2048,256]{0,1:T(8,128)(2,1)} %convolution_convert_fusion.2) | copy-start | bytes 3145732
  583.1 0.7 copy-start.22
  608.3 57.9 %copy-start.6 = (bf16[320,2048]{1,0:T(8,128)(2,1)S(1)}, bf16[320,2048]{1,0:T(8,128)(2,1)}, u32[]{:S(2)}) copy-start(bf16[320,2048]{1,0:T(8,128)(2,1)} %get-tuple-element.48) | copy-start | bytes 3932164
  608.3 57.9 %copy-start.8 = (f32[320,2048]{1,0:T(8,128)S(1)}, f32[320,2048]{1,0:T(8,128)}, u32[]{:S(2)}) copy-start(f32[320,2048]{1,0:T(8,128)} %get-tuple-element.56) | copy-start | bytes 7864324
  669.8 68.8 %copy-start.11 = (bf16[512,2048]{1,0:T(8,128)(2,1)S(1)}, bf16[512,2048]{1,0:T(8,128)(2,1)}, u32[]{:S(2)}) copy-start(bf16[512,2048]{1,0:T(8,128)(2,1)} %reduce-scatter.6.cloned.1.call-done) | copy-start | bytes 6291460
  738.6 2.5 copy-start.15
  742.9 2.4 copy-start.12
  745.3 3.2 copy-start.13
  745.5 4.1 copy-start.1
Sparse Core Ops, SparseCore 0:
  56.5 61.0 all-gather.2
  119.1 28.8 all-gather.4
  389.6 75.7 reduce-scatter.3
  467.8 147.4 reduce-scatter.5
  617.6 101.0 reduce-scatter.7

commit v3 on v2

--- a/solution.py
+++ b/solution.py
@@ -2,6 +2,7 @@
 
 import jax
 import jax.numpy as jnp
+import numpy as np
 from jax import lax
 from jax.experimental import pallas as pl
 from jax.experimental.pallas import tpu as pltpu
@@ -31,11 +32,14 @@
     return (segment, indices - offsets)
 
 
-def rope_tables(position):
-    frequency = ROPE_BASE ** (-jnp.arange(0, HD, 2, dtype=jnp.float32) / HD)
-    angles = position.astype(jnp.float32)[:, None] * frequency[None, :]
-    cosine, sine = jnp.cos(angles), jnp.sin(angles)
-    return (jnp.concatenate([cosine, cosine], -1), jnp.concatenate([-sine, sine], -1))
+def rope_tables(index, begin):
+    frequency = ROPE_BASE ** (-np.arange(0, HD, 2, dtype=np.float64) / HD)
+    angles = np.asarray(index, np.float64)[:, None] * frequency
+    sign = np.concatenate([-np.ones(HD // 2), np.ones(HD // 2)])
+    twice = lambda value: np.concatenate([value, value], -1).astype(np.float32)
+    cosine, sine = jnp.asarray(twice(np.cos(angles))), jnp.asarray(twice(np.sin(angles)))
+    shift = begin.astype(jnp.float32)[..., None] * jnp.asarray(twice(frequency))
+    return cosine, sine, jnp.cos(shift), jnp.sin(shift), jnp.asarray(sign.astype(np.float32))
 
 
 def rms_pair(values):
@@ -176,6 +180,57 @@
                 self.twin(k, part).wait_send()
             if self.width == 8:
                 self.relay(part).wait_send()
+
+
+def run_sums(width, sums, produce, beside=None, steps=0):
+    half = sums.half
+    rows = 2 * half
+
+    def give(k, part=None):
+        if part is None:
+            produce(k + 1, 0, rows, sums.odd.at[k // 2])
+            sums.give(k)
+        else:
+            produce(k + 1, part * half, half, sums.odd.at[k // 2, sums.rows(part)])
+            sums.twin(k, part).start()
+
+    def merge(k, part=None):
+        if part is None:
+            sums.got(k)
+            produce(k, 0, rows, sums.even.at[k // 2 - 1], (sums.from_twin.at[k // 2],))
+        else:
+            sums.twin(k, part).wait_recv()
+            at = sums.rows(part)
+            produce(k, part * half, half, sums.even.at[k // 2 - 1, at], (sums.from_twin.at[k // 2, at],))
+
+    if width == 8:
+        give(6, 0)
+        give(6, 1)
+        merge(6, 0)
+        sums.relay(0).start()
+        merge(6, 1)
+        sums.relay(1).start()
+        give(2)
+        give(4)
+        merge(2)
+        sums.far(2, 0).start()
+        merge(4)
+        sums.far(4, 1).start()
+        sums.pass_on(2, 1)
+        sums.pass_on(4, 0)
+        give(0)
+    else:
+        for k in range(0, width, 2):
+            give(k)
+        for k in range(2, width, 2):
+            merge(k)
+            sums.far(k, 0).start()
+            sums.far(k, 1).start()
+    if beside is not None:
+        beside(0, steps)
+    sums.got(0)
+    produce(0, 0, rows, sums.out, (sums.from_twin.at[0],))
+    sums.finish()
 
 
 def sum_scratch(width, rows, cols):
@@ -304,18 +359,24 @@
     return outs[0] if side is None else outs
 
 
-def scatter_body(width, slots, flat, count, step, *refs):
+def scatter_body(width, slots, flat, count, step, finish, *refs):
     lefts, rights = refs[:count], refs[count : 2 * count]
-    out_ref = refs[2 * count]
+    if finish == "norm":
+        x_ref, gain_ref, hidden_ref, low_ref, out_ref, inv_ref = refs[2 * count : 2 * count + 6]
+        rest = refs[2 * count + 6 :]
+    else:
+        more_ref, low_ref, out_ref = refs[2 * count : 2 * count + 3]
+        rest = refs[2 * count + 3 :]
     me = lax.axis_index("wide")
     rows, cols = out_ref.shape
     hello(wide_peers(width, me))
-    sums = Sums(width, me, out_ref, refs[2 * count + 1 :])
+    sums = Sums(width, me, out_ref, rest)
     dims = (((1,), (1 if flat else 0,)), ((), ()))
 
-    def produce(k, put, adds=()):
+    def produce(k, first, some, put, adds=()):
         who = flip(me, k)
-        start = pl.multiple_of(((who % slots) * (width // slots) + who // slots) * rows, rows)
+        start = ((who % slots) * (width // slots) + who // slots) * rows + first
+        start = pl.multiple_of(start, rows // 2)
 
         def tile(n, carry):
             at = pl.ds(pl.multiple_of(n * step, step), step)
@@ -323,7 +384,7 @@
             for left, right in zip(lefts, rights):
                 other = right[at, :] if flat else right[:, at]
                 term = lax.dot_general(
-                    left[pl.ds(start, rows), :], other, dims, preferred_element_type=jnp.float32
+                    left[pl.ds(start, some), :], other, dims, preferred_element_type=jnp.float32
                 )
                 total = term if total is None else total + term
             for ref in adds:
@@ -333,53 +394,53 @@
 
         lax.fori_loop(0, cols // step, tile, 0)
 
-    def give(k):
-        produce(k + 1, sums.odd.at[k // 2])
-        sums.give(k)
-
-    def merge(k):
-        sums.got(k)
-        produce(k, sums.even.at[k // 2 - 1], (sums.from_twin.at[k // 2],))
-
-    if width == 8:
-        give(6)
-        give(2)
-        give(4)
-        merge(6)
-        sums.relay(0).start()
-        sums.relay(1).start()
-        merge(2)
-        sums.far(2, 0).start()
-        merge(4)
-        sums.far(4, 1).start()
-        give(0)
-        sums.pass_on(2, 1)
-        sums.pass_on(4, 0)
-    else:
-        for k in range(0, width, 2):
-            give(k)
-        for k in range(2, width, 2):
-            merge(k)
-            sums.far(k, 0).start()
-            sums.far(k, 1).start()
-    sums.got(0)
-    produce(0, out_ref, (sums.from_twin.at[0],))
-    sums.finish()
-
-
-def scatter(lefts, rights, width, slots, flat, ident, name, step=1024):
+    run_sums(width, sums, produce)
+    if finish == "add":
+        def close(n, carry):
+            at = pl.ds(pl.multiple_of(n * 32, 32), 32)
+            low_ref[at, :] = (out_ref[at, :] + more_ref[at, :]).astype(low_ref.dtype)
+            return carry
+
+        lax.fori_loop(0, rows // 32, close, 0)
+    if finish != "norm":
+        return
+    few = 32
+
+    def norm(n, carry):
+        at = pl.ds(pl.multiple_of(n * few, few), few)
+        value = out_ref[at, :]
+        inverse = lax.rsqrt(jnp.sum(value * value, axis=-1, keepdims=True) * (1.0 / cols) + EPS)
+        value = value * inverse
+        out_ref[at, :] = value
+        inv_ref[at, :] = inverse
+        hidden = x_ref[at, :].astype(jnp.float32) + value * gain_ref[...]
+        hidden_ref[at, :] = hidden
+        low_ref[at, :] = hidden.astype(low_ref.dtype)
+        return carry
+
+    lax.fori_loop(0, rows // few, norm, 0)
+
+
+def scatter(lefts, rights, width, slots, flat, ident, name, finish, more, step=1024):
     rows = lefts[0].shape[0] // width
     cols = rights[0].shape[0 if flat else 1]
-    return pl.pallas_call(
-        functools.partial(scatter_body, width, slots, flat, len(lefts), step),
-        out_shape=jax.ShapeDtypeStruct((rows, cols), jnp.float32),
-        in_specs=[pl.BlockSpec(memory_space=pltpu.VMEM)] * (2 * len(lefts)),
-        out_specs=pl.BlockSpec(memory_space=pltpu.VMEM),
-        scratch_shapes=sum_scratch(width, rows, cols),
+    f32, vmem = jnp.float32, pl.BlockSpec(memory_space=pltpu.VMEM)
+    whole, low = jax.ShapeDtypeStruct((rows, cols), f32), jax.ShapeDtypeStruct((rows, cols), lefts[0].dtype)
+    shapes = [whole, low, whole, jax.ShapeDtypeStruct((rows, 1), f32)] if finish == "norm" else [low]
+    scratch = sum_scratch(width, rows, cols)
+    if finish == "add":
+        scratch = [pltpu.VMEM((rows, cols), f32)] + scratch
+    outs = pl.pallas_call(
+        functools.partial(scatter_body, width, slots, flat, len(lefts), step, finish),
+        out_shape=shapes,
+        in_specs=[vmem] * (2 * len(lefts) + len(more)),
+        out_specs=[vmem] * len(shapes),
+        scratch_shapes=scratch,
         cost_estimate=busy(10),
         compiler_params=pltpu.CompilerParams(collective_id=ident, has_side_effects=True, vmem_limit_bytes=VMEM_LIMIT),
         name=name,
-    )(*lefts, *rights)
+    )(*lefts, *rights, *more)
+    return outs if finish == "norm" else outs[0]
 
 
 def total_body(axis, width, x_ref, out_ref, slots, send, recv):
@@ -493,7 +554,7 @@
 
             self.when(self.active, receive)
 
-    def join(self, many, some, send, recv, across, start):
+    def join(self, many, some, send, recv, across, start, ready=None):
         if across:
             here = self.plane
             index = self.plane // self.per
@@ -504,14 +565,18 @@
             address = lambda who: {"wide": who * self.slots + self.slot}
 
         def give():
-            for k in range(1, self.planes):
+            for k in list(range(1, self.planes)) + [0]:
                 who = (here + k) % self.planes
-                far = self.remote(
-                    self.cut(many, who), self.cut(some, index), send.at[k], recv.at[index], address(who)
-                )
-                far.start() if start else far.wait_send()
-            own = pltpu.make_async_copy(self.cut(many, here), self.cut(some, index), send.at[0])
-            own.start() if start else own.wait()
+                if ready is not None:
+                    ready(who)
+                if k:
+                    copy = self.remote(
+                        self.cut(many, who), self.cut(some, index), send.at[k], recv.at[index], address(who)
+                    )
+                    copy.start() if start else copy.wait_send()
+                else:
+                    own = pltpu.make_async_copy(self.cut(many, here), self.cut(some, index), send.at[0])
+                    own.start() if start else own.wait()
 
         self.when(self.active, give)
         if not start:
@@ -524,6 +589,34 @@
                 elif self.per > 1:
                     pl.when(jnp.logical_not(self.active))(arrival.wait)
 
+    def arrival(self, some, many, send, recv, across):
+        here = self.plane if across else self.chip
+        own_piece = self.plane // self.per if across else self.chip % self.count
+
+        def ready(who):
+            block = self.cut(many, who)
+
+            @pl.when(who == here)
+            def _():
+                pltpu.make_async_copy(self.cut(some, own_piece), block, send.at[own_piece]).wait()
+
+            @pl.when(who != here)
+            def _():
+                pltpu.make_async_copy(block, block, recv.at[(who - here + self.planes) % self.planes]).wait()
+
+        return ready
+
+    def sent(self, some, many, send, across):
+        pieces = self.plane // self.per if across else self.chip
+        for k in range(self.count):
+            piece = (pieces + k) % self.count
+            block = self.cut(some, piece)
+            out = pltpu.make_async_copy(block, block, send.at[piece])
+            if k:
+                out.wait()
+            elif self.per > 1:
+                pl.when(jnp.logical_not(self.active))(out.wait)
+
 
 def hello(peers):
     barrier = pltpu.get_barrier_semaphore()
@@ -536,20 +629,39 @@
     hops = Hops(planes, slots, x_ref.shape[0])
     hello(hops.peers())
     hops.spread(x_ref, near_x, sems[0], sems[1], False, True)
-    hops.spread(x_ref, near_x, sems[0], sems[1], False, False)
-    hops.join(near_x, out_ref, sems[2], sems[3], True, True)
+    ready = hops.arrival(x_ref, near_x, sems[0], sems[1], False)
+    hops.join(near_x, out_ref, sems[2], sems[3], True, True, ready)
+    hops.sent(x_ref, near_x, sems[0], False)
     hops.spread(c_ref, near_c, sems[4], sems[5], False, True)
     hops.spread(c_ref, near_c, sems[4], sems[5], False, False)
     hops.join(near_x, out_ref, sems[2], sems[3], True, False)
 
 
-def turn_out_body(planes, slots, x_ref, far_c, far_x, out_c, out_ref, *sems):
+def turn_out_body(planes, slots, x_ref, far_c, v_ref, far_x, out_c, out_ref, v_out, *sems):
     hops = Hops(planes, slots, x_ref.shape[0])
     hello(hops.peers())
+    parts, send, recv = sems[6:]
+    moves = []
+    for k in range(1, planes):
+        copy = hops.remote(
+            v_ref, parts.at[planes - k - 1], send.at[k - 1], recv.at[planes - k - 1],
+            {"blk": (hops.plane + k) % planes},
+        )
+        copy.start()
+        moves.append(copy)
     hops.spread(x_ref, far_x, sems[0], sems[1], True, True)
     hops.join(far_c, out_c, sems[2], sems[3], False, True)
-    hops.spread(x_ref, far_x, sems[0], sems[1], True, False)
-    hops.join(far_x, out_ref, sems[4], sems[5], False, True)
+    ready = hops.arrival(x_ref, far_x, sems[0], sems[1], True)
+    hops.join(far_x, out_ref, sems[4], sems[5], False, True, ready)
+    hops.sent(x_ref, far_x, sems[0], True)
+    amount = v_ref[...]
+    for k in range(1, planes):
+        block = parts.at[k - 1]
+        pltpu.make_async_copy(block, block, recv.at[k - 1]).wait()
+        amount = amount + parts[k - 1]
+    v_out[...] = amount
+    for copy in moves:
+        copy.wait_send()
     hops.join(far_c, out_c, sems[2], sems[3], False, False)
     hops.join(far_x, out_ref, sems[4], sems[5], False, False)
 
@@ -559,20 +671,26 @@
     return planes * (rows // count)
 
 
-def turn(body, inputs, outputs, planes, slots, ident, name):
+def turn(body, inputs, outputs, planes, slots, ident, name, extra=None):
     rows, cols = inputs[0].shape
     low = inputs[0].dtype
+    dma = pltpu.SemaphoreType.DMA
     shape = lambda many: jax.ShapeDtypeStruct((many_rows(planes, rows) if many else rows, cols), low)
+    anywhere, vmem = pl.BlockSpec(memory_space=pl.ANY), pl.BlockSpec(memory_space=pltpu.VMEM)
+    more = [] if extra is None else [extra]
+    scratch = [dma((planes,))] * 6
+    for value in more:
+        scratch += [pltpu.VMEM((planes - 1,) + value.shape, value.dtype), dma((planes - 1,)), dma((planes - 1,))]
     return pl.pallas_call(
         functools.partial(body, planes, slots),
-        out_shape=[shape(many) for many in outputs],
-        in_specs=[pl.BlockSpec(memory_space=pl.ANY)] * len(inputs),
-        out_specs=[pl.BlockSpec(memory_space=pl.ANY)] * len(outputs),
-        scratch_shapes=[pltpu.SemaphoreType.DMA((planes,))] * 6,
+        out_shape=[shape(many) for many in outputs] + [jax.ShapeDtypeStruct(v.shape, v.dtype) for v in more],
+        in_specs=[anywhere] * len(inputs) + [vmem] * len(more),
+        out_specs=[anywhere] * len(outputs) + [vmem] * len(more),
+        scratch_shapes=scratch,
         cost_estimate=busy(10),
         compiler_params=pltpu.CompilerParams(collective_id=ident, has_side_effects=True, vmem_limit_bytes=VMEM_LIMIT),
         name=name,
-    )(*inputs)
+    )(*inputs, *more)
 
 
 def mask_scores(scores, first, begin, size):
@@ -735,9 +853,13 @@
     )(queries, keys, values, grads, logs, pre, pre, inverse, gains, cosine, sine, begin)
 
 
-def feed_body(width, slots, step, h_ref, c_ref, wg_hbm, wu_hbm, wd_hbm, out_ref, all_ref, act_ref, one_ref,
-              two_ref, c_out, buf, wg, wu, wd, stage, here, load, send, recv, side_send, side_recv, store,
-              keep, *sum_refs):
+def row_sums(value):
+    return jnp.sum(value.reshape(-1, 8, value.shape[-1]), axis=0)
+
+
+def feed_body(width, slots, step, h_ref, c_ref, wg_hbm, wu_hbm, wd_hbm, hidden_ref, gain_ref, block_ref,
+              first_ref, second_ref, gain_out, all_ref, act_ref, one_ref, two_ref, c_out, buf, wg, wu, wd, stage, out_ref,
+              c_held, here, load, send, recv, side_send, side_recv, store, keep, *sum_refs):
     me = lax.axis_index("wide")
     planes = width // slots
     rows, cols = h_ref.shape
@@ -912,62 +1034,100 @@
     out_ref[...] = out_ref[...] + sums.from_twin[0].astype(jnp.float32)
     sums.finish()
     flow.finish()
+    hops.join(c_ref, c_out, side_send, side_recv, True, False)
+    held = pltpu.make_async_copy(c_out, c_held, here)
+    held.start()
+    held.wait()
+    gain_out[...] = jnp.zeros_like(gain_out)
+    few = 32
+    own = cols // planes
+    half_own = own // 2
+
+    def norm(n, carry):
+        at = pl.ds(pl.multiple_of(n * few, few), few)
+        value = out_ref[at, :]
+        inverse = lax.rsqrt(jnp.sum(value * value, axis=-1, keepdims=True) * (1.0 / cols) + EPS)
+        normed = value * inverse
+        block_ref[at, :] = (hidden_ref[at, :] + normed * gain_ref[...]).astype(low)
+        grad = c_held[at, :].astype(jnp.float32)
+        gain_out[...] = gain_out[...] + row_sums(grad * normed)
+        grad = grad * gain_ref[...]
+        mean = jnp.sum(grad * normed, axis=-1, keepdims=True) * (1.0 / cols)
+        grad = (inverse * (grad - normed * mean)).astype(low)
+        for b in range(planes):
+            for side in (0, 1):
+                first = b * own + side * half_own
+                (first_ref, second_ref)[side][at, b * half_own : (b + 1) * half_own] = grad[:, first : first + half_own]
+        return carry
+
+    lax.fori_loop(0, rows // few, norm, 0)
     for copy in kept + pending[0] + pending[1]:
         copy.wait()
-    hops.join(c_ref, c_out, side_send, side_recv, True, False)
-
-
-def feed(h, side_x, gate_weight, up_weight, down_weight, width, slots, ident, name):
+
+
+def feed(h, side_x, gate_weight, up_weight, down_weight, hidden, gain, width, slots, ident, name):
     rows, cols = h.shape
-    hidden = gate_weight.shape[1]
-    low, dma = h.dtype, pltpu.SemaphoreType.DMA
-    step = min(512, hidden)
-    anywhere = pl.BlockSpec(memory_space=pl.ANY)
-    saved = jax.ShapeDtypeStruct((rows * width, hidden), low)
+    inner = gate_weight.shape[1]
+    low, f32, dma = h.dtype, jnp.float32, pltpu.SemaphoreType.DMA
+    step = min(512, inner)
+    anywhere, vmem = pl.BlockSpec(memory_space=pl.ANY), pl.BlockSpec(memory_space=pltpu.VMEM)
+    saved = jax.ShapeDtypeStruct((rows * width, inner), low)
     return pl.pallas_call(
         functools.partial(feed_body, width, slots, step),
         out_shape=[
-            jax.ShapeDtypeStruct((rows, cols), jnp.float32), jax.ShapeDtypeStruct((rows * width, cols), low),
+            jax.ShapeDtypeStruct((rows, cols), low), jax.ShapeDtypeStruct((rows, cols // 2), low),
+            jax.ShapeDtypeStruct((rows, cols // 2), low),
+            jax.ShapeDtypeStruct((8, cols), f32), jax.ShapeDtypeStruct((rows * width, cols), low),
             saved, saved, saved, jax.ShapeDtypeStruct((rows, cols), low),
         ],
-        in_specs=[anywhere] * 5,
-        out_specs=[pl.BlockSpec(memory_space=pltpu.VMEM)] + [anywhere] * 5,
+        in_specs=[anywhere] * 5 + [vmem] * 2,
+        out_specs=[vmem] * 4 + [anywhere] * 5,
         scratch_shapes=[
-            pltpu.VMEM((width, rows, cols), low), pltpu.VMEM((cols, hidden), low), pltpu.VMEM((cols, hidden), low),
-            pltpu.VMEM((hidden, cols), low), pltpu.VMEM((2, 3, rows, hidden), low),
+            pltpu.VMEM((width, rows, cols), low), pltpu.VMEM((cols, inner), low), pltpu.VMEM((cols, inner), low),
+            pltpu.VMEM((inner, cols), low), pltpu.VMEM((2, 3, rows, inner), low),
+            pltpu.VMEM((rows, cols), f32), pltpu.VMEM((rows, cols), low),
             dma, dma((3,)), dma((width, 2)), dma((width, 2)), dma((width // slots,)), dma((width // slots,)),
             dma((2, 3)), dma((width,)),
         ] + sum_scratch(width, rows, cols),
         cost_estimate=busy(90),
         compiler_params=pltpu.CompilerParams(collective_id=ident, has_side_effects=True, vmem_limit_bytes=VMEM_LIMIT),
         name=name,
-    )(h, side_x, gate_weight, up_weight, down_weight)
-
-
-def push_body(width, slots, step, g_ref, c_ref, wd_hbm, act_hbm, one_hbm, two_hbm, down_ref, gg_ref, gu_ref, c_out,
-              buf, wd, held, ins, outs, here, load, send, recv, side_send, side_recv, fetch, store):
+    )(h, side_x, gate_weight, up_weight, down_weight, hidden, gain)
+
+
+def push_body(second, width, slots, *refs):
+    if second:
+        (g_ref, act_hbm, wd_hbm, one_hbm, two_hbm, first_hbm, down_ref, gg_ref, gu_ref,
+         buf, held, acts, here, send, recv, fetch, wd, before, ins, outs, load, take, store) = refs
+    else:
+        (g_ref, act_hbm, c_ref, down_ref, all_ref, c_out,
+         buf, held, acts, here, send, recv, fetch, keep, side_send, side_recv) = refs
     me = lax.axis_index("wide")
     planes = width // slots
+    pairs = width // 2
     rows, cols = g_ref.shape
-    hidden = wd.shape[0]
+    inner = down_ref.shape[0]
     half = rows // 2
     low = jnp.bfloat16
-    weights = pltpu.make_async_copy(wd_hbm, wd, load)
     mine = pltpu.make_async_copy(g_ref, buf.at[me // 2, me % 2], here)
     mine.start()
-    weights.start()
-    sources = (act_hbm, one_hbm, two_hbm)
 
     def where(pair, side):
         who = flip(me // 2, pair) * 2 + side
         return pl.ds(pl.multiple_of(((who % slots) * planes + who // slots) * rows, rows), rows)
 
     def fetches(pair):
-        return [
-            pltpu.make_async_copy(ref.at[where(pair, side)], ins.at[pair % 2, i, side], fetch.at[pair % 2, i, side])
-            for i, ref in enumerate(sources)
+        copies = [
+            pltpu.make_async_copy(act_hbm.at[where(pair, side)], acts.at[pair % 2, side], fetch.at[pair % 2, side])
             for side in (0, 1)
         ]
+        if second:
+            copies += [
+                pltpu.make_async_copy(ref.at[where(pair, side)], ins.at[pair % 2, i, side], take.at[pair % 2, i, side])
+                for i, ref in enumerate((one_hbm, two_hbm))
+                for side in (0, 1)
+            ]
+        return copies
 
     def stores(pair):
         return [
@@ -976,12 +1136,31 @@
             for side in (0, 1)
         ]
 
+    def keeps(pair):
+        chip = flip(me // 2, pair)
+        return pltpu.make_async_copy(buf.at[chip], all_ref.at[chip], keep.at[pair])
+
     for copy in fetches(0):
         copy.start()
-    hops = Hops(planes, slots, rows)
-    hello(wide_peers(width, me) + [{"blk": (hops.plane + k) % planes} for k in range(1, planes)])
+    peers = wide_peers(width, me)
+    if second:
+        own = cols // planes
+        loads = [
+            pltpu.make_async_copy(
+                wd_hbm.at[:, pl.ds((2 * b + side) * own, own)], wd.at[:, pl.ds(side * cols + b * own, own)],
+                load.at[b, side],
+            )
+            for b in range(planes)
+            for side in (0, 1)
+        ]
+        loads.append(pltpu.make_async_copy(first_hbm, before, load.at[planes, 0]))
+        for copy in loads:
+            copy.start()
+    else:
+        hops = Hops(planes, slots, rows)
+        peers = peers + [{"blk": (hops.plane + k) % planes} for k in range(1, planes)]
+    hello(peers)
     flow = Flow(me, g_ref, lambda who, part: buf.at[who // 2, who % 2, pl.ds(part * half, half)], half, send, recv)
-    pairs = width // 2
 
     def work(pair):
         for copy in fetches(pair):
@@ -989,30 +1168,33 @@
         if pair + 1 < pairs:
             for copy in fetches(pair + 1):
                 copy.start()
-        if pair >= 2:
-            for copy in stores(pair - 2):
-                copy.wait()
         chip = flip(me // 2, pair)
         slot = pair % 2
         grads = buf[chip].reshape(2 * rows, cols)
-
-        def inner(n, carry):
-            at = pl.ds(pl.multiple_of(n * step, step), step)
-            grad = lax.dot_general(
-                grads, wd[at, :], (((1,), (1,)), ((), ())), preferred_element_type=jnp.float32
-            ).reshape(2, rows, step)
-            outs[slot, 0, :, :, at] = (grad * ins[slot, 2, :, :, at].astype(jnp.float32)).astype(low)
-            outs[slot, 1, :, :, at] = (grad * ins[slot, 1, :, :, at].astype(jnp.float32)).astype(low)
-            return carry
-
-        lax.fori_loop(0, hidden // step, inner, 0)
-        for copy in stores(pair):
-            copy.start()
-        tall = min(256, hidden)
+        if second:
+            if pair >= 2:
+                for copy in stores(pair - 2):
+                    copy.wait()
+            old = before[chip].reshape(2 * rows, cols)
+            step = min(512, inner)
+
+            def units(n, carry):
+                at = pl.ds(pl.multiple_of(n * step, step), step)
+                grad = (nt(old, wd[at, :cols]) + nt(grads, wd[at, cols:])).reshape(2, rows, step)
+                outs[slot, 0, :, :, at] = (grad * ins[slot, 1, :, :, at].astype(jnp.float32)).astype(low)
+                outs[slot, 1, :, :, at] = (grad * ins[slot, 0, :, :, at].astype(jnp.float32)).astype(low)
+                return carry
+
+            lax.fori_loop(0, inner // step, units, 0)
+            for copy in stores(pair):
+                copy.start()
+        else:
+            keeps(pair).start()
+        tall = min(512, inner)
 
         def outer(n, carry):
             at = pl.ds(pl.multiple_of(n * tall, tall), tall)
-            act = ins[slot, 0, :, :, at].reshape(2 * rows, tall)
+            act = acts[slot, :, :, at].reshape(2 * rows, tall)
             term = lax.dot_general(act, grads, (((0,), (0,)), ((), ())), preferred_element_type=jnp.float32)
             if pair:
                 term = term + held[at, :]
@@ -1022,7 +1204,7 @@
                 down_ref[at, :] = term.astype(low)
             return carry
 
-        lax.fori_loop(0, hidden // tall, outer, 0)
+        lax.fori_loop(0, inner // tall, outer, 0)
 
     def pair_ready(k):
         for part in (0, 1):
@@ -1039,9 +1221,12 @@
             flow.go(None, k, k, 1)
     flow.go(None, 1, 1, 0)
     flow.go(None, 1, 1, 1)
-    hops.spread(c_ref, c_out, side_send, side_recv, True, True)
+    if second:
+        for copy in loads:
+            copy.wait()
+    else:
+        hops.spread(c_ref, c_out, side_send, side_recv, True, True)
     mine.wait()
-    weights.wait()
     pair_ready(0)
     work(0)
     if width == 8:
@@ -1072,51 +1257,88 @@
             pair_ready(k)
             work(k // 2)
     flow.finish()
-    for pair in (pairs - 2, pairs - 1):
-        for copy in stores(pair):
-            copy.wait()
-    hops.spread(c_ref, c_out, side_send, side_recv, True, False)
-
-
-def push(g, side_x, down_weight, act, one, two, width, slots, ident, name):
+    if second:
+        for pair in (pairs - 2, pairs - 1):
+            for copy in stores(pair):
+                copy.wait()
+    else:
+        for pair in range(pairs):
+            keeps(pair).wait()
+        hops.spread(c_ref, c_out, side_send, side_recv, True, False)
+
+
+def push(second, g, act, width, slots, ident, name, others):
     rows, cols = g.shape
-    hidden = down_weight.shape[0]
+    inner = act.shape[1]
     low, dma = g.dtype, pltpu.SemaphoreType.DMA
-    step = min(512, hidden)
-    planes = width // slots
-    anywhere = pl.BlockSpec(memory_space=pl.ANY)
-    saved = jax.ShapeDtypeStruct((rows * width, hidden), low)
+    planes, pairs = width // slots, width // 2
+    anywhere, vmem = pl.BlockSpec(memory_space=pl.ANY), pl.BlockSpec(memory_space=pltpu.VMEM)
+    blocks = (pairs, 2, rows, cols)
+    scratch = [
+        pltpu.VMEM(blocks, low), pltpu.VMEM((inner, cols), jnp.float32), pltpu.VMEM((2, 2, rows, inner), low),
+        dma, dma((width, 2)), dma((width, 2)), dma((2, 2)),
+    ]
+    shapes = [jax.ShapeDtypeStruct((inner, cols), low)]
+    if second:
+        saved = jax.ShapeDtypeStruct((rows * width, inner), low)
+        shapes += [saved, saved]
+        scratch += [
+            pltpu.VMEM((inner, 2 * cols), low), pltpu.VMEM(blocks, low), pltpu.VMEM((2, 2, 2, rows, inner), low),
+            pltpu.VMEM((2, 2, 2, rows, inner), low), dma((planes + 1, 2)), dma((2, 2, 2)), dma((2, 2, 2)),
+        ]
+    else:
+        shapes += [
+            jax.ShapeDtypeStruct(blocks, low),
+            jax.ShapeDtypeStruct((many_rows(planes, rows), others[0].shape[1]), low),
+        ]
+        scratch += [dma((pairs,)), dma((planes,)), dma((planes,))]
+    inputs = [g, act] + others
     return pl.pallas_call(
-        functools.partial(push_body, width, slots, step),
-        out_shape=[
-            jax.ShapeDtypeStruct((hidden, cols), low), saved, saved,
-            jax.ShapeDtypeStruct((many_rows(planes, rows), cols), low),
-        ],
-        in_specs=[anywhere] * 6,
-        out_specs=[pl.BlockSpec(memory_space=pltpu.VMEM)] + [anywhere] * 3,
-        scratch_shapes=[
-            pltpu.VMEM((width // 2, 2, rows, cols), low), pltpu.VMEM((hidden, cols), low),
-            pltpu.VMEM((hidden, cols), jnp.float32), pltpu.VMEM((2, 3, 2, rows, hidden), low),
-            pltpu.VMEM((2, 2, 2, rows, hidden), low),
-            dma, dma, dma((width, 2)), dma((width, 2)), dma((planes,)), dma((planes,)),
-            dma((2, 3, 2)), dma((2, 2, 2)),
-        ],
+        functools.partial(push_body, second, width, slots),
+        out_shape=shapes,
+        in_specs=[anywhere] * len(inputs),
+        out_specs=[vmem] + [anywhere] * (len(shapes) - 1),
+        scratch_shapes=scratch,
         cost_estimate=busy(10),
         compiler_params=pltpu.CompilerParams(collective_id=ident, has_side_effects=True, vmem_limit_bytes=VMEM_LIMIT),
         name=name,
-    )(g, side_x, down_weight, act, one, two)
-
-
-def pull_body(width, slots, step, chunk, gg_hbm, gu_hbm, wg_hbm, wu_hbm, h_hbm, out_ref, dw_hbm, gg, gu, wg, wu,
-              columns, tiles, load, fetch, store, *sum_refs):
+    )(*inputs)
+
+
+def pull_body(width, slots, step, chunk, gg_hbm, gu_hbm, wg_hbm, wu_hbm, h_hbm, c_ref, normed_ref, inv_ref, gain_ref,
+              out_ref, proj_ref, gain_out, du_hbm, gg, gu, wg, wu, columns, tiles, load, take, fetch, store, *sum_refs):
     me = lax.axis_index("wide")
     planes = width // slots
     rows, cols = out_ref.shape
-    hidden = wg.shape[1]
-    loads = local_copies([(wg_hbm, wg), (wu_hbm, wu), (gg_hbm, gg), (gu_hbm, gu)], load)
+    half = rows // 2
+    chunks = cols // chunk
+    loads = local_copies([(wg_hbm, wg), (wu_hbm, wu)], load)
     for copy in loads:
         copy.start()
-    chunks = cols // chunk
+
+    def where(k, first, count):
+        who = flip(me, k)
+        start = ((who % slots) * planes + who // slots) * rows + first
+        return pl.ds(pl.multiple_of(start, half), count)
+
+    def takes(k):
+        at = where(k, 0, rows)
+        return [
+            pltpu.make_async_copy(src.at[at], dst.at[at], take.at[k, i])
+            for i, (src, dst) in enumerate(((gg_hbm, gg), (gu_hbm, gu)))
+        ]
+
+    order = [7, 6, 3, 5, 2, 4, 1, 0] if width == 8 else [k ^ 1 for k in range(width)]
+    for k in order:
+        for copy in takes(k):
+            copy.start()
+    taken = []
+
+    def need(k):
+        if k not in taken:
+            taken.append(k)
+            for copy in takes(k):
+                copy.wait()
 
     def fetched(n):
         at = pl.ds(pl.multiple_of(n * chunk, chunk), chunk)
@@ -1124,15 +1346,18 @@
 
     def stored(n):
         at = pl.ds(pl.multiple_of(n * chunk, chunk), chunk)
-        return pltpu.make_async_copy(tiles.at[n % 2], dw_hbm.at[at], store.at[n % 2])
+        return [
+            pltpu.make_async_copy(tiles.at[n % 2, i], ref.at[at], store.at[n % 2, i])
+            for i, ref in enumerate((du_hbm,))
+        ]
 
     fetched(0).start()
     hello(wide_peers(width, me))
     sums = Sums(width, me, out_ref, sum_refs)
 
-    def produce(k, put, adds=()):
-        who = flip(me, k)
-        at_rows = pl.ds(pl.multiple_of(((who % slots) * planes + who // slots) * rows, rows), rows)
+    def produce(k, first, count, put, adds=()):
+        need(k)
+        at_rows = where(k, first, count)
 
         def tile(n, carry):
             at = pl.ds(pl.multiple_of(n * step, step), step)
@@ -1145,6 +1370,9 @@
         lax.fori_loop(0, cols // step, tile, 0)
 
     def grads(first, last):
+        for k in order:
+            need(k)
+
         def one_chunk(n, carry):
             fetched(n).wait()
 
@@ -1154,83 +1382,96 @@
 
             @pl.when(n >= 2)
             def _():
-                stored(n - 2).wait()
-
-            for i, ref in enumerate((gg, gu)):
-                tiles[n % 2, :, pl.ds(i * hidden, hidden)] = lax.dot_general(
+                for copy in stored(n - 2):
+                    copy.wait()
+
+            for i, ref in enumerate((gu,)):
+                tiles[n % 2, i] = lax.dot_general(
                     columns[n % 2], ref[...], (((0,), (0,)), ((), ())), preferred_element_type=jnp.float32
                 ).astype(jnp.bfloat16)
-            stored(n).start()
+            for copy in stored(n):
+                copy.start()
             return carry
 
         lax.fori_loop(first, last, one_chunk, 0)
-
-    def give(k):
-        produce(k + 1, sums.odd.at[k // 2])
-        sums.give(k)
-
-    def merge(k):
-        sums.got(k)
-        produce(k, sums.even.at[k // 2 - 1], (sums.from_twin.at[k // 2],))
 
     for copy in loads:
         copy.wait()
-    if width == 8:
-        give(6)
-        give(2)
-        give(4)
-        merge(6)
-        sums.relay(0).start()
-        sums.relay(1).start()
-        merge(2)
-        sums.far(2, 0).start()
-        merge(4)
-        sums.far(4, 1).start()
-        give(0)
-        middle = (3 * chunks) // 8
-        grads(0, middle)
-        sums.pass_on(2, 1)
-        sums.pass_on(4, 0)
-        grads(middle, chunks)
-    else:
-        for k in range(0, width, 2):
-            give(k)
-        for k in range(2, width, 2):
-            merge(k)
-            sums.far(k, 0).start()
-            sums.far(k, 1).start()
-        grads(0, chunks)
-    sums.got(0)
-    produce(0, out_ref, (sums.from_twin.at[0],))
-    sums.finish()
-    stored(chunks - 2).wait()
-    stored(chunks - 1).wait()
-
-
-def pull(grad_gate, grad_up, gate_weight, up_weight, gathered, width, slots, ident, name):
+    run_sums(width, sums, produce, grads, chunks)
+    gain_out[...] = jnp.zeros_like(gain_out)
+    few = 32
+
+    def norm(n, carry):
+        at = pl.ds(pl.multiple_of(n * few, few), few)
+        grad = out_ref[at, :] + c_ref[at, :].astype(jnp.float32)
+        out_ref[at, :] = grad
+        normed = normed_ref[at, :]
+        gain_out[...] = gain_out[...] + row_sums(grad * normed)
+        grad = grad * gain_ref[...]
+        mean = jnp.sum(grad * normed, axis=-1, keepdims=True) * (1.0 / cols)
+        proj_ref[at, :] = (inv_ref[at, :] * (grad - normed * mean)).astype(jnp.bfloat16)
+        return carry
+
+    lax.fori_loop(0, rows // few, norm, 0)
+    for copy in stored(chunks - 2) + stored(chunks - 1):
+        copy.wait()
+
+
+def pull(grad_gate, grad_up, gate_weight, up_weight, gathered, grad_out, normed, inverse, gain, width, slots, ident, name):
     count, cols = gathered.shape
-    hidden = gate_weight.shape[1]
+    inner = gate_weight.shape[1]
     rows = count // width
-    low, dma = gathered.dtype, pltpu.SemaphoreType.DMA
+    low, f32, dma = gathered.dtype, jnp.float32, pltpu.SemaphoreType.DMA
     chunk = 256
-    anywhere = pl.BlockSpec(memory_space=pl.ANY)
+    anywhere, vmem = pl.BlockSpec(memory_space=pl.ANY), pl.BlockSpec(memory_space=pltpu.VMEM)
     return pl.pallas_call(
         functools.partial(pull_body, width, slots, 1024, chunk),
         out_shape=[
-            jax.ShapeDtypeStruct((rows, cols), jnp.float32), jax.ShapeDtypeStruct((cols, 2 * hidden), low),
+            jax.ShapeDtypeStruct((rows, cols), f32), jax.ShapeDtypeStruct((rows, cols), low),
+            jax.ShapeDtypeStruct((8, cols), f32), jax.ShapeDtypeStruct((cols, inner), low),
         ],
-        in_specs=[anywhere] * 5,
-        out_specs=[pl.BlockSpec(memory_space=pltpu.VMEM), anywhere],
+        in_specs=[anywhere] * 5 + [vmem] * 4,
+        out_specs=[vmem] * 3 + [anywhere],
         scratch_shapes=[
-            pltpu.VMEM((count, hidden), low), pltpu.VMEM((count, hidden), low),
-            pltpu.VMEM((cols, hidden), low), pltpu.VMEM((cols, hidden), low),
-            pltpu.VMEM((2, count, chunk), low), pltpu.VMEM((2, chunk, 2 * hidden), low),
-            dma((4,)), dma((2,)), dma((2,)),
+            pltpu.VMEM((count, inner), low), pltpu.VMEM((count, inner), low),
+            pltpu.VMEM((cols, inner), low), pltpu.VMEM((cols, inner), low),
+            pltpu.VMEM((2, count, chunk), low), pltpu.VMEM((2, 1, chunk, inner), low),
+            dma((2,)), dma((width, 2)), dma((2,)), dma((2, 1)),
         ] + sum_scratch(width, rows, cols),
         cost_estimate=busy(10),
         compiler_params=pltpu.CompilerParams(collective_id=ident, has_side_effects=True, vmem_limit_bytes=VMEM_LIMIT),
         name=name,
-    )(grad_gate, grad_up, gate_weight, up_weight, gathered)
+    )(grad_gate, grad_up, gate_weight, up_weight, gathered, grad_out, normed, inverse, gain)
+
+
+def side_body(x_ref, p_ref, g_ref, m_ref, out_ref):
+    dims = (((0,), (0,)), ((), ()))
+    split = g_ref.shape[1]
+    out_ref[:, :split] = lax.dot_general(
+        x_ref[...], g_ref[...], dims, preferred_element_type=jnp.float32
+    ).astype(out_ref.dtype)
+    out_ref[:, split:] = lax.dot_general(
+        p_ref[...], m_ref[...], dims, preferred_element_type=jnp.float32
+    ).astype(out_ref.dtype)
+
+
+def side_grads(inputs, grad_proj, grads, mixed):
+    count, cols = inputs.shape
+    extent = grads.shape[1] + mixed.shape[1]
+    chunk = 256
+    return pl.pallas_call(
+        side_body,
+        grid=(cols // chunk,),
+        out_shape=jax.ShapeDtypeStruct((cols, extent), inputs.dtype),
+        in_specs=[
+            pl.BlockSpec((count, chunk), lambda n: (0, n)), pl.BlockSpec((count, chunk), lambda n: (0, n)),
+            pl.BlockSpec(grads.shape, lambda n: (0, 0)), pl.BlockSpec(mixed.shape, lambda n: (0, 0)),
+        ],
+        out_specs=pl.BlockSpec((chunk, extent), lambda n: (n, 0)),
+        compiler_params=pltpu.CompilerParams(vmem_limit_bytes=VMEM_LIMIT),
+        cost_estimate=busy(10),
+        name="side_grads",
+    )(inputs, grad_proj, grads, mixed)
 
 
 def local(
@@ -1260,26 +1501,30 @@
     plane, place = lax.axis_index("blk"), lax.axis_index("wide")
     after = lambda value, *others: lax.optimization_barrier((value,) + others)[0]
 
-    def over_blk(value, axis):
-        return lax.psum_scatter(
-            value.astype(low), "blk", scatter_dimension=axis, tiled=True
-        ).astype(f32)
+    def sum_blk(value, axis):
+        return lax.psum_scatter(value, "blk", scatter_dimension=axis, tiled=True)
 
     _, near_cotangent, mine = turn(
         turn_in_body, [tokens[0], cotangent[0]], [True, True, False], planes, slots, 1, "turn_in"
     )
-    qkv_rows = after(jnp.concatenate([query_weight, key_weight, value_weight], 1), mine)
-    w_qkv = lax.all_gather(qkv_rows, "blk", axis=0, tiled=True)
-    w_o = lax.all_gather(after(output_weight, w_qkv), "blk", axis=1, tiled=True)
+    w_qkv = after(jnp.concatenate([query_weight, key_weight, value_weight], 1), mine)
+    w_qkv = lax.all_gather(w_qkv, "blk", axis=0, tiled=True)
     gains = jnp.stack([query_gain, key_gain]).astype(f32)
     plane_lengths = lax.dynamic_slice_in_dim(lengths, plane * slots, slots, 0)
     segment, position = jax.vmap(lambda one: layout(one, span))(plane_lengths)
     begin = (jnp.arange(span, dtype=jnp.int32)[None] - position)[:, None, :]
     pairs, piece = piece_map(span, rows)
     order = sorted(pairs, key=lambda pair: pair[1])
-    position = jnp.concatenate([position[:, at : at + piece] for at, _ in order], 1)
-    cosine, sine = rope_tables(position.reshape(-1))
-    cosine, sine = cosine.reshape(slots, span, HD), sine.reshape(slots, span, HD)
+    index = np.concatenate([np.arange(at, at + piece) for at, _ in order])
+    starts = jnp.stack([plane_lengths[:, 0] * 0, plane_lengths[:, 0], plane_lengths[:, 0] + plane_lengths[:, 1]], 1)
+    cos_a, sin_a, cos_b, sin_b, sign = rope_tables(index, starts)
+    group = jnp.concatenate([segment[:, at : at + piece] for at, _ in order], 1)[..., None]
+    pick = lambda table: jnp.where(
+        group == 0, table[:, 0:1], jnp.where(group == 1, table[:, 1:2], table[:, 2:3])
+    )
+    cos_b, sin_b = pick(cos_b), pick(sin_b)
+    cosine = cos_a * cos_b + sin_a * sin_b
+    sine = (sin_a * cos_b - cos_a * sin_b) * sign
 
     inputs = gather(mine, width, slots, 2, "gather_tokens")
     pre = dot(inputs, w_qkv)
@@ -1293,44 +1538,50 @@
     gain_mix, gain_feed = both[0], both[1]
     inverse = lax.rsqrt(squares[: 2 * count // 128].reshape(2, count) / D + EPS)
     inv_cols = inverse.T.reshape(slots, span, 2)
+    w_o = lax.all_gather(after(output_weight, w_qkv), "blk", axis=1, tiled=True)
     pre_groups = pre.reshape(slots, span, 3 * share)
     queries, keys, values, mixed, logs = attend(
         pre_groups, inv_cols, gains, cosine, sine, begin, heads, rows
     )
     mixed = mixed.reshape(count, share)
-    projected = scatter([mixed], [w_o], width, slots, False, 4, "scatter_mixed")
-    proj_normed, proj_inv = rms_pair(projected)
-    hidden = mine.astype(f32) + proj_normed * gain_mix
-    reduced, gathered, activated, up_factor, gate_factor, grad_out = feed(
-        hidden.astype(low), near_cotangent, gate_weight, up_weight, down_weight, width, slots, 5, "feed"
-    )
-    grad_out = grad_out.astype(f32)
-    red_normed, red_inv = rms_pair(reduced)
-    block_output = (hidden + red_normed * gain_feed).astype(low)
-
-    feed_gain_part = jnp.sum(grad_out * red_normed, axis=0)
-    grad_reduced = norm_back(red_normed, red_inv, grad_out * gain_feed).astype(low)
-    down_part, grad_gate, grad_up, far_output = push(
-        grad_reduced, block_output, down_weight, activated, up_factor, gate_factor, width, slots, 7, "push"
-    )
-    down_grad = over_blk(down_part, 1)
-    hidden_part, inner_part = pull(
-        grad_gate, grad_up, gate_weight, up_weight, gathered, width, slots, 8, "pull"
-    )
-    grad_hidden = grad_out + hidden_part
-    inner_grad = over_blk(inner_part, 0)
-    mix_gain_part = jnp.sum(grad_hidden * proj_normed, axis=0)
-    grad_proj = norm_back(proj_normed, proj_inv, grad_hidden * gain_mix).astype(low)
+    hidden, hidden_low, proj_normed, proj_inv = scatter(
+        [mixed], [w_o], width, slots, False, 4, "scatter_mixed", "norm", (mine, gain_mix[None])
+    )
+    block_output, first_half, second_half, feed_gain_part, gathered, activated, up_factor, gate_factor, grad_out = feed(
+        hidden_low, near_cotangent, gate_weight, up_weight, down_weight, hidden, gain_feed[None], width, slots, 5,
+        "feed",
+    )
+    down_first, first_rows, far_output = push(
+        False, first_half, activated, width, slots, 6, "push_first", [block_output]
+    )
+    down_first = sum_blk(down_first, 1)
+    down_second, grad_gate, grad_up = push(
+        True, second_half, activated, width, slots, 7, "push_second",
+        [down_weight, up_factor, gate_factor, first_rows],
+    )
+    down_second = sum_blk(down_second, 1)
+    gate_part = contract_rows(gathered, grad_gate).astype(low)
+    gate_grad = sum_blk(gate_part, 0)
+    grad_hidden, grad_proj, mix_gain_part, up_part = pull(
+        after(grad_gate, gate_part, down_first), grad_up, gate_weight, up_weight, gathered, grad_out, proj_normed,
+        proj_inv, gain_mix[None], width, slots, 8, "pull",
+    )
+    up_grad = sum_blk(up_part, 0)
     grad_proj = gather(grad_proj, width, slots, 9, "gather_proj")
-    output_part = contract_rows(grad_proj, mixed).astype(low)
-    grad_proj = after(grad_proj, down_grad)
-    grad_mixed = contract_cols(grad_proj, w_o).astype(low).reshape(slots, span, share)
+    grad_mixed = contract_cols(after(grad_proj, down_first, down_second), w_o).astype(low).reshape(slots, span, share)
     scaled_q, scaled_k, grad_v, sums, parts = attend_back(
         queries, keys, values, grad_mixed, logs, pre_groups, inv_cols, gains, cosine, sine, begin,
         heads, rows,
     )
     means = jnp.sum(sums, axis=0).reshape(count, 2).T.reshape(-1, 128)
-    means = total(means, "wide", width, 10, "total_means").reshape(2, count) / D
+    local_gains = lax.dynamic_update_slice(
+        jnp.zeros((2, D), f32), jnp.sum(parts, axis=0), (0, place * share)
+    )
+    gain_parts = jnp.concatenate([local_gains, jnp.stack([mix_gain_part.sum(0), feed_gain_part.sum(0)])])
+    means = jnp.concatenate([means, gain_parts.reshape(-1, 128)])
+    means = total(after(means, gate_grad), "wide", width, 10, "total_means")
+    gain_parts = means[2 * count // 128 :]
+    means = means[: 2 * count // 128].reshape(2, count) / D
 
     def finish(scaled, index):
         normed = pre[:, index * share : (index + 1) * share] * inverse[index][:, None]
@@ -1338,19 +1589,20 @@
         return (inverse[index][:, None] * (scaled - normed * means[index][:, None])).astype(low)
 
     grads = jnp.concatenate([finish(scaled_q, 0), finish(scaled_k, 1), grad_v.reshape(count, share)], 1)
-    tokens_part = scatter([grads], [w_qkv], width, slots, True, 11, "scatter_tokens")
-    _, block_output, tokens_grad = turn(
-        turn_out_body, [after((grad_hidden + tokens_part).astype(low), inner_grad), far_output], [True, False, False],
-        planes, slots, 14, "turn_out",
-    )
-    qkv_part = contract_rows(inputs, grads).astype(low)
-    side_grad = over_blk(jnp.concatenate([qkv_part, output_part], 1), 0)
-
-    gain_parts = jnp.sum(parts, axis=0)
-    local_gains = lax.dynamic_update_slice(jnp.zeros((2, D), f32), gain_parts, (0, place * share))
-    sums = jnp.concatenate([local_gains, jnp.stack([mix_gain_part, feed_gain_part])])
-    sums = total(sums.reshape(-1, 128), "wide", width, 12, "total_gains")
-    sums = total(sums, "blk", planes, 13, "total_gains_blk").reshape(4, D)
+    side_part = side_grads(inputs, grad_proj, grads, mixed)
+    tokens_low = scatter(
+        [grads], [w_qkv], width, slots, True, 11, "scatter_tokens", "add", (grad_hidden,)
+    )
+    down_grad = jnp.concatenate([down_first, down_second], 1).astype(f32)
+    gate_grad, up_grad = gate_grad.astype(f32), up_grad.astype(f32)
+    tokens_low, down_grad, gate_grad, up_grad = lax.optimization_barrier((tokens_low, down_grad, gate_grad, up_grad))
+    _, block_output, tokens_grad, gain_sums = turn(
+        turn_out_body, [tokens_low, far_output], [True, False, False],
+        planes, slots, 14, "turn_out", gain_parts,
+    )
+    side_grad = sum_blk(side_part, 0).astype(f32)
+
+    sums = gain_sums.reshape(4, D)
     portion = D // (planes * width)
     sums = lax.dynamic_slice_in_dim(sums, (plane * width + place) * portion, portion, 1)
     return (
@@ -1363,8 +1615,8 @@
         sums[0],
         sums[1],
         sums[2],
-        inner_grad[:, : gate_weight.shape[1]],
-        inner_grad[:, gate_weight.shape[1] :],
+        gate_grad,
+        up_grad,
         down_grad,
         sums[3],
     )

time: 763 us -> 756 us (level)
  other arithmetic: 53.8 us -> 29.5 us
  Pallas kernels: 627 us -> 641 us
    pallas_call x1 -> x3, Pallas kernels: 62.5 us -> 90.8 us  [the longest x2 72.7 us: push(): pl.pallas_call(functools.partial(push_body, second, width, slots), out_sh...]
    pallas_call x4 -> x2, Pallas kernels: 34.9 us -> 17.9 us  [total(): pl.pallas_call(functools.partial(total_body, axis, width), out_shape=jax....]
    pallas_call x2, Pallas kernels: 117 us -> 104 us  [turn(): pl.pallas_call(functools.partial(body, planes, slots), out_shape=[shape(m...]
    reduce_sum x5 -> x3, other arithmetic: 12.1 us -> 0.74 us  [the longest x1 0.7 us: local(): jnp.sum(parts, axis=0)]
    dot_general x2 -> x1, matrix products: 19.3 us -> 16.9 us  [contract_rows(): lax.dot_general(left, right, (((0,), (0,)), ((), ())), preferred_element_...]
  transfers between devices with their start and end apart: 5 -> 7, of which waited for: 1 -> 1; matrix products, arithmetic and copies ran while one was open for 11% -> 9% of each run, Pallas kernels for 49% -> 54%
where the time goes in v3:
time: 756 us; the launch traced here: 745 us
  Pallas kernels  641 us (85%)
  matrix products  37.6 us (5%)
  other arithmetic  29.5 us (4%)
  between operations  15 us (2%)
  local copies, waits for them, and re-layouts  14.1 us (2%)
    pallas_call x2, Pallas kernels, scatter(): pl.pallas_call(functools.partial(scatter_body, width, slots, flat, len(le...  115 us
    pallas_call x2, Pallas kernels, turn(): pl.pallas_call(functools.partial(body, planes, slots), out_shape=[shape(m...  104 us
    pallas_call x1, Pallas kernels, feed(): pl.pallas_call(functools.partial(feed_body, width, slots, step), out_shap...  101 us
    pallas_call x2, Pallas kernels, gather(): pl.pallas_call(functools.partial(gather_body, width, slots, side), out_sh...  98.5 us
    pallas_call x2, Pallas kernels, push(): pl.pallas_call(functools.partial(push_body, second, width, slots), out_sh...  72.7 us
    pallas_call x1, Pallas kernels, pull(): pl.pallas_call(functools.partial(pull_body, width, slots, 1024, chunk), o...  69.4 us
    pallas_call x1, Pallas kernels, attend_back(): pl.pallas_call(functools.partial(attend_back_body, size), grid=(slots, he...  27 us
    pallas_call x1, Pallas kernels, side_grads(): pl.pallas_call(side_body, grid=(cols // chunk,), out_shape=jax.ShapeDtype...  18 us
  transfers between devices with their start and end apart: 7, of which 1 were waited for; matrix products, arithmetic and copies ran while one was open for 9% of the time, Pallas kernels for 54%

profile of v3, /device:TPU:8, one launch (start us, length us, event | category | flops | bytes accessed | tf_op | source)
XLA Modules:
  0.0 745.0 jit_solution(4549116940424885962)
XLA Ops:
  7.3 47.0 %turn_in.1 = (bf16[320,2048]{1,0:T(8,128)(2,1)}, bf16[320,2048]{1,0:T(8,128)(2,1)}, bf16[320,2048]{1,0:T(8,128)(2,1)}) custom-call(bf16[320,2048]{1,0:T(8,128)(2,1)} %bitcast.84, bf16[320,2048]{1,0:T(8,128)(2,1)} %bitcast.85), custom_call_target="tpu_custom_call" | custom-call | bytes 35000000 | tf_op jit(solution)/shard_map/turn_in/pallas_call | solution.py:684
  54.3 0.9 pad_maximum_fusion.1
  55.4 50.4 %gather_tokens.1.x_ref = bf16[2560,2048]{1,0:T(8,128)(2,1)} custom-call(bf16[320,2048]{1,0:T(8,128)(2,1)} %get-tuple-element.60.refs_0_.refs_2_), custom_call_target="tpu_custom_call" | custom-call | bytes 35000000 | tf_op jit(solution)/shard_map/gather_tokens/pallas_call | solution.py:349
  106.4 0.6 maximum_convert_fusion.1.gain_ref
  107.2 0.7 compare_select_fusion.1.begin_ref
  108.0 2.5 subtract_multiply_fusion
  110.4 7.0 all-gather.3.cloned.1.call-done.refs_1_
  117.5 12.1 %fusion.9 = f32[2560,768]{1,0:T(8,128)S(1)} fusion(bf16[2560,2048]{1,0:T(8,128)(2,1)} %gather_tokens.1.x_ref, bf16[2048,768]{1,0:T(8,128)(2,1)} %all-gather.3.cloned.1.call-done.refs_1_), kind=kOutput, calls=%fused_computation.63 | convolution fusion | flops 8053063680 | bytes 21495808 | tf_op jit(solution)/shard_map/dot_general | solution.py:55
  129.6 3.1 copy-done.2
  132.7 0.7 multiply_reduce_fusion.1
  133.6 0.6 pad_maximum_fusion.3.x_ref
  134.2 8.3 %total_squares.1 = f32[72,128]{1,0:T(8,128)} custom-call(f32[72,128]{1,0:T(8,128)} %pad_maximum_fusion.3.x_ref), custom_call_target="tpu_custom_call" | custom-call | bytes 24500000 | tf_op jit(solution)/shard_map/total_squares/pallas_call | solution.py:471
  142.5 0.7 add_rsqrt_fusion
  143.2 1.5 copy.33
  144.7 17.7 %attend.1 = (bf16[2,1280,256]{2,1,0:T(8,128)(2,1)}, bf16[2,1280,256]{2,1,0:T(8,128)(2,1)}, bf16[2,1280,256]{2,1,0:T(8,128)(2,1)}, bf16[2,1280,256]{2,1,0:T(8,128)(2,1)}, f32[2,2,1,1280]{3,2,1,0:T(1,128)}) custom-call(f32[2,1280,768]{2,1,0:T(8,128)} %bitcast.73, f32[2,1280,768]{2,1,0:T(8,128)} %bitcast.74, f32[2,1280,768]{2,1,0:T(8,128)} %bitcast.75, ...), custom_call_target="tpu_custom_call" | custom-call | bytes 17500000 | tf_op jit(solution)/shard_map/attend/pallas_call | solution.py:767
  162.4 1.3 fusion.7
  163.7 56.9 %scatter_mixed.1 = (f32[320,2048]{1,0:T(8,128)}, bf16[320,2048]{1,0:T(8,128)(2,1)}, f32[320,2048]{1,0:T(8,128)}, f32[320,1]{1,0:T(8,128)}) custom-call(bf16[2560,256]{1,0:T(8,128)(2,1)} %bitcast.81, bf16[256,2048]{1,0:T(8,128)(2,1)} %all-gather.5.cloned.1.call-done.refs_1_, bf16[320,2048]{1,0:T(8,128)(2,1)} %get-tuple-element.60.refs_0_.refs_2_, ...), custom_call_target="tpu_custom_call" | custom-call | bytes 35000000 | tf_op jit(solution)/shard_map/scatter_mixed/pallas_call | solution.py:433
  220.7 100.9 %feed.1 = (bf16[320,2048]{1,0:T(8,128)(2,1)}, bf16[320,1024]{1,0:T(8,128)(2,1)}, bf16[320,1024]{1,0:T(8,128)(2,1)}, f32[8,2048]{1,0:T(8,128)}, bf16[2560,2048]{1...) custom-call(bf16[320,2048]{1,0:T(8,128)(2,1)} %get-tuple-element.67., ...), custom_call_target="tpu_custom_call" | custom-call | bytes 315000000 | tf_op jit(solution)/shard_map/feed/pallas_call | solution.py:1075
  321.6 33.1 %push_first.1 = (bf16[1024,1024]{1,0:T(8,128)(2,1)}, bf16[4,2,320,1024]{3,2,1,0:T(8,128)(2,1)}, bf16[320,2048]{1,0:T(8,128)(2,1)}) custom-call(bf16[320,1024]{1,0:T(8,128)(2,1)} %get-tuple-element.74.refs_0_, bf16[2560,1024]{1,0:T(8,128)(2,1)} %get-tuple-element.71.refs_1_, bf16[320,2048]{1,0:T(8,128)(2,1)} %get-tuple-element.75.refs_2_), custom_call_target="tpu_custom_call" | custom-call | bytes 35000000 | tf_op jit(solution)/shard_map/push_first/pallas_call | solution.py:1296
  354.7 39.7 %push_second.1 = (bf16[1024,1024]{1,0:T(8,128)(2,1)}, bf16[2560,1024]{1,0:T(8,128)(2,1)}, bf16[2560,1024]{1,0:T(8,128)(2,1)}) custom-call(bf16[320,1024]{1,0:T(8,128)(2,1)} %get-tuple-element.70.refs_0_, bf16[2560,1024]{1,0:T(8,128)(2,1)} %get-tuple-element.71.refs_1_, bf16[1024,2048]{1,0:T(8,128)(2,1)} %refs_2_.1, ...), custom_call_target="tpu_custom_call" | custom-call | bytes 35000000 | tf_op jit(solution)/shard_map/push_second/pallas_call | solution.py:1296
  394.5 16.9 %convolution_convert_fusion.1 = bf16[2048,1024]{1,0:T(8,128)(2,1)} fusion(bf16[2560,2048]{1,0:T(8,128)(2,1)} %get-tuple-element.78.h_hbm, bf16[2560,1024]{1,0:T(8,128)(2,1)} %get-tuple-element.80.gg_hbm), kind=kOutput, calls=%fused_computation.2 | convolution fusion | flops 10739515392 | bytes 19922944 | tf_op jit(solution)/shard_map/dot_general | solution.py:59
  411.4 69.4 %pull.1 = (f32[320,2048]{1,0:T(8,128)}, bf16[320,2048]{1,0:T(8,128)(2,1)}, f32[8,2048]{1,0:T(8,128)}, bf16[2048,1024]{1,0:T(8,128)(2,1)}) custom-call(bf16[2560,1024]{1,0:T(8,128)(2,1)} %get-tuple-element.80.gg_hbm, bf16[2560,1024]{1,0:T(8,128)(2,1)} %get-tuple-element.81.gu_hbm, bf16[2048,1024]{1,0:T(8,128)(2,1)} %wg_hbm.3, bf16[2048,1024]{1,0:T(8,128)(2,1)} %wu_hbm.3, ...), custom_call_target="tpu_custom_call" | custom-call | bytes 35000000 | tf_op jit(solution)/shard_map/pull/pallas_call | solution.py:1427
  480.9 0.7 copy-done.16
  481.7 48.1 %gather_proj.1.p_ref = bf16[2560,2048]{1,0:T(8,128)(2,1)} custom-call(bf16[320,2048]{1,0:T(8,128)(2,1)} %get-tuple-element.85.refs_0_), custom_call_target="tpu_custom_call" | custom-call | bytes 35000000 | tf_op jit(solution)/shard_map/gather_proj/pallas_call | solution.py:349
  529.9 8.7 %convolution_convert_fusion = bf16[2560,256]{1,0:T(8,128)(2,1)} fusion(bf16[2560,2048]{1,0:T(8,128)(2,1)} %gather_proj.1.p_ref, bf16[256,2048]{1,0:T(8,128)(2,1)S(1)} %copy-done.6), kind=kOutput, calls=%fused_computation.1 | convolution fusion | flops 2685009920 | bytes 12845056 | tf_op jit(solution)/shard_map/dot_general | solution.py:65
  538.5 27.0 %attend_back.1 = (f32[2,1280,256]{2,1,0:T(8,128)}, f32[2,1280,256]{2,1,0:T(8,128)}, bf16[2,1280,256]{2,1,0:T(8,128)(2,1)}, f32[2,2,1280,2]{3,2,1,0:T(8,128)}, f32[2,2,256]{2,1,0:T(2,128)}) custom-call(bf16[2,1280,256]{2,1,0:T(8,128)(2,1)} %get-tuple-element.62.q_ref, bf16[2,1280,256]{2,1,0:T(8,128)(2,1)} %get-tuple-element.63.k_ref, ...), custom_call_target="tpu_custom_call" | custom-call | bytes 17500000 | tf_op jit(solution)/shard_map/attend_back/pallas_call | solution.py:830
  565.5 0.7 reduce_sum.57
  566.3 2.1 reduce_sum.56
  568.9 0.6 pad_maximum_fusion.2.x_ref
  569.5 9.6 %total_means.1 = f32[104,128]{1,0:T(8,128)} custom-call(f32[104,128]{1,0:T(8,128)} %pad_maximum_fusion.2.x_ref), custom_call_target="tpu_custom_call" | custom-call | bytes 24500000 | tf_op jit(solution)/shard_map/total_means/pallas_call | solution.py:471
  579.1 0.7 slice_multiply_fusion
  579.9 5.5 fusion.3
  585.3 2.0 pad_maximum_fusion.refs_0_.g_ref
  587.4 18.0 %side_grads.1 = bf16[2048,1024]{1,0:T(8,128)(2,1)} custom-call(bf16[2560,2048]{1,0:T(8,128)(2,1)} %gather_tokens.1.x_ref, bf16[2560,2048]{1,0:T(8,128)(2,1)} %gather_proj.1.p_ref, bf16[2560,768]{1,0:T(8,128)(2,1)} %pad_maximum_fusion.refs_0_.g_ref, bf16[2560,256]{1,0:T(8,128)(2,1)} %bitcast.82), custom_call_target="tpu_custom_call" | custom-call | bytes 35000000 | tf_op jit(solution)/shard_map/side_grads/pallas_call | solution.py:1462
  605.4 1.0 copy-done.10
  606.6 1.6 maximum_convert_fusion
  608.2 0.6 slice.186.v_ref
  608.8 1.6 convert_element_type.79
  610.4 58.3 %scatter_tokens.1.x_ref = bf16[320,2048]{1,0:T(8,128)(2,1)} custom-call(bf16[2560,768]{1,0:T(8,128)(2,1)} %pad_maximum_fusion.refs_0_.g_ref, bf16[2048,768]{1,0:T(8,128)(2,1)} %all-gather.3.cloned.1.call-done.refs_1_, f32[320,2048]{1,0:T(8,128)} %get-tuple-element.97.refs_2_), custom_call_target="tpu_custom_call" | custom-call | bytes 35000000 | tf_op jit(solution)/shard_map/scatter_tokens/pallas_call | solution.py:433
  668.7 2.8 convert_element_type.80
  671.5 57.0 %turn_out.1 = (bf16[320,2048]{1,0:T(8,128)(2,1)}, bf16[320,2048]{1,0:T(8,128)(2,1)}, bf16[320,2048]{1,0:T(8,128)(2,1)}, f32[64,128]{1,0:T(8,128)}) custom-call(bf16[320,2048]{1,0:T(8,128)(2,1)} %scatter_tokens.1.x_ref, bf16[320,2048]{1,0:T(8,128)(2,1)} %get-tuple-element.100.far_c, f32[64,128]{1,0:T(8,128)} %slice.186.v_ref), custom_call_target="tpu_custom_call" | custom-call | bytes 35000000 | tf_op jit(solution)/shard_map/turn_out/pallas_call | solution.py:684
  728.5 0.8 reshape.481
  729.4 0.5 slice_bitcast_fusion.11
  729.9 3.1 bitcast_convert_fusion
  733.0 1.5 convert_element_type.83
  734.7 1.0 copy.35
  735.7 1.2 fusion.6
  736.8 1.1 copy.43
  (100 shorter events, 2.1 us)
Async XLA Ops:
  7.2 98.8 %copy-start = (s32[8,3]{0,1:T(4,128)S(1)}, s32[8,3]{0,1:T(4,128)}, u32[]{:S(2)}) copy-start(s32[8,3]{0,1:T(4,128)} %param.19) | copy-start | bytes 292
  7.2 47.1 %copy-start.12 = (bf16[512,256]{1,0:T(8,128)(2,1)S(1)}, bf16[512,256]{1,0:T(8,128)(2,1)}, u32[]{:S(2)}) copy-start(bf16[512,256]{1,0:T(8,128)(2,1)} %param.22) | copy-start | bytes 786436
  7.2 47.1 %copy-start.13 = (bf16[512,256]{1,0:T(8,128)(2,1)S(1)}, bf16[512,256]{1,0:T(8,128)(2,1)}, u32[]{:S(2)}) copy-start(bf16[512,256]{1,0:T(8,128)(2,1)} %param.21) | copy-start | bytes 786436
  7.2 47.1 %copy-start.14 = (bf16[512,256]{1,0:T(8,128)(2,1)S(1)}, bf16[512,256]{1,0:T(8,128)(2,1)}, u32[]{:S(2)}) copy-start(bf16[512,256]{1,0:T(8,128)(2,1)} %param.20) | copy-start | bytes 786436
  7.2 110.2 %all-gather.3.cloned.1.call-start = ((), (), s32[]{:S(2)}) async-start(), calls=%async_computation.5 | async-start | bytes 3932160 | tf_op jit(solution)/shard_map/all_gather | solution.py:1511
  55.3 108.5 %all-gather.5.cloned.1.call-start = ((), (), s32[]{:S(2)}) async-start(), calls=%async_computation.6 | async-start | bytes 1310720 | tf_op jit(solution)/shard_map/all_gather | solution.py:1541
  55.3 50.5 %copy-start.20 = (bf16[256]{0:T(256)(128)(2,1)S(1)}, bf16[256]{0:T(256)(128)(2,1)}, u32[]{:S(2)}) copy-start(bf16[256]{0:T(256)(128)(2,1)} %param.24) | copy-start | bytes 1540
  55.3 50.6 %copy-start.21 = (bf16[256]{0:T(256)(128)(2,1)S(1)}, bf16[256]{0:T(256)(128)(2,1)}, u32[]{:S(2)}) copy-start(bf16[256]{0:T(256)(128)(2,1)} %param.25) | copy-start | bytes 1540
  55.4 50.6 %copy-start.22 = (bf16[256]{0:T(256)(128)(2,1)S(1)}, bf16[256]{0:T(256)(128)(2,1)}, u32[]{:S(2)}) copy-start(bf16[256]{0:T(256)(128)(2,1)} %param.26) | copy-start | bytes 1540
  55.4 50.6 %copy-start.23 = (bf16[256]{0:T(256)(128)(2,1)S(1)}, bf16[256]{0:T(256)(128)(2,1)}, u32[]{:S(2)}) copy-start(bf16[256]{0:T(256)(128)(2,1)} %param.30) | copy-start | bytes 1540
  55.4 51.7 %copy-start.19 = (f32[128]{0:T(128)S(1)}, f32[128]{0:T(128)}, u32[]{:S(2)}) copy-start(f32[128]{0:T(128)} %constant.45.clone) | copy-start | bytes 1540
  55.4 52.5 %copy-start.8 = (f32[1280,128]{1,0:T(8,128)S(1)}, f32[1280,128]{1,0:T(8,128)}, u32[]{:S(2)}) copy-start(f32[1280,128]{1,0:T(8,128)} %constant.44.clone) | copy-start | bytes 1966084
  55.4 52.5 %copy-start.9 = (f32[1280,128]{1,0:T(8,128)S(1)}, f32[1280,128]{1,0:T(8,128)}, u32[]{:S(2)}) copy-start(f32[1280,128]{1,0:T(8,128)} %constant.15.clone) | copy-start | bytes 1966084
  55.4 52.5 %copy-start.18 = (f32[128]{0:T(128)S(1)}, f32[128]{0:T(128)}, u32[]{:S(2)}) copy-start(f32[128]{0:T(128)} %constant.46.clone) | copy-start | bytes 1540
  117.5 293.9 %reduce-scatter.6.cloned.1.call-start = ((), (), s32[]{:S(2)}) async-start(), calls=%async_computation.7 | async-start | bytes 2621440 | tf_op jit(solution)/shard_map/reduce_scatter | solution.py:1505
  129.6 3.1 copy-start.2
  354.7 175.1 %reduce-scatter.8.cloned.1.call-start = ((), (), s32[]{:S(2)}) async-start(), calls=%async_computation.8 | async-start | bytes 2621440 | tf_op jit(solution)/shard_map/reduce_scatter | solution.py:1505
  394.4 175.1 %reduce-scatter.10.cloned.1.call-start = ((), (), s32[]{:S(2)}) async-start(), calls=%async_computation.9 | async-start | bytes 5242880 | tf_op jit(solution)/shard_map/reduce_scatter | solution.py:1505
  411.4 257.4 %reduce-scatter.12.cloned.1.call-start = ((), (), s32[]{:S(2)}) async-start(), calls=%async_computation.10 | async-start | bytes 5242880 | tf_op jit(solution)/shard_map/reduce_scatter | solution.py:1505
  480.8 0.8 copy-start.16
  480.9 252.2 %reduce-scatter.14.cloned.1.call-start = ((), (), s32[]{:S(2)}) async-start(), calls=%async_computation.11 | async-start | bytes 5242880 | tf_op jit(solution)/shard_map/reduce_scatter | solution.py:1505
  481.7 48.1 %copy-start.17 = (f32[8,2048]{1,0:T(8,128)S(1)}, f32[8,2048]{1,0:T(8,128)}, u32[]{:S(2)}) copy-start(f32[8,2048]{1,0:T(8,128)} %get-tuple-element.92) | copy-start | bytes 196612
  481.7 48.2 %copy-start.6 = (bf16[256,2048]{1,0:T(8,128)(2,1)S(1)}, bf16[256,2048]{1,0:T(8,128)(2,1)}, u32[]{:S(2)}) copy-start(bf16[256,2048]{1,0:T(8,128)(2,1)} %all-gather.5.cloned.1.call-done.refs_1_) | copy-start | bytes 3145732
  579.8 5.5 copy-start.5
  605.4 1.0 copy-start.10
  605.4 1.2 copy-start.11
  605.4 2.8 copy-start.15
  605.4 3.4 copy-start.7
  733.0 2.6 copy-start.3
  734.6 2.2 copy-start.4
  734.7 3.2 copy-start.1
Sparse Core Ops, SparseCore 0:
  55.4 62.0 all-gather.2
  119.0 28.8 all-gather.4
  354.8 40.5 reduce-scatter.5
  397.7 43.1 reduce-scatter.7
  443.1 78.3 reduce-scatter.9
  523.7 77.2 reduce-scatter.11
  605.5 93.2 reduce-scatter.13

commit v4 on v3

--- a/solution.py
+++ b/solution.py
@@ -251,112 +251,141 @@
     return [pltpu.make_async_copy(src, dst, sem.at[i]) for i, (src, dst) in enumerate(pairs)]
 
 
-def gather_body(width, slots, side, *refs):
-    if side is None:
+def gather_body(width, slots, weights, *refs):
+    if weights:
+        x_ref, w_ref, lower_ref, upper_ref, out_ref, w_out, here, send, recv, keep, w_send, w_recv = refs
+    else:
         x_ref, out_ref, here, send, recv = refs
-    else:
-        x_ref, side_ref, out_ref, side_out, here, send, recv, side_send, side_recv = refs
     me = lax.axis_index("wide")
+    planes = width // slots
     rows = x_ref.shape[0]
     half = rows // 2
-    evens = list(range(2, width, 2))
-    peers = [{"wide": flip(me, k)} for k in [1] + evens]
-    if side is not None:
-        hops = Hops(width // slots, slots, rows)
-        peers = peers + [{"blk": (hops.plane + k) % hops.planes} for k in range(1, hops.planes)]
+    peers = wide_peers(width, me)
+    if weights:
+        plane = lax.axis_index("blk")
+        extent = w_ref.shape[0]
+        peers = peers + [{"blk": (plane + k) % planes} for k in range(1, planes)]
+
+        def shard(which):
+            return w_out.at[pl.ds(pl.multiple_of(which * extent, extent), extent)]
+
+        def pass_on(step, far):
+            way = 0 if step > 0 else 1
+            origin = plane - step * far
+            source = shard(origin) if far > 1 else (lower_ref, upper_ref)[way]
+            return pltpu.make_async_remote_copy(
+                src_ref=source, dst_ref=shard(origin), send_sem=w_send.at[way, far], recv_sem=w_recv.at[way, far + 1],
+                device_id={"blk": plane + step}, device_id_type=MESH,
+            )
+
+        def between(step, far, action):
+            first, last = plane - step * far, plane + step
+            fits = (first >= 0) & (first < planes) & (last >= 0) & (last < planes)
+            pl.when(fits)(action)
+
+        def landed(step, far):
+            way = 0 if step > 0 else 1
+            block = shard(plane - step * far)
+            copy = pltpu.make_async_copy(block, block, w_recv.at[way, far])
+            beyond(plane, planes, -step * far, copy.wait)
+
+        keeps = [
+            (0, pltpu.make_async_copy(w_ref, shard(plane), keep.at[0])),
+            (-1, pltpu.make_async_copy(lower_ref, shard(plane - 1), keep.at[1])),
+            (1, pltpu.make_async_copy(upper_ref, shard(plane + 1), keep.at[2])),
+        ]
     hello(peers)
-    if side is not None:
-        job = hops.join if side == "join" else hops.spread
-        job(side_ref, side_out, side_send, side_recv, True, True)
-
-    def spot(who, first, count):
-        base = ((who % slots) * (width // slots) + who // slots) * rows
-        return out_ref.at[pl.ds(pl.multiple_of(base + first, half), count)]
-
-    def move(origin, target, k, part):
-        if origin is None:
-            source = x_ref.at[pl.ds(part * half, half)]
-        else:
-            source = spot(flip(me, origin), part * half, half)
-        return pltpu.make_async_remote_copy(
-            src_ref=source,
-            dst_ref=spot(flip(flip(me, target), k), part * half, half),
-            send_sem=send.at[k, part],
-            recv_sem=recv.at[k, part],
-            device_id={"wide": flip(me, target)},
-            device_id_type=MESH,
-        )
-
-    def arrived(k, part):
-        block = spot(flip(me, k), part * half, half)
-        pltpu.make_async_copy(block, block, recv.at[k, part]).wait()
-
-    moves = []
-
-    def go(origin, target, k, part):
-        copy = move(origin, target, k, part)
+    if weights:
+        for step in (1, -1):
+            between(step, 1, lambda step=step: pass_on(step, 1).start())
+
+    def spot(who, part):
+        base = ((who % slots) * planes + who // slots) * rows + part * half
+        return out_ref.at[pl.ds(pl.multiple_of(base, half), half)]
+
+    flow = Flow(me, x_ref, spot, half, send, recv)
+    mine = [
+        pltpu.make_async_copy(x_ref.at[pl.ds(part * half, half)], spot(me, part), here.at[part]) for part in (0, 1)
+    ]
+    for copy in mine:
         copy.start()
-        moves.append(copy)
-
-    mine = pltpu.make_async_copy(x_ref, spot(me, 0, rows), here)
-    mine.start()
+
+    def relay_weights(far):
+        if weights and far < planes:
+            for step in (1, -1):
+                landed(step, far)
+                between(step, far, lambda step=step: pass_on(step, far).start())
+
     if width == 8:
-        go(None, 2, 2, 0)
-        go(None, 4, 4, 1)
-        go(None, 2, 2, 1)
-        go(None, 4, 4, 0)
-        go(None, 1, 1, 0)
-        go(None, 1, 1, 1)
-        arrived(2, 0)
-        go(2, 4, 6, 0)
-        go(2, 1, 3, 0)
-        arrived(4, 1)
-        go(4, 2, 6, 1)
-        go(4, 1, 5, 1)
+        flow.go(None, 2, 2, 0)
+        flow.go(None, 4, 4, 1)
+        flow.go(None, 2, 2, 1)
+        flow.go(None, 4, 4, 0)
+        flow.go(None, 1, 1, 0)
+        flow.go(None, 1, 1, 1)
+        if weights:
+            for step, copy in keeps:
+                beyond(plane, planes, step, copy.start)
+        flow.arrived(2, 0)
+        flow.go(2, 4, 6, 0)
+        flow.go(2, 1, 3, 0)
+        flow.arrived(4, 1)
+        flow.go(4, 2, 6, 1)
+        flow.go(4, 1, 5, 1)
+        relay_weights(2)
         order = [(2, 1), (4, 0), (6, 0), (6, 1)]
     else:
-        for k in evens:
-            go(None, k, k, 0)
-            go(None, k, k, 1)
-        go(None, 1, 1, 0)
-        go(None, 1, 1, 1)
-        order = [(k, part) for k in evens for part in (0, 1)]
+        for k in range(2, width, 2):
+            flow.go(None, k, k, 0)
+            flow.go(None, k, k, 1)
+        flow.go(None, 1, 1, 0)
+        flow.go(None, 1, 1, 1)
+        if weights:
+            for step, copy in keeps:
+                beyond(plane, planes, step, copy.start)
+        relay_weights(2)
+        order = [(k, part) for k in range(2, width, 2) for part in (0, 1)]
     for k, part in order:
-        arrived(k, part)
-        go(k, 1, k + 1, part)
+        flow.arrived(k, part)
+        flow.go(k, 1, k + 1, part)
+    for far in range(3, planes):
+        relay_weights(far)
     for k in range(1, width, 2):
         for part in (0, 1):
-            arrived(k, part)
-    for copy in moves:
-        copy.wait_send()
-    mine.wait()
-    if side is not None:
-        job(side_ref, side_out, side_send, side_recv, True, False)
-
-
-def gather(x, width, slots, ident, name, side=None, side_x=None):
+            flow.arrived(k, part)
+    flow.finish()
+    for copy in mine:
+        copy.wait()
+    if weights:
+        for step, copy in keeps:
+            beyond(plane, planes, step, copy.wait)
+        for far in range(1, planes - 1):
+            for step in (1, -1):
+                between(step, far, lambda step=step, far=far: pass_on(step, far).wait_send())
+
+
+def gather(x, width, slots, ident, name, weights=()):
     rows, cols = x.shape
     planes = width // slots
     dma = pltpu.SemaphoreType.DMA
     shapes = [jax.ShapeDtypeStruct((rows * width, cols), x.dtype)]
-    scratch = [dma, dma((width, 2)), dma((width, 2))]
-    inputs = [x]
-    if side is not None:
-        inputs.append(side_x)
-        extent = rows if side == "join" else many_rows(planes, rows)
-        shapes.append(jax.ShapeDtypeStruct((extent, cols), side_x.dtype))
-        scratch += [dma((planes,)), dma((planes,))]
+    scratch = [dma((2,)), dma((width, 2)), dma((width, 2))]
+    if weights:
+        extent, share = weights[0].shape
+        shapes.append(jax.ShapeDtypeStruct((planes * extent, share), x.dtype))
+        scratch += [dma((3,)), dma((2, planes + 1)), dma((2, planes + 1))]
+    anywhere = pl.BlockSpec(memory_space=pl.ANY)
     outs = pl.pallas_call(
-        functools.partial(gather_body, width, slots, side),
+        functools.partial(gather_body, width, slots, bool(weights)),
         out_shape=shapes,
-        in_specs=[pl.BlockSpec(memory_space=pl.ANY)] * len(inputs),
-        out_specs=[pl.BlockSpec(memory_space=pl.ANY)] * len(shapes),
+        in_specs=[anywhere] * (1 + len(weights)),
+        out_specs=[anywhere] * len(shapes),
         scratch_shapes=scratch,
         cost_estimate=busy(10),
         compiler_params=pltpu.CompilerParams(collective_id=ident, has_side_effects=True, vmem_limit_bytes=VMEM_LIMIT),
         name=name,
-    )(*inputs)
-    return outs[0] if side is None else outs
+    )(x, *weights)
+    return outs if weights else outs[0]
 
 
 def scatter_body(width, slots, flat, count, step, finish, *refs):
@@ -625,15 +654,36 @@
     pl.semaphore_wait(barrier, len(peers))
 
 
-def turn_in_body(planes, slots, x_ref, c_ref, near_x, near_c, out_ref, *sems):
+def beyond(plane, planes, step, action):
+    pl.when((plane + step >= 0) & (plane + step < planes))(action)
+
+
+def turn_in_body(planes, slots, x_ref, c_ref, w_ref, near_x, near_c, out_ref, lower_ref, upper_ref, *sems):
     hops = Hops(planes, slots, x_ref.shape[0])
     hello(hops.peers())
+    w_send, w_recv = sems[6:]
+
+    def lend(step):
+        way = 0 if step > 0 else 1
+        return hops.remote(
+            w_ref, (lower_ref, upper_ref)[way], w_send.at[way], w_recv.at[way], {"blk": hops.plane + step}
+        )
+
+    for step in (1, -1):
+        beyond(hops.plane, planes, step, lambda step=step: lend(step).start())
     hops.spread(x_ref, near_x, sems[0], sems[1], False, True)
     ready = hops.arrival(x_ref, near_x, sems[0], sems[1], False)
     hops.join(near_x, out_ref, sems[2], sems[3], True, True, ready)
     hops.sent(x_ref, near_x, sems[0], False)
     hops.spread(c_ref, near_c, sems[4], sems[5], False, True)
     hops.spread(c_ref, near_c, sems[4], sems[5], False, False)
+    for way, step in ((0, 1), (1, -1)):
+        block = (lower_ref, upper_ref)[way]
+        beyond(hops.plane, planes, step, lambda step=step: lend(step).wait_send())
+        beyond(
+            hops.plane, planes, -step,
+            lambda block=block, way=way: pltpu.make_async_copy(block, block, w_recv.at[way]).wait(),
+        )
     hops.join(near_x, out_ref, sems[2], sems[3], True, False)
 
 
@@ -671,26 +721,40 @@
     return planes * (rows // count)
 
 
-def turn(body, inputs, outputs, planes, slots, ident, name, extra=None):
-    rows, cols = inputs[0].shape
-    low = inputs[0].dtype
-    dma = pltpu.SemaphoreType.DMA
-    shape = lambda many: jax.ShapeDtypeStruct((many_rows(planes, rows) if many else rows, cols), low)
-    anywhere, vmem = pl.BlockSpec(memory_space=pl.ANY), pl.BlockSpec(memory_space=pltpu.VMEM)
-    more = [] if extra is None else [extra]
-    scratch = [dma((planes,))] * 6
-    for value in more:
-        scratch += [pltpu.VMEM((planes - 1,) + value.shape, value.dtype), dma((planes - 1,)), dma((planes - 1,))]
+def turn_in(x, side, weight, planes, slots, ident, name):
+    rows, cols = x.shape
+    low, dma = x.dtype, pltpu.SemaphoreType.DMA
+    anywhere = pl.BlockSpec(memory_space=pl.ANY)
+    many, one = (jax.ShapeDtypeStruct((extent, cols), low) for extent in (many_rows(planes, rows), rows))
+    piece = jax.ShapeDtypeStruct(weight.shape, low)
     return pl.pallas_call(
-        functools.partial(body, planes, slots),
-        out_shape=[shape(many) for many in outputs] + [jax.ShapeDtypeStruct(v.shape, v.dtype) for v in more],
-        in_specs=[anywhere] * len(inputs) + [vmem] * len(more),
-        out_specs=[anywhere] * len(outputs) + [vmem] * len(more),
-        scratch_shapes=scratch,
+        functools.partial(turn_in_body, planes, slots),
+        out_shape=[many, many, one, piece, piece],
+        in_specs=[anywhere] * 3,
+        out_specs=[anywhere] * 5,
+        scratch_shapes=[dma((planes,))] * 6 + [dma((2,)), dma((2,))],
         cost_estimate=busy(10),
         compiler_params=pltpu.CompilerParams(collective_id=ident, has_side_effects=True, vmem_limit_bytes=VMEM_LIMIT),
         name=name,
-    )(*inputs, *more)
+    )(x, side, weight)
+
+
+def turn_out(x, side, extra, planes, slots, ident, name):
+    rows, cols = x.shape
+    low, dma = x.dtype, pltpu.SemaphoreType.DMA
+    anywhere, vmem = pl.BlockSpec(memory_space=pl.ANY), pl.BlockSpec(memory_space=pltpu.VMEM)
+    many, one = (jax.ShapeDtypeStruct((extent, cols), low) for extent in (many_rows(planes, rows), rows))
+    return pl.pallas_call(
+        functools.partial(turn_out_body, planes, slots),
+        out_shape=[many, one, one, jax.ShapeDtypeStruct(extra.shape, extra.dtype)],
+        in_specs=[anywhere] * 2 + [vmem],
+        out_specs=[anywhere] * 3 + [vmem],
+        scratch_shapes=[dma((planes,))] * 6
+        + [pltpu.VMEM((planes - 1,) + extra.shape, extra.dtype), dma((planes - 1,)), dma((planes - 1,))],
+        cost_estimate=busy(10),
+        compiler_params=pltpu.CompilerParams(collective_id=ident, has_side_effects=True, vmem_limit_bytes=VMEM_LIMIT),
+        name=name,
+    )(x, side, extra)
 
 
 def mask_scores(scores, first, begin, size):
@@ -1504,11 +1568,10 @@
     def sum_blk(value, axis):
         return lax.psum_scatter(value, "blk", scatter_dimension=axis, tiled=True)
 
-    _, near_cotangent, mine = turn(
-        turn_in_body, [tokens[0], cotangent[0]], [True, True, False], planes, slots, 1, "turn_in"
+    w_rows = jnp.concatenate([query_weight, key_weight, value_weight], 1)
+    _, near_cotangent, mine, lower, upper = turn_in(
+        tokens[0], cotangent[0], w_rows, planes, slots, 1, "turn_in"
     )
-    w_qkv = after(jnp.concatenate([query_weight, key_weight, value_weight], 1), mine)
-    w_qkv = lax.all_gather(w_qkv, "blk", axis=0, tiled=True)
     gains = jnp.stack([query_gain, key_gain]).astype(f32)
     plane_lengths = lax.dynamic_slice_in_dim(lengths, plane * slots, slots, 0)
     segment, position = jax.vmap(lambda one: layout(one, span))(plane_lengths)
@@ -1526,7 +1589,7 @@
     cosine = cos_a * cos_b + sin_a * sin_b
     sine = (sin_a * cos_b - cos_a * sin_b) * sign
 
-    inputs = gather(mine, width, slots, 2, "gather_tokens")
+    inputs, w_qkv = gather(mine, width, slots, 2, "gather_tokens", (w_rows, lower, upper))
     pre = dot(inputs, w_qkv)
     squares = jnp.stack([jnp.sum(pre[:, a * share : (a + 1) * share] ** 2, -1) for a in (0, 1)])
     both = lax.dynamic_update_slice(
@@ -1538,7 +1601,7 @@
     gain_mix, gain_feed = both[0], both[1]
     inverse = lax.rsqrt(squares[: 2 * count // 128].reshape(2, count) / D + EPS)
     inv_cols = inverse.T.reshape(slots, span, 2)
-    w_o = lax.all_gather(after(output_weight, w_qkv), "blk", axis=1, tiled=True)
+    w_o = lax.all_gather(after(output_weight, inputs), "blk", axis=1, tiled=True)
     pre_groups = pre.reshape(slots, span, 3 * share)
     queries, keys, values, mixed, logs = attend(
         pre_groups, inv_cols, gains, cosine, sine, begin, heads, rows
@@ -1596,9 +1659,8 @@
     down_grad = jnp.concatenate([down_first, down_second], 1).astype(f32)
     gate_grad, up_grad = gate_grad.astype(f32), up_grad.astype(f32)
     tokens_low, down_grad, gate_grad, up_grad = lax.optimization_barrier((tokens_low, down_grad, gate_grad, up_grad))
-    _, block_output, tokens_grad, gain_sums = turn(
-        turn_out_body, [tokens_low, far_output], [True, False, False],
-        planes, slots, 14, "turn_out", gain_parts,
+    _, block_output, tokens_grad, gain_sums = turn_out(
+        tokens_low, far_output, gain_parts, planes, slots, 14, "turn_out"
     )
     side_grad = sum_blk(side_part, 0).astype(f32)
 

time: 756 us -> 817 us (1.081)
  Pallas kernels: 641 us -> 707 us
    pallas_call x4, Pallas kernels: 203 us -> 270 us  [the longest x2 162 us: gather(): pl.pallas_call(functools.partial(gather_body, width, slots, bool(weights)...]
  transfers between devices with their start and end apart: 7 -> 6, of which waited for: 1 -> 0; matrix products, arithmetic and copies ran while one was open for 9% -> 9% of each run, Pallas kernels for 54% -> 44%
where the time goes in v4:
time: 817 us; the launch traced here: 807 us
  Pallas kernels  707 us (87%)
  matrix products  37.7 us (5%)
  other arithmetic  28.5 us (3%)
  local copies, waits for them, and re-layouts  17.8 us (2%)
  between operations  14.9 us (2%)
    pallas_call x2, Pallas kernels, gather(): pl.pallas_call(functools.partial(gather_body, width, slots, bool(weights)...  162 us
    pallas_call x2, Pallas kernels, scatter(): pl.pallas_call(functools.partial(scatter_body, width, slots, flat, len(le...  115 us
    pallas_call x1, Pallas kernels, feed(): pl.pallas_call(functools.partial(feed_body, width, slots, step), out_shap...  99.7 us
    pallas_call x2, Pallas kernels, push(): pl.pallas_call(functools.partial(push_body, second, width, slots), out_sh...  71.8 us
    pallas_call x1, Pallas kernels, pull(): pl.pallas_call(functools.partial(pull_body, width, slots, 1024, chunk), o...  69.4 us
    pallas_call x1, Pallas kernels, turn_out(): pl.pallas_call(functools.partial(turn_out_body, planes, slots), out_shape...  58 us
    pallas_call x1, Pallas kernels, turn_in(): pl.pallas_call(functools.partial(turn_in_body, planes, slots), out_shape=...  50 us
    pallas_call x1, Pallas kernels, attend_back(): pl.pallas_call(functools.partial(attend_back_body, size), grid=(slots, he...  27 us
  transfers between devices with their start and end apart: 6, of which 0 were waited for; matrix products, arithmetic and copies ran while one was open for 9% of the time, Pallas kernels for 44%

profile of v4, /device:TPU:8, one launch (start us, length us, event | category | flops | bytes accessed | tf_op | source)
XLA Modules:
  0.0 806.6 jit_solution(17053086577263695859)
XLA Ops:
  7.2 1.0 constant_dynamic-update-slice_fusion.2
  8.2 1.0 constant_dynamic-update-slice_fusion.1
  9.2 1.0 constant_dynamic-update-slice_fusion.w_ref.refs_1_
  10.2 0.9 copy-done.4
  11.0 50.0 %turn_in.1 = (bf16[320,2048]{1,0:T(8,128)(2,1)}, bf16[320,2048]{1,0:T(8,128)(2,1)}, bf16[320,2048]{1,0:T(8,128)(2,1)}, bf16[512,768]{1,0:T(8,128)(2,1)}, bf16[512,768]{1,0:T(8,128)(2,1)}) custom-call(bf16[320,2048]{1,0:T(8,128)(2,1)} %bitcast.84, bf16[320,2048]{1,0:T(8,128)(2,1)} %bitcast.85, bf16[512,768]{1,0:T(8,128)(2,1)} %copy-done.4), custom_call_target="tpu_custom_call" | custom-call | bytes 35000000 | tf_op jit(solution)/shard_map/turn_in/pallas_call | solution.py:730
  61.1 114.4 %gather_tokens.1 = (bf16[2560,2048]{1,0:T(8,128)(2,1)}, bf16[2048,768]{1,0:T(8,128)(2,1)}) custom-call(bf16[320,2048]{1,0:T(8,128)(2,1)} %get-tuple-element.63.refs_0_.refs_2_, bf16[512,768]{1,0:T(8,128)(2,1)} %copy-done.4, bf16[512,768]{1,0:T(8,128)(2,1)} %get-tuple-element.64.refs_2_, bf16[512,768]{1,0:T(8,128)(2,1)} %get-tuple-element.65.refs_3_), custom_call_target="tpu_custom_call" | custom-call | bytes 35000000 | tf_op jit(solution)/shard_map/gather_tokens/pallas_call | solution.py:378
  175.8 0.7 compare_select_fusion.1.begin_ref
  176.7 12.1 %fusion.9 = f32[2560,768]{1,0:T(8,128)S(1)} fusion(bf16[2560,2048]{1,0:T(8,128)(2,1)} %get-tuple-element.66.x_ref, bf16[2048,768]{1,0:T(8,128)(2,1)} %get-tuple-element.67.refs_1_), kind=kOutput, calls=%fused_computation.65 | convolution fusion | flops 8053063680 | bytes 21495808 | tf_op jit(solution)/shard_map/dot_general | solution.py:55
  188.7 3.1 copy-done.2
  191.9 0.7 multiply_reduce_fusion.1
  192.7 0.6 pad_maximum_fusion.2.x_ref
  193.3 8.2 %total_squares.1 = f32[72,128]{1,0:T(8,128)} custom-call(f32[72,128]{1,0:T(8,128)} %pad_maximum_fusion.2.x_ref), custom_call_target="tpu_custom_call" | custom-call | bytes 24500000 | tf_op jit(solution)/shard_map/total_squares/pallas_call | solution.py:500
  201.5 0.7 add_rsqrt_fusion
  202.3 1.5 copy.33
  204.7 2.5 subtract_multiply_fusion
  207.2 17.7 %attend.1 = (bf16[2,1280,256]{2,1,0:T(8,128)(2,1)}, bf16[2,1280,256]{2,1,0:T(8,128)(2,1)}, bf16[2,1280,256]{2,1,0:T(8,128)(2,1)}, bf16[2,1280,256]{2,1,0:T(8,128)(2,1)}, f32[2,2,1,1280]{3,2,1,0:T(1,128)}) custom-call(f32[2,1280,768]{2,1,0:T(8,128)} %bitcast.73, f32[2,1280,768]{2,1,0:T(8,128)} %bitcast.74, f32[2,1280,768]{2,1,0:T(8,128)} %bitcast.75, ...), custom_call_target="tpu_custom_call" | custom-call | bytes 17500000 | tf_op jit(solution)/shard_map/attend/pallas_call | solution.py:831
  224.9 1.3 fusion.7
  226.2 57.1 %scatter_mixed.1 = (f32[320,2048]{1,0:T(8,128)}, bf16[320,2048]{1,0:T(8,128)(2,1)}, f32[320,2048]{1,0:T(8,128)}, f32[320,1]{1,0:T(8,128)}) custom-call(bf16[2560,256]{1,0:T(8,128)(2,1)} %bitcast.81, bf16[256,2048]{1,0:T(8,128)(2,1)} %all-gather.2.cloned.1.call-done.refs_1_, bf16[320,2048]{1,0:T(8,128)(2,1)} %get-tuple-element.63.refs_0_.refs_2_, ...), custom_call_target="tpu_custom_call" | custom-call | bytes 35000000 | tf_op jit(solution)/shard_map/scatter_mixed/pallas_call | solution.py:462
  283.3 99.7 %feed.1 = (bf16[320,2048]{1,0:T(8,128)(2,1)}, bf16[320,1024]{1,0:T(8,128)(2,1)}, bf16[320,1024]{1,0:T(8,128)(2,1)}, f32[8,2048]{1,0:T(8,128)}, bf16[2560,2048]{1...) custom-call(bf16[320,2048]{1,0:T(8,128)(2,1)} %get-tuple-element.73., ...), custom_call_target="tpu_custom_call" | custom-call | bytes 315000000 | tf_op jit(solution)/shard_map/feed/pallas_call | solution.py:1139
  383.1 32.2 %push_first.1 = (bf16[1024,1024]{1,0:T(8,128)(2,1)}, bf16[4,2,320,1024]{3,2,1,0:T(8,128)(2,1)}, bf16[320,2048]{1,0:T(8,128)(2,1)}) custom-call(bf16[320,1024]{1,0:T(8,128)(2,1)} %get-tuple-element.80.refs_0_, bf16[2560,1024]{1,0:T(8,128)(2,1)} %get-tuple-element.77.refs_1_, bf16[320,2048]{1,0:T(8,128)(2,1)} %get-tuple-element.81.refs_2_), custom_call_target="tpu_custom_call" | custom-call | bytes 35000000 | tf_op jit(solution)/shard_map/push_first/pallas_call | solution.py:1360
  415.4 39.6 %push_second.1 = (bf16[1024,1024]{1,0:T(8,128)(2,1)}, bf16[2560,1024]{1,0:T(8,128)(2,1)}, bf16[2560,1024]{1,0:T(8,128)(2,1)}) custom-call(bf16[320,1024]{1,0:T(8,128)(2,1)} %get-tuple-element.76.refs_0_, bf16[2560,1024]{1,0:T(8,128)(2,1)} %get-tuple-element.77.refs_1_, bf16[1024,2048]{1,0:T(8,128)(2,1)} %refs_2_.1, ...), custom_call_target="tpu_custom_call" | custom-call | bytes 35000000 | tf_op jit(solution)/shard_map/push_second/pallas_call | solution.py:1360
  455.0 16.9 %convolution_convert_fusion.1 = bf16[2048,1024]{1,0:T(8,128)(2,1)} fusion(bf16[2560,2048]{1,0:T(8,128)(2,1)} %get-tuple-element.84.h_hbm, bf16[2560,1024]{1,0:T(8,128)(2,1)} %get-tuple-element.86.gg_hbm), kind=kOutput, calls=%fused_computation.2 | convolution fusion | flops 10739515392 | bytes 19922944 | tf_op jit(solution)/shard_map/dot_general | solution.py:59
  472.0 69.4 %pull.1 = (f32[320,2048]{1,0:T(8,128)}, bf16[320,2048]{1,0:T(8,128)(2,1)}, f32[8,2048]{1,0:T(8,128)}, bf16[2048,1024]{1,0:T(8,128)(2,1)}) custom-call(bf16[2560,1024]{1,0:T(8,128)(2,1)} %get-tuple-element.86.gg_hbm, bf16[2560,1024]{1,0:T(8,128)(2,1)} %get-tuple-element.87.gu_hbm, bf16[2048,1024]{1,0:T(8,128)(2,1)} %wg_hbm.3, bf16[2048,1024]{1,0:T(8,128)(2,1)} %wu_hbm.3, ...), custom_call_target="tpu_custom_call" | custom-call | bytes 35000000 | tf_op jit(solution)/shard_map/pull/pallas_call | solution.py:1491
  541.6 0.7 copy-done.14
  542.4 48.0 %gather_proj.1.p_ref = bf16[2560,2048]{1,0:T(8,128)(2,1)} custom-call(bf16[320,2048]{1,0:T(8,128)(2,1)} %get-tuple-element.91.refs_0_), custom_call_target="tpu_custom_call" | custom-call | bytes 35000000 | tf_op jit(solution)/shard_map/gather_proj/pallas_call | solution.py:378
  590.5 8.8 %convolution_convert_fusion = bf16[2560,256]{1,0:T(8,128)(2,1)} fusion(bf16[2560,2048]{1,0:T(8,128)(2,1)} %gather_proj.1.p_ref, bf16[256,2048]{1,0:T(8,128)(2,1)S(1)} %copy-done.7), kind=kOutput, calls=%fused_computation.1 | convolution fusion | flops 2685009920 | bytes 12845056 | tf_op jit(solution)/shard_map/dot_general | solution.py:65
  599.2 27.0 %attend_back.1 = (f32[2,1280,256]{2,1,0:T(8,128)}, f32[2,1280,256]{2,1,0:T(8,128)}, bf16[2,1280,256]{2,1,0:T(8,128)(2,1)}, f32[2,2,1280,2]{3,2,1,0:T(8,128)}, f32[2,2,256]{2,1,0:T(2,128)}) custom-call(bf16[2,1280,256]{2,1,0:T(8,128)(2,1)} %get-tuple-element.68.q_ref, bf16[2,1280,256]{2,1,0:T(8,128)(2,1)} %get-tuple-element.69.k_ref, ...), custom_call_target="tpu_custom_call" | custom-call | bytes 17500000 | tf_op jit(solution)/shard_map/attend_back/pallas_call | solution.py:894
  626.2 0.7 reduce_sum.57
  627.0 2.1 reduce_sum.56
  629.6 0.6 pad_maximum_fusion.1.x_ref
  630.2 9.5 %total_means.1 = f32[104,128]{1,0:T(8,128)} custom-call(f32[104,128]{1,0:T(8,128)} %pad_maximum_fusion.1.x_ref), custom_call_target="tpu_custom_call" | custom-call | bytes 24500000 | tf_op jit(solution)/shard_map/total_means/pallas_call | solution.py:500
  639.7 0.7 slice_multiply_fusion
  640.5 5.4 fusion.3
  645.9 2.0 pad_maximum_fusion.refs_0_.g_ref
  648.0 18.0 %side_grads.1 = bf16[2048,1024]{1,0:T(8,128)(2,1)} custom-call(bf16[2560,2048]{1,0:T(8,128)(2,1)} %get-tuple-element.66.x_ref, bf16[2560,2048]{1,0:T(8,128)(2,1)} %gather_proj.1.p_ref, bf16[2560,768]{1,0:T(8,128)(2,1)} %pad_maximum_fusion.refs_0_.g_ref, bf16[2560,256]{1,0:T(8,128)(2,1)} %bitcast.82), custom_call_target="tpu_custom_call" | custom-call | bytes 35000000 | tf_op jit(solution)/shard_map/side_grads/pallas_call | solution.py:1526
  666.0 1.0 copy-done.11
  667.2 1.6 maximum_convert_fusion
  668.8 0.6 slice.186.v_ref
  669.4 58.4 %scatter_tokens.1.x_ref = bf16[320,2048]{1,0:T(8,128)(2,1)} custom-call(bf16[2560,768]{1,0:T(8,128)(2,1)} %pad_maximum_fusion.refs_0_.g_ref, bf16[2048,768]{1,0:T(8,128)(2,1)} %get-tuple-element.67.refs_1_, f32[320,2048]{1,0:T(8,128)} %get-tuple-element.103.refs_2_), custom_call_target="tpu_custom_call" | custom-call | bytes 35000000 | tf_op jit(solution)/shard_map/scatter_tokens/pallas_call | solution.py:462
  727.8 1.6 convert_element_type.79
  729.4 2.8 convert_element_type.80
  732.2 58.0 %turn_out.1 = (bf16[320,2048]{1,0:T(8,128)(2,1)}, bf16[320,2048]{1,0:T(8,128)(2,1)}, bf16[320,2048]{1,0:T(8,128)(2,1)}, f32[64,128]{1,0:T(8,128)}) custom-call(bf16[320,2048]{1,0:T(8,128)(2,1)} %scatter_tokens.1.x_ref, bf16[320,2048]{1,0:T(8,128)(2,1)} %get-tuple-element.106.far_c, f32[64,128]{1,0:T(8,128)} %slice.186.v_ref), custom_call_target="tpu_custom_call" | custom-call | bytes 35000000 | tf_op jit(solution)/shard_map/turn_out/pallas_call | solution.py:747
  790.2 0.8 reshape.481
  791.6 3.1 bitcast_convert_fusion
  794.7 1.5 convert_element_type.83
  796.3 1.0 copy.35
  797.3 1.2 fusion.6
  798.5 1.1 copy.45
  (95 shorter events, 3.1 us)
Async XLA Ops:
  7.2 168.4 %copy-start = (s32[8,3]{0,1:T(4,128)S(1)}, s32[8,3]{0,1:T(4,128)}, u32[]{:S(2)}) copy-start(s32[8,3]{0,1:T(4,128)} %param.19) | copy-start | bytes 292
  7.2 219.1 %all-gather.2.cloned.1.call-start = ((), (), s32[]{:S(2)}) async-start(), calls=%async_computation.5 | async-start | bytes 1310720 | tf_op jit(solution)/shard_map/all_gather | solution.py:1604
  10.2 0.9 copy-start.4
  61.0 114.7 %copy-start.18 = (bf16[256]{0:T(256)(128)(2,1)S(1)}, bf16[256]{0:T(256)(128)(2,1)}, u32[]{:S(2)}) copy-start(bf16[256]{0:T(256)(128)(2,1)} %param.24) | copy-start | bytes 1540
  61.0 114.7 %copy-start.19 = (bf16[256]{0:T(256)(128)(2,1)S(1)}, bf16[256]{0:T(256)(128)(2,1)}, u32[]{:S(2)}) copy-start(bf16[256]{0:T(256)(128)(2,1)} %param.25) | copy-start | bytes 1540
  61.0 114.7 %copy-start.20 = (bf16[256]{0:T(256)(128)(2,1)S(1)}, bf16[256]{0:T(256)(128)(2,1)}, u32[]{:S(2)}) copy-start(bf16[256]{0:T(256)(128)(2,1)} %param.26) | copy-start | bytes 1540
  61.1 114.7 %copy-start.21 = (bf16[256]{0:T(256)(128)(2,1)S(1)}, bf16[256]{0:T(256)(128)(2,1)}, u32[]{:S(2)}) copy-start(bf16[256]{0:T(256)(128)(2,1)} %param.30) | copy-start | bytes 1540
  175.5 296.5 %reduce-scatter.6.cloned.1.call-start = ((), (), s32[]{:S(2)}) async-start(), calls=%async_computation.6 | async-start | bytes 2621440 | tf_op jit(solution)/shard_map/reduce_scatter | solution.py:1569
  188.7 3.1 copy-start.2
  191.8 12.0 %copy-start.17 = (f32[128]{0:T(128)S(1)}, f32[128]{0:T(128)}, u32[]{:S(2)}) copy-start(f32[128]{0:T(128)} %constant.45.clone) | copy-start | bytes 1540
  191.8 12.9 %copy-start.9 = (f32[1280,128]{1,0:T(8,128)S(1)}, f32[1280,128]{1,0:T(8,128)}, u32[]{:S(2)}) copy-start(f32[1280,128]{1,0:T(8,128)} %constant.44.clone) | copy-start | bytes 1966084
  191.8 12.9 %copy-start.10 = (f32[1280,128]{1,0:T(8,128)S(1)}, f32[1280,128]{1,0:T(8,128)}, u32[]{:S(2)}) copy-start(f32[1280,128]{1,0:T(8,128)} %constant.15.clone) | copy-start | bytes 1966084
  191.8 12.9 %copy-start.16 = (f32[128]{0:T(128)S(1)}, f32[128]{0:T(128)}, u32[]{:S(2)}) copy-start(f32[128]{0:T(128)} %constant.46.clone) | copy-start | bytes 1540
  415.3 175.1 %reduce-scatter.8.cloned.1.call-start = ((), (), s32[]{:S(2)}) async-start(), calls=%async_computation.7 | async-start | bytes 2621440 | tf_op jit(solution)/shard_map/reduce_scatter | solution.py:1569
  455.0 175.2 %reduce-scatter.10.cloned.1.call-start = ((), (), s32[]{:S(2)}) async-start(), calls=%async_computation.8 | async-start | bytes 5242880 | tf_op jit(solution)/shard_map/reduce_scatter | solution.py:1569
  472.0 257.4 %reduce-scatter.12.cloned.1.call-start = ((), (), s32[]{:S(2)}) async-start(), calls=%async_computation.9 | async-start | bytes 5242880 | tf_op jit(solution)/shard_map/reduce_scatter | solution.py:1569
  541.5 0.8 copy-start.14
  541.5 253.2 %reduce-scatter.14.cloned.1.call-start = ((), (), s32[]{:S(2)}) async-start(), calls=%async_computation.10 | async-start | bytes 5242880 | tf_op jit(solution)/shard_map/reduce_scatter | solution.py:1569
  542.3 48.1 %copy-start.15 = (f32[8,2048]{1,0:T(8,128)S(1)}, f32[8,2048]{1,0:T(8,128)}, u32[]{:S(2)}) copy-start(f32[8,2048]{1,0:T(8,128)} %get-tuple-element.98) | copy-start | bytes 196612
  542.4 48.1 %copy-start.7 = (bf16[256,2048]{1,0:T(8,128)(2,1)S(1)}, bf16[256,2048]{1,0:T(8,128)(2,1)}, u32[]{:S(2)}) copy-start(bf16[256,2048]{1,0:T(8,128)(2,1)} %all-gather.2.cloned.1.call-done.refs_1_) | copy-start | bytes 3145732
  640.5 5.5 copy-start.6
  666.0 1.0 copy-start.11
  666.0 1.2 copy-start.12
  666.0 2.8 copy-start.13
  669.4 58.4 %copy-start.8 = (bf16[512,1024]{1,0:T(8,128)(2,1)S(1)}, bf16[512,1024]{1,0:T(8,128)(2,1)}, u32[]{:S(2)}) copy-start(bf16[512,1024]{1,0:T(8,128)(2,1)} %reduce-scatter.10.cloned.1.call-done) | copy-start | bytes 3145732
  794.7 2.6 copy-start.3
  796.2 2.2 copy-start.5
  796.3 3.2 copy-start.1
Sparse Core Ops, SparseCore 0:
  175.6 26.9 all-gather.1
  415.4 41.4 reduce-scatter.5
  459.4 43.1 reduce-scatter.7
  504.7 78.3 reduce-scatter.9
  585.4 77.2 reduce-scatter.11
  666.1 94.9 reduce-scatter.13

commit v5 on v3

--- a/solution.py
+++ b/solution.py
@@ -757,7 +757,7 @@
         log_ref[:, cols] = top + jnp.log(weight)
 
 
-def attend(pre, inverse, gains, cosine, sine, begin, heads, size):
+def attend(pre, rows, inverse, gains, cosine, sine, begin, heads, size):
     slots, span, _ = pre.shape
     low, f32 = jnp.bfloat16, jnp.float32
     head = lambda offset: pl.BlockSpec((None, span, HD), lambda g, h: (g, 0, offset + h))
@@ -769,14 +769,14 @@
         grid=(slots, heads),
         out_shape=[out, out, out, out, jax.ShapeDtypeStruct((slots, heads, 1, span), f32)],
         in_specs=[
-            head(0), head(heads), head(2 * heads), every(2),
+            head(0), head(heads), head(0), every(2),
             pl.BlockSpec((2, HD), lambda g, h: (0, h)), every(HD), every(HD), line,
         ],
         out_specs=[head(0)] * 4 + [pl.BlockSpec((None, None, 1, span), lambda g, h: (g, h, 0, 0))],
         compiler_params=pltpu.CompilerParams(vmem_limit_bytes=VMEM_LIMIT),
         cost_estimate=busy(5),
         name="attend",
-    )(pre, pre, pre, inverse, gains, cosine, sine, begin)
+    )(pre, pre, rows, inverse, gains, cosine, sine, begin)
 
 
 def attend_back_body(size, q_ref, k_ref, v_ref, g_ref, log_ref, qp_ref, kp_ref, inv_ref, gain_ref,
@@ -1444,20 +1444,19 @@
     )(grad_gate, grad_up, gate_weight, up_weight, gathered, grad_out, normed, inverse, gain)
 
 
-def side_body(x_ref, p_ref, g_ref, m_ref, out_ref):
-    dims = (((0,), (0,)), ((), ()))
-    split = g_ref.shape[1]
-    out_ref[:, :split] = lax.dot_general(
-        x_ref[...], g_ref[...], dims, preferred_element_type=jnp.float32
-    ).astype(out_ref.dtype)
-    out_ref[:, split:] = lax.dot_general(
-        p_ref[...], m_ref[...], dims, preferred_element_type=jnp.float32
-    ).astype(out_ref.dtype)
-
-
-def side_grads(inputs, grad_proj, grads, mixed):
+def side_body(x_ref, p_ref, qk_ref, v_ref, m_ref, out_ref):
+    first = 0
+    for left, right in ((x_ref, qk_ref), (x_ref, v_ref), (p_ref, m_ref)):
+        last = first + right.shape[1]
+        out_ref[:, first:last] = lax.dot_general(
+            left[...], right[...], (((0,), (0,)), ((), ())), preferred_element_type=jnp.float32
+        ).astype(out_ref.dtype)
+        first = last
+
+
+def side_grads(inputs, grad_proj, grad_qk, grad_v, mixed):
     count, cols = inputs.shape
-    extent = grads.shape[1] + mixed.shape[1]
+    extent = grad_qk.shape[1] + grad_v.shape[1] + mixed.shape[1]
     chunk = 256
     return pl.pallas_call(
         side_body,
@@ -1465,13 +1464,14 @@
         out_shape=jax.ShapeDtypeStruct((cols, extent), inputs.dtype),
         in_specs=[
             pl.BlockSpec((count, chunk), lambda n: (0, n)), pl.BlockSpec((count, chunk), lambda n: (0, n)),
-            pl.BlockSpec(grads.shape, lambda n: (0, 0)), pl.BlockSpec(mixed.shape, lambda n: (0, 0)),
+            pl.BlockSpec(grad_qk.shape, lambda n: (0, 0)), pl.BlockSpec(grad_v.shape, lambda n: (0, 0)),
+            pl.BlockSpec(mixed.shape, lambda n: (0, 0)),
         ],
         out_specs=pl.BlockSpec((chunk, extent), lambda n: (n, 0)),
         compiler_params=pltpu.CompilerParams(vmem_limit_bytes=VMEM_LIMIT),
         cost_estimate=busy(10),
         name="side_grads",
-    )(inputs, grad_proj, grads, mixed)
+    )(inputs, grad_proj, grad_qk, grad_v, mixed)
 
 
 def local(
@@ -1507,8 +1507,8 @@
     _, near_cotangent, mine = turn(
         turn_in_body, [tokens[0], cotangent[0]], [True, True, False], planes, slots, 1, "turn_in"
     )
-    w_qkv = after(jnp.concatenate([query_weight, key_weight, value_weight], 1), mine)
-    w_qkv = lax.all_gather(w_qkv, "blk", axis=0, tiled=True)
+    w_qk = after(jnp.concatenate([query_weight, key_weight], 1), mine)
+    w_qk = lax.all_gather(w_qk, "blk", axis=0, tiled=True)
     gains = jnp.stack([query_gain, key_gain]).astype(f32)
     plane_lengths = lax.dynamic_slice_in_dim(lengths, plane * slots, slots, 0)
     segment, position = jax.vmap(lambda one: layout(one, span))(plane_lengths)
@@ -1527,7 +1527,9 @@
     sine = (sin_a * cos_b - cos_a * sin_b) * sign
 
     inputs = gather(mine, width, slots, 2, "gather_tokens")
-    pre = dot(inputs, w_qkv)
+    w_v = lax.all_gather(after(value_weight, inputs), "blk", axis=0, tiled=True)
+    pre = dot(inputs, w_qk)
+    w_o = lax.all_gather(after(output_weight, pre), "blk", axis=1, tiled=True)
     squares = jnp.stack([jnp.sum(pre[:, a * share : (a + 1) * share] ** 2, -1) for a in (0, 1)])
     both = lax.dynamic_update_slice(
         jnp.zeros((2, D), f32), jnp.stack([attention_gain, feedforward_gain]).astype(f32), (0, place * share)
@@ -1538,10 +1540,10 @@
     gain_mix, gain_feed = both[0], both[1]
     inverse = lax.rsqrt(squares[: 2 * count // 128].reshape(2, count) / D + EPS)
     inv_cols = inverse.T.reshape(slots, span, 2)
-    w_o = lax.all_gather(after(output_weight, w_qkv), "blk", axis=1, tiled=True)
-    pre_groups = pre.reshape(slots, span, 3 * share)
+    pre_groups = pre.reshape(slots, span, 2 * share)
+    value_rows = dot(inputs, after(w_v, squares)).astype(low).reshape(slots, span, share)
     queries, keys, values, mixed, logs = attend(
-        pre_groups, inv_cols, gains, cosine, sine, begin, heads, rows
+        pre_groups, value_rows, inv_cols, gains, cosine, sine, begin, heads, rows
     )
     mixed = mixed.reshape(count, share)
     hidden, hidden_low, proj_normed, proj_inv = scatter(
@@ -1588,10 +1590,11 @@
         scaled = scaled.reshape(count, share)
         return (inverse[index][:, None] * (scaled - normed * means[index][:, None])).astype(low)
 
-    grads = jnp.concatenate([finish(scaled_q, 0), finish(scaled_k, 1), grad_v.reshape(count, share)], 1)
-    side_part = side_grads(inputs, grad_proj, grads, mixed)
+    grad_qk = jnp.concatenate([finish(scaled_q, 0), finish(scaled_k, 1)], 1)
+    grad_v = grad_v.reshape(count, share)
+    side_part = side_grads(inputs, grad_proj, grad_qk, grad_v, mixed)
     tokens_low = scatter(
-        [grads], [w_qkv], width, slots, True, 11, "scatter_tokens", "add", (grad_hidden,)
+        [grad_qk, grad_v], [w_qk, w_v], width, slots, True, 11, "scatter_tokens", "add", (grad_hidden,)
     )
     down_grad = jnp.concatenate([down_first, down_second], 1).astype(f32)
     gate_grad, up_grad = gate_grad.astype(f32), up_grad.astype(f32)

time: 756 us -> 750 us (level)
    dot_general x1 -> x2, matrix products: 12.1 us -> 17.3 us  [dot(): return jnp.dot(left, right, preferred_element_type=jnp.float32)]
  transfers between devices with their start and end apart: 7 -> 8, of which waited for: 1 -> 2; matrix products, arithmetic and copies ran while one was open for 9% -> 10% of each run, Pallas kernels for 54% -> 54%
where the time goes in v5:
time: 750 us; the launch traced here: 742 us
  Pallas kernels  640 us (85%)
  matrix products  42.8 us (6%)
  other arithmetic  30 us (4%)
  between operations  14.9 us (2%)
  local copies, waits for them, and re-layouts  12.5 us (2%)
    pallas_call x2, Pallas kernels, scatter(): pl.pallas_call(functools.partial(scatter_body, width, slots, flat, len(le...  115 us
    pallas_call x2, Pallas kernels, turn(): pl.pallas_call(functools.partial(body, planes, slots), out_shape=[shape(m...  104 us
    pallas_call x1, Pallas kernels, feed(): pl.pallas_call(functools.partial(feed_body, width, slots, step), out_shap...  100 us
    pallas_call x2, Pallas kernels, gather(): pl.pallas_call(functools.partial(gather_body, width, slots, side), out_sh...  98.8 us
    pallas_call x2, Pallas kernels, push(): pl.pallas_call(functools.partial(push_body, second, width, slots), out_sh...  72.6 us
    pallas_call x1, Pallas kernels, pull(): pl.pallas_call(functools.partial(pull_body, width, slots, 1024, chunk), o...  69.1 us
    pallas_call x1, Pallas kernels, attend_back(): pl.pallas_call(functools.partial(attend_back_body, size), grid=(slots, he...  27 us
    pallas_call x1, Pallas kernels, side_grads(): pl.pallas_call(side_body, grid=(cols // chunk,), out_shape=jax.ShapeDtype...  18 us
  transfers between devices with their start and end apart: 8, of which 2 were waited for; matrix products, arithmetic and copies ran while one was open for 10% of the time, Pallas kernels for 54%

profile of v5, /device:TPU:8, one launch (start us, length us, event | category | flops | bytes accessed | tf_op | source)
XLA Modules:
  0.0 742.4 jit_solution(6304121881423575770)
XLA Ops:
  7.2 1.9 pad_maximum_fusion.1
  9.1 47.0 %turn_in.1 = (bf16[320,2048]{1,0:T(8,128)(2,1)}, bf16[320,2048]{1,0:T(8,128)(2,1)}, bf16[320,2048]{1,0:T(8,128)(2,1)}) custom-call(bf16[320,2048]{1,0:T(8,128)(2,1)} %bitcast.89, bf16[320,2048]{1,0:T(8,128)(2,1)} %bitcast.90), custom_call_target="tpu_custom_call" | custom-call | bytes 35000000 | tf_op jit(solution)/shard_map/turn_in/pallas_call | solution.py:684
  56.2 50.5 %gather_tokens.1.x_ref = bf16[2560,2048]{1,0:T(8,128)(2,1)} custom-call(bf16[320,2048]{1,0:T(8,128)(2,1)} %get-tuple-element.62.refs_0_.refs_2_), custom_call_target="tpu_custom_call" | custom-call | bytes 35000000 | tf_op jit(solution)/shard_map/gather_tokens/pallas_call | solution.py:349
  107.1 0.7 compare_select_fusion.1.begin_ref
  108.0 0.6 maximum_convert_fusion.1.gain_ref
  108.9 2.5 subtract_multiply_fusion
  111.4 9.1 %fusion.9 = f32[2560,512]{1,0:T(8,128)S(1)} fusion(bf16[2560,2048]{1,0:T(8,128)(2,1)} %gather_tokens.1.x_ref, bf16[2048,512]{1,0:T(8,128)(2,1)} %all-gather.4.cloned.1.call-done.refs_2_), kind=kOutput, calls=%fused_computation.64 | convolution fusion | flops 5368709120 | bytes 17825792 | tf_op jit(solution)/shard_map/dot_general | solution.py:55
  120.5 0.7 multiply_reduce_fusion.1
  121.3 1.6 copy-done.2
  122.9 0.6 pad_maximum_fusion.3.x_ref
  123.5 8.2 %total_squares.1 = f32[72,128]{1,0:T(8,128)} custom-call(f32[72,128]{1,0:T(8,128)} %pad_maximum_fusion.3.x_ref), custom_call_target="tpu_custom_call" | custom-call | bytes 24500000 | tf_op jit(solution)/shard_map/total_squares/pallas_call | solution.py:471
  131.9 0.7 add_rsqrt_fusion
  132.6 1.2 all-gather.6.cloned.1.call-done.refs_3_
  133.8 1.5 copy.33
  135.3 8.2 %convolution_convert_fusion.1 = bf16[2560,256]{1,0:T(8,128)(2,1)} fusion(bf16[2560,2048]{1,0:T(8,128)(2,1)} %gather_tokens.1.x_ref, bf16[2048,256]{1,0:T(8,128)(2,1)} %all-gather.6.cloned.1.call-done.refs_3_), kind=kOutput, calls=%fused_computation.1 | convolution fusion | flops 2685009920 | bytes 12845056 | tf_op jit(solution)/shard_map/dot_general | solution.py:55
  143.5 17.6 %attend.1 = (bf16[2,1280,256]{2,1,0:T(8,128)(2,1)}, bf16[2,1280,256]{2,1,0:T(8,128)(2,1)}, bf16[2,1280,256]{2,1,0:T(8,128)(2,1)}, bf16[2,1280,256]{2,1,0:T(8,128)(2,1)}, f32[2,2,1,1280]{3,2,1,0:T(1,128)}) custom-call(f32[2,1280,512]{2,1,0:T(8,128)} %bitcast.76, f32[2,1280,512]{2,1,0:T(8,128)} %bitcast.77, bf16[2,1280,256]{2,1,0:T(8,128)(2,1)} %bitcast.88, ...), custom_call_target="tpu_custom_call" | custom-call | bytes 17500000 | tf_op jit(solution)/shard_map/attend/pallas_call | solution.py:767
  161.1 1.3 fusion.7
  162.9 56.2 %scatter_mixed.1 = (f32[320,2048]{1,0:T(8,128)}, bf16[320,2048]{1,0:T(8,128)(2,1)}, f32[320,2048]{1,0:T(8,128)}, f32[320,1]{1,0:T(8,128)}) custom-call(bf16[2560,256]{1,0:T(8,128)(2,1)} %bitcast.83, bf16[256,2048]{1,0:T(8,128)(2,1)} %all-gather.8.cloned.1.call-done.refs_1_, bf16[320,2048]{1,0:T(8,128)(2,1)} %get-tuple-element.62.refs_0_.refs_2_, ...), custom_call_target="tpu_custom_call" | custom-call | bytes 35000000 | tf_op jit(solution)/shard_map/scatter_mixed/pallas_call | solution.py:433
  219.0 100.3 %feed.1 = (bf16[320,2048]{1,0:T(8,128)(2,1)}, bf16[320,1024]{1,0:T(8,128)(2,1)}, bf16[320,1024]{1,0:T(8,128)(2,1)}, f32[8,2048]{1,0:T(8,128)}, bf16[2560,2048]{1...) custom-call(bf16[320,2048]{1,0:T(8,128)(2,1)} %get-tuple-element.71., ...), custom_call_target="tpu_custom_call" | custom-call | bytes 315000000 | tf_op jit(solution)/shard_map/feed/pallas_call | solution.py:1075
  319.3 32.7 %push_first.1 = (bf16[1024,1024]{1,0:T(8,128)(2,1)}, bf16[4,2,320,1024]{3,2,1,0:T(8,128)(2,1)}, bf16[320,2048]{1,0:T(8,128)(2,1)}) custom-call(bf16[320,1024]{1,0:T(8,128)(2,1)} %get-tuple-element.78.refs_0_, bf16[2560,1024]{1,0:T(8,128)(2,1)} %get-tuple-element.75.refs_1_, bf16[320,2048]{1,0:T(8,128)(2,1)} %get-tuple-element.79.refs_2_), custom_call_target="tpu_custom_call" | custom-call | bytes 35000000 | tf_op jit(solution)/shard_map/push_first/pallas_call | solution.py:1296
  352.0 39.9 %push_second.1 = (bf16[1024,1024]{1,0:T(8,128)(2,1)}, bf16[2560,1024]{1,0:T(8,128)(2,1)}, bf16[2560,1024]{1,0:T(8,128)(2,1)}) custom-call(bf16[320,1024]{1,0:T(8,128)(2,1)} %get-tuple-element.74.refs_0_, bf16[2560,1024]{1,0:T(8,128)(2,1)} %get-tuple-element.75.refs_1_, bf16[1024,2048]{1,0:T(8,128)(2,1)} %refs_2_.1, ...), custom_call_target="tpu_custom_call" | custom-call | bytes 35000000 | tf_op jit(solution)/shard_map/push_second/pallas_call | solution.py:1296
  392.1 16.8 %convolution_convert_fusion.2 = bf16[2048,1024]{1,0:T(8,128)(2,1)} fusion(bf16[2560,2048]{1,0:T(8,128)(2,1)} %get-tuple-element.82.h_hbm, bf16[2560,1024]{1,0:T(8,128)(2,1)} %get-tuple-element.84.gg_hbm), kind=kOutput, calls=%fused_computation.2 | convolution fusion | flops 10739515392 | bytes 19922944 | tf_op jit(solution)/shard_map/dot_general | solution.py:59
  408.9 69.1 %pull.1 = (f32[320,2048]{1,0:T(8,128)}, bf16[320,2048]{1,0:T(8,128)(2,1)}, f32[8,2048]{1,0:T(8,128)}, bf16[2048,1024]{1,0:T(8,128)(2,1)}) custom-call(bf16[2560,1024]{1,0:T(8,128)(2,1)} %get-tuple-element.84.gg_hbm, bf16[2560,1024]{1,0:T(8,128)(2,1)} %get-tuple-element.85.gu_hbm, bf16[2048,1024]{1,0:T(8,128)(2,1)} %wg_hbm.3, bf16[2048,1024]{1,0:T(8,128)(2,1)} %wu_hbm.3, ...), custom_call_target="tpu_custom_call" | custom-call | bytes 35000000 | tf_op jit(solution)/shard_map/pull/pallas_call | solution.py:1427
  478.2 0.7 copy-done.12
  479.0 48.4 %gather_proj.1.p_ref = bf16[2560,2048]{1,0:T(8,128)(2,1)} custom-call(bf16[320,2048]{1,0:T(8,128)(2,1)} %get-tuple-element.89.refs_0_), custom_call_target="tpu_custom_call" | custom-call | bytes 35000000 | tf_op jit(solution)/shard_map/gather_proj/pallas_call | solution.py:349
  527.4 8.8 %convolution_convert_fusion = bf16[2560,256]{1,0:T(8,128)(2,1)} fusion(bf16[2560,2048]{1,0:T(8,128)(2,1)} %gather_proj.1.p_ref, bf16[256,2048]{1,0:T(8,128)(2,1)S(1)} %copy-done.6), kind=kOutput, calls=%fused_computation | convolution fusion | flops 2685009920 | bytes 12845056 | tf_op jit(solution)/shard_map/dot_general | solution.py:65
  536.2 27.0 %attend_back.1 = (f32[2,1280,256]{2,1,0:T(8,128)}, f32[2,1280,256]{2,1,0:T(8,128)}, bf16[2,1280,256]{2,1,0:T(8,128)(2,1)}, f32[2,2,1280,2]{3,2,1,0:T(8,128)}, f32[2,2,256]{2,1,0:T(2,128)}) custom-call(bf16[2,1280,256]{2,1,0:T(8,128)(2,1)} %get-tuple-element.66.q_ref, bf16[2,1280,256]{2,1,0:T(8,128)(2,1)} %get-tuple-element.67.k_ref, ...), custom_call_target="tpu_custom_call" | custom-call | bytes 17500000 | tf_op jit(solution)/shard_map/attend_back/pallas_call | solution.py:830
  563.2 0.7 reduce_sum.57
  564.0 2.1 reduce_sum.56
  566.6 0.6 pad_maximum_fusion.2.x_ref
  567.2 9.6 %total_means.1 = f32[104,128]{1,0:T(8,128)} custom-call(f32[104,128]{1,0:T(8,128)} %pad_maximum_fusion.2.x_ref), custom_call_target="tpu_custom_call" | custom-call | bytes 24500000 | tf_op jit(solution)/shard_map/total_means/pallas_call | solution.py:471
  576.8 0.7 slice_multiply_fusion
  577.5 5.3 fusion.3
  582.8 1.7 pad_maximum_fusion.refs_0_.qk_ref
  584.5 18.0 %side_grads.1 = bf16[2048,1024]{1,0:T(8,128)(2,1)} custom-call(bf16[2560,2048]{1,0:T(8,128)(2,1)} %gather_tokens.1.x_ref, bf16[2560,2048]{1,0:T(8,128)(2,1)} %gather_proj.1.p_ref, bf16[2560,512]{1,0:T(8,128)(2,1)} %pad_maximum_fusion.refs_0_.qk_ref, bf16[2560,256]{1,0:T(8,128)(2,1)} %bitcast.85, bf16[2560,256]{1,0:T(8,128)(2,1)} %bitcast.84), custom_call_target="tpu_custom_call" | custom-call | bytes 35000000 | tf_op jit(solution)/shard_map/side_grads/pallas_call | solution.py:1461
  602.6 1.0 copy-done.9
  603.8 1.6 maximum_convert_fusion
  605.4 0.6 slice.186.v_ref
  606.0 1.6 convert_element_type.83
  607.6 58.4 %scatter_tokens.1.x_ref = bf16[320,2048]{1,0:T(8,128)(2,1)} custom-call(bf16[2560,512]{1,0:T(8,128)(2,1)} %pad_maximum_fusion.refs_0_.qk_ref, bf16[2560,256]{1,0:T(8,128)(2,1)} %bitcast.86, bf16[2048,512]{1,0:T(8,128)(2,1)} %all-gather.4.cloned.1.call-done.refs_2_, bf16[2048,256]{1,0:T(8,128)(2,1)} %all-gather.6.cloned.1.call-done.refs_3_, ...), custom_call_target="tpu_custom_call" | custom-call | bytes 35000000 | tf_op jit(solution)/shard_map/scatter_tokens/pallas_call | solution.py:433
  666.0 2.8 convert_element_type.84
  668.8 57.2 %turn_out.1 = (bf16[320,2048]{1,0:T(8,128)(2,1)}, bf16[320,2048]{1,0:T(8,128)(2,1)}, bf16[320,2048]{1,0:T(8,128)(2,1)}, f32[64,128]{1,0:T(8,128)}) custom-call(bf16[320,2048]{1,0:T(8,128)(2,1)} %scatter_tokens.1.x_ref, bf16[320,2048]{1,0:T(8,128)(2,1)} %get-tuple-element.104.far_c, f32[64,128]{1,0:T(8,128)} %slice.186.v_ref), custom_call_target="tpu_custom_call" | custom-call | bytes 35000000 | tf_op jit(solution)/shard_map/turn_out/pallas_call | solution.py:684
  726.0 0.8 reshape.485
  727.4 3.1 bitcast_convert_fusion
  730.5 1.5 convert_element_type.87
  732.1 1.0 copy.35
  733.1 1.2 fusion.6
  734.3 1.1 copy.43
  (96 shorter events, 3.1 us)
Async XLA Ops:
  7.2 99.6 %copy-start = (s32[8,3]{0,1:T(4,128)S(1)}, s32[8,3]{0,1:T(4,128)}, u32[]{:S(2)}) copy-start(s32[8,3]{0,1:T(4,128)} %param.19) | copy-start | bytes 292
  7.2 104.2 %all-gather.4.cloned.1.call-start = ((), (), s32[]{:S(2)}) async-start(), calls=%async_computation.5 | async-start | bytes 2621440 | tf_op jit(solution)/shard_map/all_gather | solution.py:1511
  56.1 50.8 %copy-start.16 = (bf16[256]{0:T(256)(128)(2,1)S(1)}, bf16[256]{0:T(256)(128)(2,1)}, u32[]{:S(2)}) copy-start(bf16[256]{0:T(256)(128)(2,1)} %param.24) | copy-start | bytes 1540
  56.1 50.8 %copy-start.17 = (bf16[256]{0:T(256)(128)(2,1)S(1)}, bf16[256]{0:T(256)(128)(2,1)}, u32[]{:S(2)}) copy-start(bf16[256]{0:T(256)(128)(2,1)} %param.25) | copy-start | bytes 1540
  56.1 50.8 %copy-start.18 = (bf16[256]{0:T(256)(128)(2,1)S(1)}, bf16[256]{0:T(256)(128)(2,1)}, u32[]{:S(2)}) copy-start(bf16[256]{0:T(256)(128)(2,1)} %param.26) | copy-start | bytes 1540
  56.1 50.8 %copy-start.19 = (bf16[256]{0:T(256)(128)(2,1)S(1)}, bf16[256]{0:T(256)(128)(2,1)}, u32[]{:S(2)}) copy-start(bf16[256]{0:T(256)(128)(2,1)} %param.30) | copy-start | bytes 1540
  56.1 52.6 %copy-start.15 = (f32[128]{0:T(128)S(1)}, f32[128]{0:T(128)}, u32[]{:S(2)}) copy-start(f32[128]{0:T(128)} %constant.45.clone) | copy-start | bytes 1540
  56.2 52.7 %copy-start.7 = (f32[1280,128]{1,0:T(8,128)S(1)}, f32[1280,128]{1,0:T(8,128)}, u32[]{:S(2)}) copy-start(f32[1280,128]{1,0:T(8,128)} %constant.44.clone) | copy-start | bytes 1966084
  56.2 52.7 %copy-start.8 = (f32[1280,128]{1,0:T(8,128)S(1)}, f32[1280,128]{1,0:T(8,128)}, u32[]{:S(2)}) copy-start(f32[1280,128]{1,0:T(8,128)} %constant.15.clone) | copy-start | bytes 1966084
  56.2 52.7 %copy-start.14 = (f32[128]{0:T(128)S(1)}, f32[128]{0:T(128)}, u32[]{:S(2)}) copy-start(f32[128]{0:T(128)} %constant.46.clone) | copy-start | bytes 1540
  56.2 77.6 %all-gather.6.cloned.1.call-start = ((), (), s32[]{:S(2)}) async-start(), calls=%async_computation.6 | async-start | bytes 1310720 | tf_op jit(solution)/shard_map/all_gather | solution.py:1530
  106.7 56.1 %all-gather.8.cloned.1.call-start = ((), (), s32[]{:S(2)}) async-start(), calls=%async_computation.7 | async-start | bytes 1310720 | tf_op jit(solution)/shard_map/all_gather | solution.py:1532
  120.5 2.3 copy-start.2
  131.8 277.1 %reduce-scatter.6.cloned.1.call-start = ((), (), s32[]{:S(2)}) async-start(), calls=%async_computation.8 | async-start | bytes 2621440 | tf_op jit(solution)/shard_map/reduce_scatter | solution.py:1505
  352.0 175.4 %reduce-scatter.8.cloned.1.call-start = ((), (), s32[]{:S(2)}) async-start(), calls=%async_computation.9 | async-start | bytes 2621440 | tf_op jit(solution)/shard_map/reduce_scatter | solution.py:1505
  392.0 175.2 %reduce-scatter.10.cloned.1.call-start = ((), (), s32[]{:S(2)}) async-start(), calls=%async_computation.10 | async-start | bytes 5242880 | tf_op jit(solution)/shard_map/reduce_scatter | solution.py:1505
  408.9 257.1 %reduce-scatter.12.cloned.1.call-start = ((), (), s32[]{:S(2)}) async-start(), calls=%async_computation.11 | async-start | bytes 5242880 | tf_op jit(solution)/shard_map/reduce_scatter | solution.py:1505
  478.1 0.8 copy-start.12
  478.1 252.4 %reduce-scatter.14.cloned.1.call-start = ((), (), s32[]{:S(2)}) async-start(), calls=%async_computation.12 | async-start | bytes 5242880 | tf_op jit(solution)/shard_map/reduce_scatter | solution.py:1505
  478.9 48.4 %copy-start.13 = (f32[8,2048]{1,0:T(8,128)S(1)}, f32[8,2048]{1,0:T(8,128)}, u32[]{:S(2)}) copy-start(f32[8,2048]{1,0:T(8,128)} %get-tuple-element.96) | copy-start | bytes 196612
  478.9 48.5 %copy-start.6 = (bf16[256,2048]{1,0:T(8,128)(2,1)S(1)}, bf16[256,2048]{1,0:T(8,128)(2,1)}, u32[]{:S(2)}) copy-start(bf16[256,2048]{1,0:T(8,128)(2,1)} %all-gather.8.cloned.1.call-done.refs_1_) | copy-start | bytes 3145732
  602.6 1.0 copy-start.9
  602.6 1.2 copy-start.10
  602.6 2.8 copy-start.11
  602.6 3.4 copy-start.5
  730.5 2.6 copy-start.3
  732.1 2.2 copy-start.4
  732.1 3.2 copy-start.1
Sparse Core Ops, SparseCore 0:
  56.2 45.1 all-gather.3
  106.9 26.9 all-gather.5
  135.4 27.4 all-gather.7
  352.1 41.0 reduce-scatter.5
  395.4 43.1 reduce-scatter.7
  440.8 78.4 reduce-scatter.9
  521.6 77.2 reduce-scatter.11
  602.7 82.8 reduce-scatter.13

commit v6 on v5

--- a/solution.py
+++ b/solution.py
@@ -17,6 +17,7 @@
 NEG_FILL = -1e30
 VMEM_LIMIT = 60 * 1024 * 1024
 SCALE = HD ** (-0.5)
+FOLD = SCALE * 1.4426950408889634
 
 
 def busy(micros):
@@ -722,7 +723,7 @@
 
 
 def attend_body(size, q_ref, k_ref, v_ref, inv_ref, gain_ref, cos_ref, sin_ref, begin_ref,
-                qo_ref, ko_ref, vo_ref, mix_ref, log_ref):
+                qo_ref, ko_ref, vo_ref, mix_ref, log_ref, raw_ref):
     low = jnp.bfloat16
     span = q_ref.shape[0]
 
@@ -743,18 +744,31 @@
     for i in range(span // size):
         last = (i + 1) * size
         cols = slice(i * size, last)
-        scores = nt(ko_ref[:last, :], qo_ref[cols, :]) * SCALE
-        scores = mask_scores(scores, i * size, begin_ref[:, cols], size)
-        top = jnp.max(scores, axis=0, keepdims=True)
-        raw = jnp.exp(scores - top)
+        first = i * size
+        begin = begin_ref[:, cols]
+        near = nt(ko_ref[first:last, :], qo_ref[cols, :])
+        index = lax.broadcasted_iota(jnp.int32, near.shape, 0)
+        query = lax.broadcasted_iota(jnp.int32, near.shape, 1)
+        near = jnp.where((index <= query) & (index >= begin - first), near, NEG_FILL)
+        top = jnp.max(near, axis=0, keepdims=True)
+        if first:
+            past = nt(ko_ref[:first, :], qo_ref[cols, :])
+            past = jnp.where(lax.broadcasted_iota(jnp.int32, past.shape, 0) >= begin, past, NEG_FILL)
+            top = jnp.maximum(top, jnp.max(past, axis=0, keepdims=True))
+        raw = jnp.exp2((near - top) * FOLD)
         weight = jnp.sum(raw, axis=0, keepdims=True)
-        mixed = nn(flipped[:, :last], raw.astype(low)) * (1.0 / weight)
+        raw_ref[first:last, :] = raw.astype(low)
+        if first:
+            raw = jnp.exp2((past - top) * FOLD)
+            weight = weight + jnp.sum(raw, axis=0, keepdims=True)
+            raw_ref[:first, :] = raw.astype(low)
+        mixed = nn(flipped[:, :last], raw_ref[:last, :]) * (1.0 / weight)
         mixed = mixed.T.astype(low)
         for natural, block in pairs:
             if i * size <= natural < last:
                 at = natural - i * size
                 mix_ref[block : block + piece, :] = mixed[at : at + piece, :]
-        log_ref[:, cols] = top + jnp.log(weight)
+        log_ref[:, cols] = top * FOLD + jnp.log2(weight)
 
 
 def attend(pre, rows, inverse, gains, cosine, sine, begin, heads, size):
@@ -773,6 +787,7 @@
             pl.BlockSpec((2, HD), lambda g, h: (0, h)), every(HD), every(HD), line,
         ],
         out_specs=[head(0)] * 4 + [pl.BlockSpec((None, None, 1, span), lambda g, h: (g, h, 0, 0))],
+        scratch_shapes=[pltpu.VMEM((span, size), low)],
         compiler_params=pltpu.CompilerParams(vmem_limit_bytes=VMEM_LIMIT),
         cost_estimate=busy(5),
         name="attend",
@@ -793,9 +808,9 @@
     for i in range(span // size):
         last = (i + 1) * size
         cols = slice(i * size, last)
-        scores = nt(k_ref[:last, :], q_ref[cols, :]) * SCALE
+        scores = nt(k_ref[:last, :], q_ref[cols, :])
         scores = mask_scores(scores, i * size, begin_ref[:, cols], size)
-        probs = jnp.exp(scores - log_ref[:, cols])
+        probs = jnp.exp2(scores * FOLD - log_ref[:, cols])
         grad_probs = nt(v_ref[:last, :], g_held[cols, :])
         delta = jnp.sum(probs * grad_probs, axis=0, keepdims=True)
         grad_scores = (probs * (grad_probs - delta)).astype(low)
@@ -1444,6 +1459,37 @@
     )(grad_gate, grad_up, gate_weight, up_weight, gathered, grad_out, normed, inverse, gain)
 
 
+def close_body(t_ref, s_ref, b_ref, tokens_ref, q_ref, k_ref, v_ref, o_ref, block_ref):
+    share = q_ref.shape[1]
+    tokens_ref[...] = t_ref[...].astype(jnp.float32)
+    block_ref[...] = b_ref[...]
+    for i, ref in enumerate((q_ref, k_ref, v_ref)):
+        ref[...] = s_ref[:, i * share : (i + 1) * share].astype(jnp.float32)
+    o_ref[...] = s_ref[:, 3 * share :].astype(jnp.float32).T
+
+
+def closing(tokens_low, side_grad, block_output):
+    rows, cols = tokens_low.shape
+    depth, extent = side_grad.shape
+    share, f32, steps = extent // 4, jnp.float32, 2
+    down = lambda a, b: pl.BlockSpec((a // steps, b), lambda n: (n, 0))
+    weight = jax.ShapeDtypeStruct((depth, share), f32)
+    return pl.pallas_call(
+        close_body,
+        grid=(steps,),
+        out_shape=[
+            jax.ShapeDtypeStruct((rows, cols), f32), weight, weight, weight,
+            jax.ShapeDtypeStruct((share, depth), f32), jax.ShapeDtypeStruct((rows, cols), block_output.dtype),
+        ],
+        in_specs=[down(rows, cols), down(depth, extent), down(rows, cols)],
+        out_specs=[down(rows, cols)] + [down(depth, share)] * 3
+        + [pl.BlockSpec((share, depth // steps), lambda n: (0, n)), down(rows, cols)],
+        compiler_params=pltpu.CompilerParams(vmem_limit_bytes=VMEM_LIMIT),
+        cost_estimate=busy(5),
+        name="closing",
+    )(tokens_low, side_grad, block_output)
+
+
 def side_body(x_ref, p_ref, qk_ref, v_ref, m_ref, out_ref):
     first = 0
     for left, right in ((x_ref, qk_ref), (x_ref, v_ref), (p_ref, m_ref)):
@@ -1603,18 +1649,20 @@
         turn_out_body, [tokens_low, far_output], [True, False, False],
         planes, slots, 14, "turn_out", gain_parts,
     )
-    side_grad = sum_blk(side_part, 0).astype(f32)
+    tokens_grad, query_grad, key_grad, value_grad, output_grad, block_output = closing(
+        tokens_grad, sum_blk(side_part, 0), block_output
+    )
 
     sums = gain_sums.reshape(4, D)
     portion = D // (planes * width)
     sums = lax.dynamic_slice_in_dim(sums, (plane * width + place) * portion, portion, 1)
     return (
         block_output[None],
-        tokens_grad[None].astype(f32),
-        side_grad[:, :share],
-        side_grad[:, share : 2 * share],
-        side_grad[:, 2 * share : 3 * share],
-        side_grad[:, 3 * share :].T,
+        tokens_grad[None],
+        query_grad,
+        key_grad,
+        value_grad,
+        output_grad,
         sums[0],
         sums[1],
         sums[2],

time: 750 us -> 748 us (level)
  transfers between devices with their start and end apart: 8 -> 8, of which waited for: 2 -> 1; matrix products, arithmetic and copies ran while one was open for 10% -> 10% of each run, Pallas kernels for 54% -> 55%
where the time goes in v6:
time: 748 us; the launch traced here: 741 us
  Pallas kernels  647 us (86%)
  matrix products  42.8 us (6%)
  other arithmetic  25.3 us (3%)
  between operations  14.9 us (2%)
  local copies, waits for them, and re-layouts  9.2 us (1%)
    pallas_call x2, Pallas kernels, scatter(): pl.pallas_call(functools.partial(scatter_body, width, slots, flat, len(le...  114 us
    pallas_call x2, Pallas kernels, turn(): pl.pallas_call(functools.partial(body, planes, slots), out_shape=[shape(m...  105 us
    pallas_call x1, Pallas kernels, feed(): pl.pallas_call(functools.partial(feed_body, width, slots, step), out_shap...  100 us
    pallas_call x2, Pallas kernels, gather(): pl.pallas_call(functools.partial(gather_body, width, slots, side), out_sh...  98.8 us
    pallas_call x2, Pallas kernels, push(): pl.pallas_call(functools.partial(push_body, second, width, slots), out_sh...  72.6 us
    pallas_call x1, Pallas kernels, pull(): pl.pallas_call(functools.partial(pull_body, width, slots, 1024, chunk), o...  69.1 us
    pallas_call x1, Pallas kernels, attend_back(): pl.pallas_call(functools.partial(attend_back_body, size), grid=(slots, he...  26.3 us
    pallas_call x1, Pallas kernels, attend(): pl.pallas_call(functools.partial(attend_body, size), grid=(slots, heads),...  20.8 us
  transfers between devices with their start and end apart: 8, of which 1 were waited for; matrix products, arithmetic and copies ran while one was open for 10% of the time, Pallas kernels for 55%

profile of v6, /device:TPU:8, one launch (start us, length us, event | category | flops | bytes accessed | tf_op | source)
XLA Modules:
  0.0 741.0 jit_solution(13620671823680973966)
XLA Ops:
  7.2 1.9 pad_maximum_fusion.1
  9.1 47.0 %turn_in.1 = (bf16[320,2048]{1,0:T(8,128)(2,1)}, bf16[320,2048]{1,0:T(8,128)(2,1)}, bf16[320,2048]{1,0:T(8,128)(2,1)}) custom-call(bf16[320,2048]{1,0:T(8,128)(2,1)} %bitcast.85, bf16[320,2048]{1,0:T(8,128)(2,1)} %bitcast.86), custom_call_target="tpu_custom_call" | custom-call | bytes 35000000 | tf_op jit(solution)/shard_map/turn_in/pallas_call | solution.py:685
  56.2 50.5 %gather_tokens.1.x_ref = bf16[2560,2048]{1,0:T(8,128)(2,1)} custom-call(bf16[320,2048]{1,0:T(8,128)(2,1)} %get-tuple-element.68.refs_0_.refs_2_), custom_call_target="tpu_custom_call" | custom-call | bytes 35000000 | tf_op jit(solution)/shard_map/gather_tokens/pallas_call | solution.py:350
  107.1 0.7 compare_select_fusion.1.begin_ref
  108.0 0.6 maximum_convert_fusion.1.gain_ref
  108.7 0.1 multiply_cosine_fusion
  108.9 2.5 subtract_multiply_fusion
  111.4 9.1 %fusion.8 = f32[2560,512]{1,0:T(8,128)S(1)} fusion(bf16[2560,2048]{1,0:T(8,128)(2,1)} %gather_tokens.1.x_ref, bf16[2048,512]{1,0:T(8,128)(2,1)} %all-gather.4.cloned.1.call-done.refs_2_), kind=kOutput, calls=%fused_computation.61 | convolution fusion | flops 5368709120 | bytes 17825792 | tf_op jit(solution)/shard_map/dot_general | solution.py:56
  120.5 0.7 multiply_reduce_fusion.1
  121.3 1.6 copy-done.2
  122.9 0.6 pad_maximum_fusion.3.x_ref
  123.5 8.2 %total_squares.1 = f32[72,128]{1,0:T(8,128)} custom-call(f32[72,128]{1,0:T(8,128)} %pad_maximum_fusion.3.x_ref), custom_call_target="tpu_custom_call" | custom-call | bytes 24500000 | tf_op jit(solution)/shard_map/total_squares/pallas_call | solution.py:472
  131.8 0.7 add_rsqrt_fusion
  132.6 1.2 all-gather.6.cloned.1.call-done.refs_3_
  133.8 1.5 copy.32
  135.3 8.2 %convolution_convert_fusion.1 = bf16[2560,256]{1,0:T(8,128)(2,1)} fusion(bf16[2560,2048]{1,0:T(8,128)(2,1)} %gather_tokens.1.x_ref, bf16[2048,256]{1,0:T(8,128)(2,1)} %all-gather.6.cloned.1.call-done.refs_3_), kind=kOutput, calls=%fused_computation.1 | convolution fusion | flops 2685009920 | bytes 12845056 | tf_op jit(solution)/shard_map/dot_general | solution.py:56
  143.5 20.8 %attend.1 = (bf16[2,1280,256]{2,1,0:T(8,128)(2,1)}, bf16[2,1280,256]{2,1,0:T(8,128)(2,1)}, bf16[2,1280,256]{2,1,0:T(8,128)(2,1)}, bf16[2,1280,256]{2,1,0:T(8,128)(2,1)}, f32[2,2,1,1280]{3,2,1,0:T(1,128)}) custom-call(f32[2,1280,512]{2,1,0:T(8,128)} %bitcast.72, f32[2,1280,512]{2,1,0:T(8,128)} %bitcast.73, bf16[2,1280,256]{2,1,0:T(8,128)(2,1)} %bitcast.84, ...), custom_call_target="tpu_custom_call" | custom-call | bytes 17500000 | tf_op jit(solution)/shard_map/attend/pallas_call | solution.py:781
  164.3 1.3 fusion.6
  165.6 56.2 %scatter_mixed.1 = (f32[320,2048]{1,0:T(8,128)}, bf16[320,2048]{1,0:T(8,128)(2,1)}, f32[320,2048]{1,0:T(8,128)}, f32[320,1]{1,0:T(8,128)}) custom-call(bf16[2560,256]{1,0:T(8,128)(2,1)} %bitcast.79, bf16[256,2048]{1,0:T(8,128)(2,1)} %all-gather.8.cloned.1.call-done.refs_1_, bf16[320,2048]{1,0:T(8,128)(2,1)} %get-tuple-element.68.refs_0_.refs_2_, ...), custom_call_target="tpu_custom_call" | custom-call | bytes 35000000 | tf_op jit(solution)/shard_map/scatter_mixed/pallas_call | solution.py:434
  221.8 100.4 %feed.1 = (bf16[320,2048]{1,0:T(8,128)(2,1)}, bf16[320,1024]{1,0:T(8,128)(2,1)}, bf16[320,1024]{1,0:T(8,128)(2,1)}, f32[8,2048]{1,0:T(8,128)}, bf16[2560,2048]{1...) custom-call(bf16[320,2048]{1,0:T(8,128)(2,1)} %get-tuple-element.77., ...), custom_call_target="tpu_custom_call" | custom-call | bytes 315000000 | tf_op jit(solution)/shard_map/feed/pallas_call | solution.py:1090
  322.2 32.7 %push_first.1 = (bf16[1024,1024]{1,0:T(8,128)(2,1)}, bf16[4,2,320,1024]{3,2,1,0:T(8,128)(2,1)}, bf16[320,2048]{1,0:T(8,128)(2,1)}) custom-call(bf16[320,1024]{1,0:T(8,128)(2,1)} %get-tuple-element.84.refs_0_, bf16[2560,1024]{1,0:T(8,128)(2,1)} %get-tuple-element.81.refs_1_, bf16[320,2048]{1,0:T(8,128)(2,1)} %get-tuple-element.85.refs_2_), custom_call_target="tpu_custom_call" | custom-call | bytes 35000000 | tf_op jit(solution)/shard_map/push_first/pallas_call | solution.py:1311
  354.9 40.0 %push_second.1 = (bf16[1024,1024]{1,0:T(8,128)(2,1)}, bf16[2560,1024]{1,0:T(8,128)(2,1)}, bf16[2560,1024]{1,0:T(8,128)(2,1)}) custom-call(bf16[320,1024]{1,0:T(8,128)(2,1)} %get-tuple-element.80.refs_0_, bf16[2560,1024]{1,0:T(8,128)(2,1)} %get-tuple-element.81.refs_1_, bf16[1024,2048]{1,0:T(8,128)(2,1)} %refs_2_.1, ...), custom_call_target="tpu_custom_call" | custom-call | bytes 35000000 | tf_op jit(solution)/shard_map/push_second/pallas_call | solution.py:1311
  395.0 16.8 %convolution_convert_fusion.2 = bf16[2048,1024]{1,0:T(8,128)(2,1)} fusion(bf16[2560,2048]{1,0:T(8,128)(2,1)} %get-tuple-element.88.h_hbm, bf16[2560,1024]{1,0:T(8,128)(2,1)} %get-tuple-element.90.gg_hbm), kind=kOutput, calls=%fused_computation.2 | convolution fusion | flops 10739515392 | bytes 19922944 | tf_op jit(solution)/shard_map/dot_general | solution.py:60
  411.9 69.1 %pull.1 = (f32[320,2048]{1,0:T(8,128)}, bf16[320,2048]{1,0:T(8,128)(2,1)}, f32[8,2048]{1,0:T(8,128)}, bf16[2048,1024]{1,0:T(8,128)(2,1)}) custom-call(bf16[2560,1024]{1,0:T(8,128)(2,1)} %get-tuple-element.90.gg_hbm, bf16[2560,1024]{1,0:T(8,128)(2,1)} %get-tuple-element.91.gu_hbm, bf16[2048,1024]{1,0:T(8,128)(2,1)} %wg_hbm.3, bf16[2048,1024]{1,0:T(8,128)(2,1)} %wu_hbm.3, ...), custom_call_target="tpu_custom_call" | custom-call | bytes 35000000 | tf_op jit(solution)/shard_map/pull/pallas_call | solution.py:1442
  481.1 0.7 copy-done.10
  481.9 48.4 %gather_proj.1.p_ref = bf16[2560,2048]{1,0:T(8,128)(2,1)} custom-call(bf16[320,2048]{1,0:T(8,128)(2,1)} %get-tuple-element.95.refs_0_), custom_call_target="tpu_custom_call" | custom-call | bytes 35000000 | tf_op jit(solution)/shard_map/gather_proj/pallas_call | solution.py:350
  530.3 8.7 %convolution_convert_fusion = bf16[2560,256]{1,0:T(8,128)(2,1)} fusion(bf16[2560,2048]{1,0:T(8,128)(2,1)} %gather_proj.1.p_ref, bf16[256,2048]{1,0:T(8,128)(2,1)S(1)} %copy-done.4), kind=kOutput, calls=%fused_computation | convolution fusion | flops 2685009920 | bytes 12845056 | tf_op jit(solution)/shard_map/dot_general | solution.py:66
  539.1 26.3 %attend_back.1 = (f32[2,1280,256]{2,1,0:T(8,128)}, f32[2,1280,256]{2,1,0:T(8,128)}, bf16[2,1280,256]{2,1,0:T(8,128)(2,1)}, f32[2,2,1280,2]{3,2,1,0:T(8,128)}, f32[2,2,256]{2,1,0:T(2,128)}) custom-call(bf16[2,1280,256]{2,1,0:T(8,128)(2,1)} %get-tuple-element.72.q_ref, bf16[2,1280,256]{2,1,0:T(8,128)(2,1)} %get-tuple-element.73.k_ref, ...), custom_call_target="tpu_custom_call" | custom-call | bytes 17500000 | tf_op jit(solution)/shard_map/attend_back/pallas_call | solution.py:845
  565.4 0.7 reduce_sum.57
  566.2 2.1 reduce_sum.56
  568.3 0.4 copy.33
  568.7 0.6 pad_maximum_fusion.2.x_ref
  569.3 9.6 %total_means.1 = f32[104,128]{1,0:T(8,128)} custom-call(f32[104,128]{1,0:T(8,128)} %pad_maximum_fusion.2.x_ref), custom_call_target="tpu_custom_call" | custom-call | bytes 24500000 | tf_op jit(solution)/shard_map/total_means/pallas_call | solution.py:472
  578.9 0.7 slice_multiply_fusion
  579.7 5.3 fusion.3
  585.0 1.7 pad_maximum_fusion.refs_0_.qk_ref
  586.7 18.1 %side_grads.1 = bf16[2048,1024]{1,0:T(8,128)(2,1)} custom-call(bf16[2560,2048]{1,0:T(8,128)(2,1)} %gather_tokens.1.x_ref, bf16[2560,2048]{1,0:T(8,128)(2,1)} %gather_proj.1.p_ref, bf16[2560,512]{1,0:T(8,128)(2,1)} %pad_maximum_fusion.refs_0_.qk_ref, bf16[2560,256]{1,0:T(8,128)(2,1)} %bitcast.81, bf16[2560,256]{1,0:T(8,128)(2,1)} %bitcast.80), custom_call_target="tpu_custom_call" | custom-call | bytes 35000000 | tf_op jit(solution)/shard_map/side_grads/pallas_call | solution.py:1507
  604.8 1.0 copy-done.7
  605.8 0.2 copy-done.8
  606.0 1.6 maximum_convert_fusion
  607.6 0.6 slice.174.v_ref
  608.2 1.6 convert_element_type.74
  609.8 58.3 %scatter_tokens.1.x_ref = bf16[320,2048]{1,0:T(8,128)(2,1)} custom-call(bf16[2560,512]{1,0:T(8,128)(2,1)} %pad_maximum_fusion.refs_0_.qk_ref, bf16[2560,256]{1,0:T(8,128)(2,1)} %bitcast.82, bf16[2048,512]{1,0:T(8,128)(2,1)} %all-gather.4.cloned.1.call-done.refs_2_, bf16[2048,256]{1,0:T(8,128)(2,1)} %all-gather.6.cloned.1.call-done.refs_3_, ...), custom_call_target="tpu_custom_call" | custom-call | bytes 35000000 | tf_op jit(solution)/shard_map/scatter_tokens/pallas_call | solution.py:434
  668.1 2.8 convert_element_type.75
  670.9 57.6 %turn_out.1 = (bf16[320,2048]{1,0:T(8,128)(2,1)}, bf16[320,2048]{1,0:T(8,128)(2,1)}, bf16[320,2048]{1,0:T(8,128)(2,1)}, f32[64,128]{1,0:T(8,128)}) custom-call(bf16[320,2048]{1,0:T(8,128)(2,1)} %scatter_tokens.1.x_ref, bf16[320,2048]{1,0:T(8,128)(2,1)} %get-tuple-element.110.far_c, f32[64,128]{1,0:T(8,128)} %slice.174.v_ref), custom_call_target="tpu_custom_call" | custom-call | bytes 35000000 | tf_op jit(solution)/shard_map/turn_out/pallas_call | solution.py:685
  728.5 0.8 reshape.483
  729.4 0.5 slice_bitcast_fusion.10
  729.9 4.1 closing.1
  (87 shorter events, 1.4 us)
Async XLA Ops:
  7.2 99.6 %copy-start = (s32[8,3]{0,1:T(4,128)S(1)}, s32[8,3]{0,1:T(4,128)}, u32[]{:S(2)}) copy-start(s32[8,3]{0,1:T(4,128)} %param.19) | copy-start | bytes 292
  7.2 104.2 %all-gather.4.cloned.1.call-start = ((), (), s32[]{:S(2)}) async-start(), calls=%async_computation.5 | async-start | bytes 2621440 | tf_op jit(solution)/shard_map/all_gather | solution.py:1557
  56.1 50.8 %copy-start.14 = (bf16[256]{0:T(256)(128)(2,1)S(1)}, bf16[256]{0:T(256)(128)(2,1)}, u32[]{:S(2)}) copy-start(bf16[256]{0:T(256)(128)(2,1)} %param.24) | copy-start | bytes 1540
  56.1 50.8 %copy-start.15 = (bf16[256]{0:T(256)(128)(2,1)S(1)}, bf16[256]{0:T(256)(128)(2,1)}, u32[]{:S(2)}) copy-start(bf16[256]{0:T(256)(128)(2,1)} %param.25) | copy-start | bytes 1540
  56.1 50.8 %copy-start.16 = (bf16[256]{0:T(256)(128)(2,1)S(1)}, bf16[256]{0:T(256)(128)(2,1)}, u32[]{:S(2)}) copy-start(bf16[256]{0:T(256)(128)(2,1)} %param.26) | copy-start | bytes 1540
  56.1 50.8 %copy-start.17 = (bf16[256]{0:T(256)(128)(2,1)S(1)}, bf16[256]{0:T(256)(128)(2,1)}, u32[]{:S(2)}) copy-start(bf16[256]{0:T(256)(128)(2,1)} %param.30) | copy-start | bytes 1540
  56.1 52.5 %copy-start.13 = (f32[128]{0:T(128)S(1)}, f32[128]{0:T(128)}, u32[]{:S(2)}) copy-start(f32[128]{0:T(128)} %constant.45.clone) | copy-start | bytes 1540
  56.2 52.7 %copy-start.5 = (f32[1280,128]{1,0:T(8,128)S(1)}, f32[1280,128]{1,0:T(8,128)}, u32[]{:S(2)}) copy-start(f32[1280,128]{1,0:T(8,128)} %constant.44.clone) | copy-start | bytes 1966084
  56.2 52.7 %copy-start.6 = (f32[1280,128]{1,0:T(8,128)S(1)}, f32[1280,128]{1,0:T(8,128)}, u32[]{:S(2)}) copy-start(f32[1280,128]{1,0:T(8,128)} %constant.15.clone) | copy-start | bytes 1966084
  56.2 52.7 %copy-start.12 = (f32[128]{0:T(128)S(1)}, f32[128]{0:T(128)}, u32[]{:S(2)}) copy-start(f32[128]{0:T(128)} %constant.46.clone) | copy-start | bytes 1540
  56.2 77.6 %all-gather.6.cloned.1.call-start = ((), (), s32[]{:S(2)}) async-start(), calls=%async_computation.6 | async-start | bytes 1310720 | tf_op jit(solution)/shard_map/all_gather | solution.py:1576
  106.7 58.9 %all-gather.8.cloned.1.call-start = ((), (), s32[]{:S(2)}) async-start(), calls=%async_computation.7 | async-start | bytes 1310720 | tf_op jit(solution)/shard_map/all_gather | solution.py:1578
  120.5 2.3 copy-start.2
  131.8 280.1 %reduce-scatter.6.cloned.1.call-start = ((), (), s32[]{:S(2)}) async-start(), calls=%async_computation.8 | async-start | bytes 2621440 | tf_op jit(solution)/shard_map/reduce_scatter | solution.py:1551
  354.9 175.4 %reduce-scatter.8.cloned.1.call-start = ((), (), s32[]{:S(2)}) async-start(), calls=%async_computation.9 | async-start | bytes 2621440 | tf_op jit(solution)/shard_map/reduce_scatter | solution.py:1551
  394.9 174.4 %reduce-scatter.10.cloned.1.call-start = ((), (), s32[]{:S(2)}) async-start(), calls=%async_computation.10 | async-start | bytes 5242880 | tf_op jit(solution)/shard_map/reduce_scatter | solution.py:1551
  411.8 256.3 %reduce-scatter.12.cloned.1.call-start = ((), (), s32[]{:S(2)}) async-start(), calls=%async_computation.11 | async-start | bytes 5242880 | tf_op jit(solution)/shard_map/reduce_scatter | solution.py:1551
  481.0 0.8 copy-start.10
  481.0 248.9 %reduce-scatter.14.cloned.1.call-start = ((), (), s32[]{:S(2)}) async-start(), calls=%async_computation.12 | async-start | bytes 5242880 | tf_op jit(solution)/shard_map/reduce_scatter | solution.py:1551
  481.9 48.4 %copy-start.11 = (f32[8,2048]{1,0:T(8,128)S(1)}, f32[8,2048]{1,0:T(8,128)}, u32[]{:S(2)}) copy-start(f32[8,2048]{1,0:T(8,128)} %get-tuple-element.102) | copy-start | bytes 196612
  481.9 48.5 %copy-start.4 = (bf16[256,2048]{1,0:T(8,128)(2,1)S(1)}, bf16[256,2048]{1,0:T(8,128)(2,1)}, u32[]{:S(2)}) copy-start(bf16[256,2048]{1,0:T(8,128)(2,1)} %all-gather.8.cloned.1.call-done.refs_1_) | copy-start | bytes 3145732
  604.8 1.0 copy-start.7
  604.8 1.2 copy-start.8
  604.8 2.8 copy-start.9
  604.8 3.4 copy-start.3
  670.9 63.1 %copy-start.1 = (s32[8,3]{0,1:T(4,128)S(1)}, s32[8,3]{0,1:T(4,128)}, u32[]{:S(2)}) copy-start(s32[8,3]{0,1:T(4,128)} %param.19) | copy-start | bytes 292
Sparse Core Ops, SparseCore 0:
  56.2 45.1 all-gather.3
  106.9 26.9 all-gather.5
  135.4 27.4 all-gather.7
  355.0 41.0 reduce-scatter.5
  398.3 43.1 reduce-scatter.7
  443.6 78.3 reduce-scatter.9
  524.4 77.2 reduce-scatter.11
  604.9 94.2 reduce-scatter.13

commit v7 on v6

--- a/solution.py
+++ b/solution.py
@@ -723,7 +723,7 @@
 
 
 def attend_body(size, q_ref, k_ref, v_ref, inv_ref, gain_ref, cos_ref, sin_ref, begin_ref,
-                qo_ref, ko_ref, vo_ref, mix_ref, log_ref, raw_ref):
+                qo_ref, ko_ref, vo_ref, mix_ref, log_ref):
     low = jnp.bfloat16
     span = q_ref.shape[0]
 
@@ -744,25 +744,12 @@
     for i in range(span // size):
         last = (i + 1) * size
         cols = slice(i * size, last)
-        first = i * size
-        begin = begin_ref[:, cols]
-        near = nt(ko_ref[first:last, :], qo_ref[cols, :])
-        index = lax.broadcasted_iota(jnp.int32, near.shape, 0)
-        query = lax.broadcasted_iota(jnp.int32, near.shape, 1)
-        near = jnp.where((index <= query) & (index >= begin - first), near, NEG_FILL)
-        top = jnp.max(near, axis=0, keepdims=True)
-        if first:
-            past = nt(ko_ref[:first, :], qo_ref[cols, :])
-            past = jnp.where(lax.broadcasted_iota(jnp.int32, past.shape, 0) >= begin, past, NEG_FILL)
-            top = jnp.maximum(top, jnp.max(past, axis=0, keepdims=True))
-        raw = jnp.exp2((near - top) * FOLD)
+        scores = nt(ko_ref[:last, :], qo_ref[cols, :])
+        scores = mask_scores(scores, i * size, begin_ref[:, cols], size)
+        top = jnp.max(scores, axis=0, keepdims=True)
+        raw = jnp.exp2((scores - top) * FOLD)
         weight = jnp.sum(raw, axis=0, keepdims=True)
-        raw_ref[first:last, :] = raw.astype(low)
-        if first:
-            raw = jnp.exp2((past - top) * FOLD)
-            weight = weight + jnp.sum(raw, axis=0, keepdims=True)
-            raw_ref[:first, :] = raw.astype(low)
-        mixed = nn(flipped[:, :last], raw_ref[:last, :]) * (1.0 / weight)
+        mixed = nn(flipped[:, :last], raw.astype(low)) * (1.0 / weight)
         mixed = mixed.T.astype(low)
         for natural, block in pairs:
             if i * size <= natural < last:
@@ -787,7 +774,6 @@
             pl.BlockSpec((2, HD), lambda g, h: (0, h)), every(HD), every(HD), line,
         ],
         out_specs=[head(0)] * 4 + [pl.BlockSpec((None, None, 1, span), lambda g, h: (g, h, 0, 0))],
-        scratch_shapes=[pltpu.VMEM((span, size), low)],
         compiler_params=pltpu.CompilerParams(vmem_limit_bytes=VMEM_LIMIT),
         cost_estimate=busy(5),
         name="attend",

time: 748 us -> 745 us (level)
  transfers between devices with their start and end apart: 8 -> 8, of which waited for: 1 -> 2; matrix products, arithmetic and copies ran while one was open for 10% -> 10% of each run, Pallas kernels for 55% -> 55%
where the time goes in v7:
time: 745 us; the launch traced here: 738 us
  Pallas kernels  644 us (86%)
  matrix products  42.8 us (6%)
  other arithmetic  25.3 us (3%)
  between operations  14.9 us (2%)
  local copies, waits for them, and re-layouts  9.2 us (1%)
    pallas_call x2, Pallas kernels, scatter(): pl.pallas_call(functools.partial(scatter_body, width, slots, flat, len(le...  114 us
    pallas_call x2, Pallas kernels, turn(): pl.pallas_call(functools.partial(body, planes, slots), out_shape=[shape(m...  105 us
    pallas_call x1, Pallas kernels, feed(): pl.pallas_call(functools.partial(feed_body, width, slots, step), out_shap...  100 us
    pallas_call x2, Pallas kernels, gather(): pl.pallas_call(functools.partial(gather_body, width, slots, side), out_sh...  98.8 us
    pallas_call x2, Pallas kernels, push(): pl.pallas_call(functools.partial(push_body, second, width, slots), out_sh...  72.6 us
    pallas_call x1, Pallas kernels, pull(): pl.pallas_call(functools.partial(pull_body, width, slots, 1024, chunk), o...  69.1 us
    pallas_call x1, Pallas kernels, attend_back(): pl.pallas_call(functools.partial(attend_back_body, size), grid=(slots, he...  26.3 us
    pallas_call x1, Pallas kernels, side_grads(): pl.pallas_call(side_body, grid=(cols // chunk,), out_shape=jax.ShapeDtype...  18.1 us
  transfers between devices with their start and end apart: 8, of which 2 were waited for; matrix products, arithmetic and copies ran while one was open for 10% of the time, Pallas kernels for 55%

profile of v7, /device:TPU:8, one launch (start us, length us, event | category | flops | bytes accessed | tf_op | source)
XLA Modules:
  0.0 738.3 jit_solution(15745544914224435)
XLA Ops:
  7.2 1.9 pad_maximum_fusion.1
  9.1 47.0 %turn_in.1 = (bf16[320,2048]{1,0:T(8,128)(2,1)}, bf16[320,2048]{1,0:T(8,128)(2,1)}, bf16[320,2048]{1,0:T(8,128)(2,1)}) custom-call(bf16[320,2048]{1,0:T(8,128)(2,1)} %bitcast.85, bf16[320,2048]{1,0:T(8,128)(2,1)} %bitcast.86), custom_call_target="tpu_custom_call" | custom-call | bytes 35000000 | tf_op jit(solution)/shard_map/turn_in/pallas_call | solution.py:685
  56.2 50.5 %gather_tokens.1.x_ref = bf16[2560,2048]{1,0:T(8,128)(2,1)} custom-call(bf16[320,2048]{1,0:T(8,128)(2,1)} %get-tuple-element.68.refs_0_.refs_2_), custom_call_target="tpu_custom_call" | custom-call | bytes 35000000 | tf_op jit(solution)/shard_map/gather_tokens/pallas_call | solution.py:350
  107.1 0.7 compare_select_fusion.1.begin_ref
  108.0 0.6 maximum_convert_fusion.1.gain_ref
  108.9 2.5 subtract_multiply_fusion
  111.4 9.1 %fusion.8 = f32[2560,512]{1,0:T(8,128)S(1)} fusion(bf16[2560,2048]{1,0:T(8,128)(2,1)} %gather_tokens.1.x_ref, bf16[2048,512]{1,0:T(8,128)(2,1)} %all-gather.4.cloned.1.call-done.refs_2_), kind=kOutput, calls=%fused_computation.61 | convolution fusion | flops 5368709120 | bytes 17825792 | tf_op jit(solution)/shard_map/dot_general | solution.py:56
  120.5 0.7 multiply_reduce_fusion.1
  121.3 1.6 copy-done.2
  122.9 0.6 pad_maximum_fusion.3.x_ref
  123.5 8.2 %total_squares.1 = f32[72,128]{1,0:T(8,128)} custom-call(f32[72,128]{1,0:T(8,128)} %pad_maximum_fusion.3.x_ref), custom_call_target="tpu_custom_call" | custom-call | bytes 24500000 | tf_op jit(solution)/shard_map/total_squares/pallas_call | solution.py:472
  131.8 0.7 add_rsqrt_fusion
  132.6 1.2 all-gather.6.cloned.1.call-done.refs_3_
  133.8 1.5 copy.32
  135.3 8.2 %convolution_convert_fusion.1 = bf16[2560,256]{1,0:T(8,128)(2,1)} fusion(bf16[2560,2048]{1,0:T(8,128)(2,1)} %gather_tokens.1.x_ref, bf16[2048,256]{1,0:T(8,128)(2,1)} %all-gather.6.cloned.1.call-done.refs_3_), kind=kOutput, calls=%fused_computation.1 | convolution fusion | flops 2685009920 | bytes 12845056 | tf_op jit(solution)/shard_map/dot_general | solution.py:56
  143.5 17.3 %attend.1 = (bf16[2,1280,256]{2,1,0:T(8,128)(2,1)}, bf16[2,1280,256]{2,1,0:T(8,128)(2,1)}, bf16[2,1280,256]{2,1,0:T(8,128)(2,1)}, bf16[2,1280,256]{2,1,0:T(8,128)(2,1)}, f32[2,2,1,1280]{3,2,1,0:T(1,128)}) custom-call(f32[2,1280,512]{2,1,0:T(8,128)} %bitcast.72, f32[2,1280,512]{2,1,0:T(8,128)} %bitcast.73, bf16[2,1280,256]{2,1,0:T(8,128)(2,1)} %bitcast.84, ...), custom_call_target="tpu_custom_call" | custom-call | bytes 17500000 | tf_op jit(solution)/shard_map/attend/pallas_call | solution.py:768
  160.8 1.3 fusion.6
  162.1 0.8 all-gather.8.cloned.1.call-done.refs_1_
  162.9 56.2 %scatter_mixed.1 = (f32[320,2048]{1,0:T(8,128)}, bf16[320,2048]{1,0:T(8,128)(2,1)}, f32[320,2048]{1,0:T(8,128)}, f32[320,1]{1,0:T(8,128)}) custom-call(bf16[2560,256]{1,0:T(8,128)(2,1)} %bitcast.79, bf16[256,2048]{1,0:T(8,128)(2,1)} %all-gather.8.cloned.1.call-done.refs_1_, bf16[320,2048]{1,0:T(8,128)(2,1)} %get-tuple-element.68.refs_0_.refs_2_, ...), custom_call_target="tpu_custom_call" | custom-call | bytes 35000000 | tf_op jit(solution)/shard_map/scatter_mixed/pallas_call | solution.py:434
  219.0 100.5 %feed.1 = (bf16[320,2048]{1,0:T(8,128)(2,1)}, bf16[320,1024]{1,0:T(8,128)(2,1)}, bf16[320,1024]{1,0:T(8,128)(2,1)}, f32[8,2048]{1,0:T(8,128)}, bf16[2560,2048]{1...) custom-call(bf16[320,2048]{1,0:T(8,128)(2,1)} %get-tuple-element.77., ...), custom_call_target="tpu_custom_call" | custom-call | bytes 315000000 | tf_op jit(solution)/shard_map/feed/pallas_call | solution.py:1076
  319.5 32.7 %push_first.1 = (bf16[1024,1024]{1,0:T(8,128)(2,1)}, bf16[4,2,320,1024]{3,2,1,0:T(8,128)(2,1)}, bf16[320,2048]{1,0:T(8,128)(2,1)}) custom-call(bf16[320,1024]{1,0:T(8,128)(2,1)} %get-tuple-element.84.refs_0_, bf16[2560,1024]{1,0:T(8,128)(2,1)} %get-tuple-element.81.refs_1_, bf16[320,2048]{1,0:T(8,128)(2,1)} %get-tuple-element.85.refs_2_), custom_call_target="tpu_custom_call" | custom-call | bytes 35000000 | tf_op jit(solution)/shard_map/push_first/pallas_call | solution.py:1297
  352.2 40.0 %push_second.1 = (bf16[1024,1024]{1,0:T(8,128)(2,1)}, bf16[2560,1024]{1,0:T(8,128)(2,1)}, bf16[2560,1024]{1,0:T(8,128)(2,1)}) custom-call(bf16[320,1024]{1,0:T(8,128)(2,1)} %get-tuple-element.80.refs_0_, bf16[2560,1024]{1,0:T(8,128)(2,1)} %get-tuple-element.81.refs_1_, bf16[1024,2048]{1,0:T(8,128)(2,1)} %refs_2_.1, ...), custom_call_target="tpu_custom_call" | custom-call | bytes 35000000 | tf_op jit(solution)/shard_map/push_second/pallas_call | solution.py:1297
  392.3 16.8 %convolution_convert_fusion.2 = bf16[2048,1024]{1,0:T(8,128)(2,1)} fusion(bf16[2560,2048]{1,0:T(8,128)(2,1)} %get-tuple-element.88.h_hbm, bf16[2560,1024]{1,0:T(8,128)(2,1)} %get-tuple-element.90.gg_hbm), kind=kOutput, calls=%fused_computation.2 | convolution fusion | flops 10739515392 | bytes 19922944 | tf_op jit(solution)/shard_map/dot_general | solution.py:60
  409.2 69.1 %pull.1 = (f32[320,2048]{1,0:T(8,128)}, bf16[320,2048]{1,0:T(8,128)(2,1)}, f32[8,2048]{1,0:T(8,128)}, bf16[2048,1024]{1,0:T(8,128)(2,1)}) custom-call(bf16[2560,1024]{1,0:T(8,128)(2,1)} %get-tuple-element.90.gg_hbm, bf16[2560,1024]{1,0:T(8,128)(2,1)} %get-tuple-element.91.gu_hbm, bf16[2048,1024]{1,0:T(8,128)(2,1)} %wg_hbm.3, bf16[2048,1024]{1,0:T(8,128)(2,1)} %wu_hbm.3, ...), custom_call_target="tpu_custom_call" | custom-call | bytes 35000000 | tf_op jit(solution)/shard_map/pull/pallas_call | solution.py:1428
  478.4 0.7 copy-done.10
  479.2 48.4 %gather_proj.1.p_ref = bf16[2560,2048]{1,0:T(8,128)(2,1)} custom-call(bf16[320,2048]{1,0:T(8,128)(2,1)} %get-tuple-element.95.refs_0_), custom_call_target="tpu_custom_call" | custom-call | bytes 35000000 | tf_op jit(solution)/shard_map/gather_proj/pallas_call | solution.py:350
  527.6 8.7 %convolution_convert_fusion = bf16[2560,256]{1,0:T(8,128)(2,1)} fusion(bf16[2560,2048]{1,0:T(8,128)(2,1)} %gather_proj.1.p_ref, bf16[256,2048]{1,0:T(8,128)(2,1)S(1)} %copy-done.4), kind=kOutput, calls=%fused_computation | convolution fusion | flops 2685009920 | bytes 12845056 | tf_op jit(solution)/shard_map/dot_general | solution.py:66
  536.4 26.3 %attend_back.1 = (f32[2,1280,256]{2,1,0:T(8,128)}, f32[2,1280,256]{2,1,0:T(8,128)}, bf16[2,1280,256]{2,1,0:T(8,128)(2,1)}, f32[2,2,1280,2]{3,2,1,0:T(8,128)}, f32[2,2,256]{2,1,0:T(2,128)}) custom-call(bf16[2,1280,256]{2,1,0:T(8,128)(2,1)} %get-tuple-element.72.q_ref, bf16[2,1280,256]{2,1,0:T(8,128)(2,1)} %get-tuple-element.73.k_ref, ...), custom_call_target="tpu_custom_call" | custom-call | bytes 17500000 | tf_op jit(solution)/shard_map/attend_back/pallas_call | solution.py:831
  562.7 0.7 reduce_sum.57
  563.5 2.1 reduce_sum.56
  565.6 0.4 copy.33
  566.0 0.6 pad_maximum_fusion.2.x_ref
  566.6 9.6 %total_means.1 = f32[104,128]{1,0:T(8,128)} custom-call(f32[104,128]{1,0:T(8,128)} %pad_maximum_fusion.2.x_ref), custom_call_target="tpu_custom_call" | custom-call | bytes 24500000 | tf_op jit(solution)/shard_map/total_means/pallas_call | solution.py:472
  576.2 0.7 slice_multiply_fusion
  577.0 5.3 fusion.3
  582.3 1.7 pad_maximum_fusion.refs_0_.qk_ref
  584.0 18.1 %side_grads.1 = bf16[2048,1024]{1,0:T(8,128)(2,1)} custom-call(bf16[2560,2048]{1,0:T(8,128)(2,1)} %gather_tokens.1.x_ref, bf16[2560,2048]{1,0:T(8,128)(2,1)} %gather_proj.1.p_ref, bf16[2560,512]{1,0:T(8,128)(2,1)} %pad_maximum_fusion.refs_0_.qk_ref, bf16[2560,256]{1,0:T(8,128)(2,1)} %bitcast.81, bf16[2560,256]{1,0:T(8,128)(2,1)} %bitcast.80), custom_call_target="tpu_custom_call" | custom-call | bytes 35000000 | tf_op jit(solution)/shard_map/side_grads/pallas_call | solution.py:1493
  602.1 1.0 copy-done.7
  603.1 0.2 copy-done.8
  603.3 1.6 maximum_convert_fusion
  604.9 0.6 slice.174.v_ref
  605.5 1.6 convert_element_type.74
  607.1 58.3 %scatter_tokens.1.x_ref = bf16[320,2048]{1,0:T(8,128)(2,1)} custom-call(bf16[2560,512]{1,0:T(8,128)(2,1)} %pad_maximum_fusion.refs_0_.qk_ref, bf16[2560,256]{1,0:T(8,128)(2,1)} %bitcast.82, bf16[2048,512]{1,0:T(8,128)(2,1)} %all-gather.4.cloned.1.call-done.refs_2_, bf16[2048,256]{1,0:T(8,128)(2,1)} %all-gather.6.cloned.1.call-done.refs_3_, ...), custom_call_target="tpu_custom_call" | custom-call | bytes 35000000 | tf_op jit(solution)/shard_map/scatter_tokens/pallas_call | solution.py:434
  665.4 2.8 convert_element_type.75
  668.2 57.6 %turn_out.1 = (bf16[320,2048]{1,0:T(8,128)(2,1)}, bf16[320,2048]{1,0:T(8,128)(2,1)}, bf16[320,2048]{1,0:T(8,128)(2,1)}, f32[64,128]{1,0:T(8,128)}) custom-call(bf16[320,2048]{1,0:T(8,128)(2,1)} %scatter_tokens.1.x_ref, bf16[320,2048]{1,0:T(8,128)(2,1)} %get-tuple-element.110.far_c, f32[64,128]{1,0:T(8,128)} %slice.174.v_ref), custom_call_target="tpu_custom_call" | custom-call | bytes 35000000 | tf_op jit(solution)/shard_map/turn_out/pallas_call | solution.py:685
  725.8 0.8 reshape.483
  726.6 0.5 slice_bitcast_fusion.10
  727.2 4.1 closing.1
  (87 shorter events, 1.6 us)
Async XLA Ops:
  7.2 99.6 %copy-start = (s32[8,3]{0,1:T(4,128)S(1)}, s32[8,3]{0,1:T(4,128)}, u32[]{:S(2)}) copy-start(s32[8,3]{0,1:T(4,128)} %param.19) | copy-start | bytes 292
  7.2 104.2 %all-gather.4.cloned.1.call-start = ((), (), s32[]{:S(2)}) async-start(), calls=%async_computation.5 | async-start | bytes 2621440 | tf_op jit(solution)/shard_map/all_gather | solution.py:1543
  56.1 50.8 %copy-start.14 = (bf16[256]{0:T(256)(128)(2,1)S(1)}, bf16[256]{0:T(256)(128)(2,1)}, u32[]{:S(2)}) copy-start(bf16[256]{0:T(256)(128)(2,1)} %param.24) | copy-start | bytes 1540
  56.1 50.8 %copy-start.15 = (bf16[256]{0:T(256)(128)(2,1)S(1)}, bf16[256]{0:T(256)(128)(2,1)}, u32[]{:S(2)}) copy-start(bf16[256]{0:T(256)(128)(2,1)} %param.25) | copy-start | bytes 1540
  56.1 50.8 %copy-start.16 = (bf16[256]{0:T(256)(128)(2,1)S(1)}, bf16[256]{0:T(256)(128)(2,1)}, u32[]{:S(2)}) copy-start(bf16[256]{0:T(256)(128)(2,1)} %param.26) | copy-start | bytes 1540
  56.1 50.8 %copy-start.17 = (bf16[256]{0:T(256)(128)(2,1)S(1)}, bf16[256]{0:T(256)(128)(2,1)}, u32[]{:S(2)}) copy-start(bf16[256]{0:T(256)(128)(2,1)} %param.30) | copy-start | bytes 1540
  56.1 52.5 %copy-start.13 = (f32[128]{0:T(128)S(1)}, f32[128]{0:T(128)}, u32[]{:S(2)}) copy-start(f32[128]{0:T(128)} %constant.45.clone) | copy-start | bytes 1540
  56.2 52.7 %copy-start.5 = (f32[1280,128]{1,0:T(8,128)S(1)}, f32[1280,128]{1,0:T(8,128)}, u32[]{:S(2)}) copy-start(f32[1280,128]{1,0:T(8,128)} %constant.44.clone) | copy-start | bytes 1966084
  56.2 52.7 %copy-start.6 = (f32[1280,128]{1,0:T(8,128)S(1)}, f32[1280,128]{1,0:T(8,128)}, u32[]{:S(2)}) copy-start(f32[1280,128]{1,0:T(8,128)} %constant.15.clone) | copy-start | bytes 1966084
  56.2 52.7 %copy-start.12 = (f32[128]{0:T(128)S(1)}, f32[128]{0:T(128)}, u32[]{:S(2)}) copy-start(f32[128]{0:T(128)} %constant.46.clone) | copy-start | bytes 1540
  56.2 77.6 %all-gather.6.cloned.1.call-start = ((), (), s32[]{:S(2)}) async-start(), calls=%async_computation.6 | async-start | bytes 1310720 | tf_op jit(solution)/shard_map/all_gather | solution.py:1562
  106.7 56.1 %all-gather.8.cloned.1.call-start = ((), (), s32[]{:S(2)}) async-start(), calls=%async_computation.7 | async-start | bytes 1310720 | tf_op jit(solution)/shard_map/all_gather | solution.py:1564
  120.5 2.3 copy-start.2
  131.8 277.4 %reduce-scatter.6.cloned.1.call-start = ((), (), s32[]{:S(2)}) async-start(), calls=%async_computation.8 | async-start | bytes 2621440 | tf_op jit(solution)/shard_map/reduce_scatter | solution.py:1537
  352.2 175.4 %reduce-scatter.8.cloned.1.call-start = ((), (), s32[]{:S(2)}) async-start(), calls=%async_computation.9 | async-start | bytes 2621440 | tf_op jit(solution)/shard_map/reduce_scatter | solution.py:1537
  392.2 174.4 %reduce-scatter.10.cloned.1.call-start = ((), (), s32[]{:S(2)}) async-start(), calls=%async_computation.10 | async-start | bytes 5242880 | tf_op jit(solution)/shard_map/reduce_scatter | solution.py:1537
  409.1 256.3 %reduce-scatter.12.cloned.1.call-start = ((), (), s32[]{:S(2)}) async-start(), calls=%async_computation.11 | async-start | bytes 5242880 | tf_op jit(solution)/shard_map/reduce_scatter | solution.py:1537
  478.3 0.8 copy-start.10
  478.3 248.8 %reduce-scatter.14.cloned.1.call-start = ((), (), s32[]{:S(2)}) async-start(), calls=%async_computation.12 | async-start | bytes 5242880 | tf_op jit(solution)/shard_map/reduce_scatter | solution.py:1537
  479.2 48.4 %copy-start.11 = (f32[8,2048]{1,0:T(8,128)S(1)}, f32[8,2048]{1,0:T(8,128)}, u32[]{:S(2)}) copy-start(f32[8,2048]{1,0:T(8,128)} %get-tuple-element.102) | copy-start | bytes 196612
  479.2 48.5 %copy-start.4 = (bf16[256,2048]{1,0:T(8,128)(2,1)S(1)}, bf16[256,2048]{1,0:T(8,128)(2,1)}, u32[]{:S(2)}) copy-start(bf16[256,2048]{1,0:T(8,128)(2,1)} %all-gather.8.cloned.1.call-done.refs_1_) | copy-start | bytes 3145732
  602.1 1.0 copy-start.7
  602.1 1.2 copy-start.8
  602.1 2.8 copy-start.9
  602.1 3.4 copy-start.3
  668.2 63.1 %copy-start.1 = (s32[8,3]{0,1:T(4,128)S(1)}, s32[8,3]{0,1:T(4,128)}, u32[]{:S(2)}) copy-start(s32[8,3]{0,1:T(4,128)} %param.19) | copy-start | bytes 292
Sparse Core Ops, SparseCore 0:
  56.2 45.1 all-gather.3
  106.9 26.9 all-gather.5
  135.4 27.4 all-gather.7
  352.3 41.0 reduce-scatter.5
  395.6 43.1 reduce-scatter.7
  441.0 78.3 reduce-scatter.9
  521.8 77.2 reduce-scatter.11
  602.2 94.1 reduce-scatter.13
